TPU v7x, 32 devices: a whole 2x2x4 slice. The times are simulated.
32 devices in a mesh: gen: 4 (over z), neur: 4 (over x, core), box: 2 (over y).
Axes of the slice: x: 2, y: 2, z: 4, core: 2. Of those that a mesh axis runs over, the one named last changes fastest.
Arguments:
- gens: bfloat16 [8, 128, 4096], P('box', 'gen'), may hold values from -1 to 1
- center: bfloat16 [8, 4096], P('box'), may hold values from -6 to 6
- weight: bfloat16 [4096, 2048], P('gen', 'neur'), may hold values from -0.09375 to 0.09375
- bias: float32 [2048], P('neur'), may hold values from -3 to 3
- phase: int32 [8, 2048], P('box', 'neur'), may hold values from 0 to 2
- gens_cot: bfloat16 [8, 128, 2048], P('box', 'gen', 'neur'), may hold values from -6 to 6
- center_cot: float32 [8, 2048], P('box', 'neur'), may hold values from -6 to 6
- offset_cot: float32 [8, 2048], P('box', 'neur'), may hold values from -6 to 6
Outputs:
- center_out: float32 [8, 2048], P('box', 'neur')
- gens_out: bfloat16 [8, 128, 2048], P('box', 'gen', 'neur')
- offset: float32 [8, 2048], P('box', 'neur')
- weight_grad: float32 [4096, 2048], P('gen', 'neur')
- bias_grad: float32 [2048], P('neur')
- gens_grad: float32 [8, 128, 4096], P('box', 'gen', 'neur')
- center_grad: float32 [8, 4096], P('box', 'neur')
Inputs may be any that keep to these rules, and one draw needn't show every extreme that they name: `phase`: 0 marks an inactive neuron, 1 an active one, 2 one that crosses zero.
All inputs are finite; a program needn't handle non-finite values.
Results may differ from a plain program's by a relative error of at most 0.006.
Values may be sent and summed in bfloat16 or wider, within the bound.
No kernel may reach another device: no remote copies, remote signals or barrier semaphores. Data moves between devices by JAX's collectives and lax.ppermute only.
A program may use at most 64 MiB of HBM per device.

v0:
```python
import jax
import jax.numpy as jnp
from jax import lax
from jax.sharding import PartitionSpec as P


def neuron(center_pre, radius, phase):
    upper = center_pre + radius
    lower = center_pre - radius
    ratio = jnp.clip(upper / (upper - lower + 1e-05), 0.0, 1.0)
    active = (phase == 1).astype(center_pre.dtype)
    crossing = (phase == 2).astype(center_pre.dtype)
    slope = active + crossing * ratio
    offset = crossing * (-ratio * lower * 0.5)
    return (slope, slope * center_pre + offset, offset)


def body(gens, center, weight, bias, phase, gens_cot, center_cot, offset_cot):
    box_dev, gen_dev, width = gens.shape
    local_cols = weight.shape[1]
    local_rows = box_dev * gen_dev
    wide = jnp.concatenate([gens.reshape(local_rows, width), center], 0)
    full_weight = lax.all_gather(weight, "gen", axis=0, tiled=True)
    product = jnp.dot(wide, full_weight, preferred_element_type=jnp.float32)
    gen_pre = product[:local_rows].reshape(box_dev, gen_dev, local_cols)
    center_pre = product[local_rows:] + bias
    part_radius = jnp.sum(jnp.abs(gen_pre), axis=1)
    cot_wide = gens_cot.astype(jnp.float32)
    radius = lax.psum(part_radius, "gen")
    slope, center_out, offset = neuron(center_pre, radius, phase)
    gens_out = (slope[:, None, :] * gen_pre).astype(jnp.bfloat16)
    intersection = lax.psum(jnp.sum(cot_wide * gen_pre, axis=1), "gen")
    unused, pull = jax.vjp(lambda a, b: neuron(a, b, phase), center_pre, radius)
    g_center, g_radius = pull((intersection, center_cot, offset_cot))
    gen_back = (slope[:, None, :] * cot_wide + jnp.sign(gen_pre) * g_radius[:, None, :]).astype(
        jnp.bfloat16
    )
    center_back = g_center.astype(jnp.bfloat16)
    back = jnp.concatenate([gen_back.reshape(local_rows, local_cols), center_back], 0)
    first_gen = (lax.axis_index("gen") == 0).astype(jnp.bfloat16)
    back_owned = jnp.concatenate(
        [gen_back.reshape(local_rows, local_cols), center_back * first_gen], 0
    )
    bias_part = jnp.sum(g_center, axis=0)
    shares = lax.psum_scatter(
        lax.dot_general(
            wide, back_owned, (((0,), (0,)), ((), ())), preferred_element_type=jnp.float32
        ),
        ("gen", "box"),
        scatter_dimension=0,
        tiled=True,
    )
    weight_grad = lax.all_gather(shares, "box", axis=0, tiled=True)
    bias_grad = lax.psum(bias_part, "box")
    partial_back = lax.dot_general(
        back, full_weight, (((1,), (1,)), ((), ())), preferred_element_type=jnp.float32
    )
    summed = lax.psum_scatter(partial_back, "neur", scatter_dimension=1, tiled=True)
    gens_grad = summed[:local_rows].reshape(box_dev, gen_dev, summed.shape[1])
    center_grad = summed[local_rows:]
    return (center_out, gens_out, offset, weight_grad, bias_grad, gens_grad, center_grad)


def solution(mesh):
    return jax.shard_map(
        body,
        mesh=mesh,
        in_specs=(
            P("box", "gen", None),
            P("box", None),
            P("gen", "neur"),
            P("neur"),
            P("box", "neur"),
            P("box", "gen", "neur"),
            P("box", "neur"),
            P("box", "neur"),
        ),
        out_specs=(
            P("box", "neur"),
            P("box", "gen", "neur"),
            P("box", "neur"),
            P("gen", "neur"),
            P("neur"),
            P("box", "gen", "neur"),
            P("box", "neur"),
        ),
        check_vma=False,
    )
```

profile of v0, /device:TPU:1, one launch (start us, length us, event | category | flops | bytes accessed | tf_op | source)
XLA Modules:
  0.0 343.2 jit_solution(5883826420351844935)
XLA Ops:
  7.2 0.0 all-gather.3.cloned.1.call-start
  7.2 0.7 all-gather.3.cloned.1.call-update
  7.9 0.0 reduce-scatter.3.cloned.1.call-start
  8.0 84.5 %all-gather.3.cloned.1.call-done = bf16[4096,512]{1,0:T(8,128)(2,1)} async-done(((bf16[1024,512]{1,0:T(8,128)(2,1)}), bf16[4096,512]{1,0:T(8,128)(2,1)}) %all-gather.3.cloned.1.call-update) | async-done | bytes 4194320 | tf_op jit(solution)/shard_map/all_gather | solution.py:23
  92.5 0.0 copy-start
  92.5 0.0 copy-start.2
  92.5 3.4 fusion.1
  95.9 0.0 copy-done.1
  95.9 0.1 fusion.4
  96.0 12.5 %all-reduce = (f32[4,512]{1,0:T(4,128)S(1)}, f32[4,512]{1,0:T(4,128)S(1)}) all-reduce(f32[4,512]{1,0:T(4,128)S(1)} %get-tuple-element.8, f32[4,512]{1,0:T(4,128)S(1)} %get-tuple-element.7), channel_id=1, replica_groups=mesh['gen'=4,'neur'=4,'box'=2] {'gen'}, use_global_device_ids=true, to_apply=%region_1.0 | all-reduce | flops 4096 | bytes 32768 | tf_op jit(solution)/shard_map/psum | solution.py:29
  108.4 0.0 copy-done.3
  108.4 0.0 copy-done.4
  108.4 0.0 copy-done.5
  108.4 0.0 copy-done.6
  108.6 0.8 fusion.3
  109.3 0.0 copy-done
  109.3 0.0 copy-done.2
  109.3 4.6 %fusion = f32[4096,512]{1,0:T(8,128)} fusion(bf16[4,4096]{1,0:T(4,128)(2,1)S(1)} %copy-done.2, bf16[128,4096]{1,0:T(8,128)(2,1)S(1)} %bitcast.13, bf16[4,512]{1,0:T(4,128)(2,1)S(1)} %get-tuple-element.16, bf16[128,512]{1,0:T(8,128)(2,1)S(1)} %bitcast.10), kind=kOutput, calls=%fused_computation.1 | convolution fusion | flops 556081152 | bytes 9605120 | tf_op jit(solution)/shard_map/dot_general | solution.py:46
  113.9 0.0 reduce-scatter.3.cloned.1.call-update
  113.9 0.0 reduce-scatter.5.cloned.1.call-start
  114.0 5.1 %fusion.7 = f32[132,4096]{1,0:T(8,128)} fusion(bf16[4096,512]{1,0:T(8,128)(2,1)} %all-gather.3.cloned.1.call-done, bf16[4,512]{1,0:T(4,128)(2,1)S(1)} %get-tuple-element.17, bf16[128,512]{1,0:T(8,128)(2,1)S(1)} %bitcast.11), kind=kOutput, calls=%fused_computation.12 | convolution fusion | flops 553918464 | bytes 6492160 | tf_op jit(solution)/shard_map/dot_general | solution.py:55
  119.0 0.0 reduce-scatter.5.cloned.1.call-update
  119.1 0.0 all-gather.5.cloned.1.call-start
  119.1 145.9 %reduce-scatter.3.cloned.1.call-done = f32[512,512]{1,0:T(8,128)} async-done(((f32[4096,512]{1,0:T(8,128)}), f32[512,512]{1,0:T(8,128)}) %reduce-scatter.3.cloned.1.call-update) | async-done | bytes 1048592 | tf_op jit(solution)/shard_map/reduce_scatter | solution.py:45
  265.0 0.0 all-gather.5.cloned.1.call-update
  265.1 4.4 %psum.23 = f32[512]{0:T(512)} all-reduce(f32[512]{0:T(512)S(1)} %get-tuple-element.11), channel_id=1, replica_groups=mesh['gen'=4,'neur'=4,'box'=2] {'box'}, use_global_device_ids=true, to_apply=%region_6.7 | all-reduce | flops 512 | bytes 4096 | tf_op jit(solution)/shard_map/psum | solution.py:54
  269.4 0.6 multiply_add_fusion.1
  270.0 28.9 %reduce-scatter.5.cloned.1.call-done = f32[132,1024]{1,0:T(8,128)} async-done(((f32[132,4096]{1,0:T(8,128)}), f32[132,1024]{1,0:T(8,128)}) %reduce-scatter.5.cloned.1.call-update) | async-done | bytes 540688 | tf_op jit(solution)/shard_map/reduce_scatter | solution.py:58
  299.0 1.4 slice.19
  300.4 1.9 slice.18
  302.2 31.3 %all-gather.5.cloned.1.call-done = f32[1024,512]{1,0:T(8,128)} async-done(((f32[512,512]{1,0:T(8,128)}), f32[1024,512]{1,0:T(8,128)}) %all-gather.5.cloned.1.call-update) | async-done | bytes 2097168 | tf_op jit(solution)/shard_map/all_gather | solution.py:53
  333.5 3.1 copy.16
  (9 shorter events, 0.1 us)
Async XLA Ops:
  7.2 85.3 %all-gather.3.cloned.1.call-start = ((), (), s32[]{:S(2)}) async-start(), calls=%async_computation.2 | async-start | bytes 5242880 | tf_op jit(solution)/shard_map/all_gather | solution.py:23
  7.9 257.1 %reduce-scatter.3.cloned.1.call-start = ((), (), s32[]{:S(2)}) async-start(), calls=%async_computation.3 | async-start | bytes 9437184 | tf_op jit(solution)/shard_map/reduce_scatter | solution.py:45
  92.5 3.4 copy-start.1
  92.5 16.0 %copy-start.3 = (f32[4,512]{1,0:T(4,128)S(1)}, f32[4,512]{1,0:T(4,128)}, u32[]{:S(2)}) copy-start(f32[4,512]{1,0:T(4,128)} %param.14) | copy-start | bytes 24580
  92.5 16.0 %copy-start.4 = (f32[4,512]{1,0:T(4,128)S(1)}, f32[4,512]{1,0:T(4,128)}, u32[]{:S(2)}) copy-start(f32[4,512]{1,0:T(4,128)} %param.15) | copy-start | bytes 24580
  92.5 16.0 %copy-start.5 = (s32[4,512]{1,0:T(4,128)S(1)}, s32[4,512]{1,0:T(4,128)}, u32[]{:S(2)}) copy-start(s32[4,512]{1,0:T(4,128)} %param.12) | copy-start | bytes 24580
  92.5 16.0 %copy-start.6 = (f32[512]{0:T(512)S(1)}, f32[512]{0:T(512)}, u32[]{:S(2)}) copy-start(f32[512]{0:T(512)} %param.11) | copy-start | bytes 6148
  92.5 16.9 %copy-start = (bf16[4,32,4096]{2,1,0:T(8,128)(2,1)S(1)}, bf16[4,32,4096]{2,1,0:T(8,128)(2,1)}, u32[]{:S(2)}) copy-start(bf16[4,32,4096]{2,1,0:T(8,128)(2,1)} %param.8) | copy-start | bytes 3145732
  92.5 16.8 %copy-start.2 = (bf16[4,4096]{1,0:T(4,128)(2,1)S(1)}, bf16[4,4096]{1,0:T(4,128)(2,1)}, u32[]{:S(2)}) copy-start(bf16[4,4096]{1,0:T(4,128)(2,1)} %param.9) | copy-start | bytes 98308
  113.9 185.1 %reduce-scatter.5.cloned.1.call-start = ((), (), s32[]{:S(2)}) async-start(), calls=%async_computation.5 | async-start | bytes 2785280 | tf_op jit(solution)/shard_map/reduce_scatter | solution.py:58
  119.1 214.5 %all-gather.5.cloned.1.call-start = ((), (), s32[]{:S(2)}) async-start(), calls=%async_computation.4 | async-start | bytes 3145728 | tf_op jit(solution)/shard_map/all_gather | solution.py:53
Sparse Core Ops, SparseCore 0:
  9.6 82.8 all-gather.2
  114.0 150.9 reduce-scatter.2
  267.8 31.1 reduce-scatter.4
  300.4 33.1 all-gather.4
where the time goes:
time: 344 us; the launch traced here: 343 us
  waiting for transfers between devices  291 us (85%)
  blocking collectives  16.8 us (5%)
  between operations  13.9 us (4%)
  matrix products  13 us (4%)
  local copies, waits for them, and re-layouts  6.35 us (2%)
    reduce_scatter x1, waiting for transfers between devices, body(): lax.psum_scatter(lax.dot_general(wide, back_owned, (((0,), (0,)), ((), ()...  146 us
    all_gather x1, waiting for transfers between devices, body(): full_weight = lax.all_gather(weight, 'gen', axis=0, tiled=True)  84.5 us
    all_gather x1, waiting for transfers between devices, body(): weight_grad = lax.all_gather(shares, 'box', axis=0, tiled=True)  31.3 us
    reduce_scatter x1, waiting for transfers between devices, body(): lax.psum_scatter(partial_back, 'neur', scatter_dimension=1, tiled=True)  28.9 us
    psum x1, blocking collectives, body(): radius = lax.psum(part_radius, 'gen')  12.5 us
  transfers between devices with their start and end apart: 4, of which 4 were waited for; matrix products, arithmetic and copies ran while one was open for 3% of the time, Pallas kernels for 0%

commit v1 on v0

v1 whole, which is shorter than its diff:
```python
import functools

import jax
import jax.numpy as jnp
from jax import lax
from jax.experimental import pallas as pl
from jax.experimental.pallas import tpu as pltpu
from jax.sharding import PartitionSpec as P

BF = jnp.bfloat16
F32 = jnp.float32
VMEM_LIMIT = 40 * 1024 * 1024


def neuron(center_pre, radius, phase):
    upper = center_pre + radius
    lower = center_pre - radius
    ratio = jnp.clip(upper / (upper - lower + 1e-05), 0.0, 1.0)
    active = (phase == 1).astype(center_pre.dtype)
    crossing = (phase == 2).astype(center_pre.dtype)
    slope = active + crossing * ratio
    offset = crossing * (-ratio * lower * 0.5)
    return (slope, slope * center_pre + offset, offset)


def general_body(gens, center, weight, bias, phase, gens_cot, center_cot, offset_cot):
    box_dev, gen_dev, width = gens.shape
    local_cols = weight.shape[1]
    local_rows = box_dev * gen_dev
    wide = jnp.concatenate([gens.reshape(local_rows, width), center], 0)
    full_weight = lax.all_gather(weight, "gen", axis=0, tiled=True)
    product = jnp.dot(wide, full_weight, preferred_element_type=F32)
    gen_pre = product[:local_rows].reshape(box_dev, gen_dev, local_cols)
    center_pre = product[local_rows:] + bias
    part_radius = jnp.sum(jnp.abs(gen_pre), axis=1)
    cot_wide = gens_cot.astype(F32)
    radius = lax.psum(part_radius, "gen")
    slope, center_out, offset = neuron(center_pre, radius, phase)
    gens_out = (slope[:, None, :] * gen_pre).astype(BF)
    intersection = lax.psum(jnp.sum(cot_wide * gen_pre, axis=1), "gen")
    unused, pull = jax.vjp(lambda a, b: neuron(a, b, phase), center_pre, radius)
    g_center, g_radius = pull((intersection, center_cot, offset_cot))
    gen_back = (slope[:, None, :] * cot_wide + jnp.sign(gen_pre) * g_radius[:, None, :]).astype(BF)
    center_back = g_center.astype(BF)
    back = jnp.concatenate([gen_back.reshape(local_rows, local_cols), center_back], 0)
    first_gen = (lax.axis_index("gen") == 0).astype(BF)
    back_owned = jnp.concatenate(
        [gen_back.reshape(local_rows, local_cols), center_back * first_gen], 0
    )
    shares = lax.psum_scatter(
        lax.dot_general(wide, back_owned, (((0,), (0,)), ((), ())), preferred_element_type=F32),
        ("gen", "box"),
        scatter_dimension=0,
        tiled=True,
    )
    weight_grad = lax.all_gather(shares, "box", axis=0, tiled=True)
    bias_grad = lax.psum(jnp.sum(g_center, axis=0), "box")
    partial_back = lax.dot_general(
        back, full_weight, (((1,), (1,)), ((), ())), preferred_element_type=F32
    )
    summed = lax.psum_scatter(partial_back, "neur", scatter_dimension=1, tiled=True)
    gens_grad = summed[:local_rows].reshape(box_dev, gen_dev, summed.shape[1])
    center_grad = summed[local_rows:]
    return (center_out, gens_out, offset, weight_grad, bias_grad, gens_grad, center_grad)


CENTER_ROWS = 16


def params():
    return pltpu.CompilerParams(vmem_limit_bytes=VMEM_LIMIT)


def cost(flops, nbytes):
    return pl.CostEstimate(flops=int(flops), bytes_accessed=int(nbytes), transcendentals=0)


def shape(dims, dtype):
    return jax.ShapeDtypeStruct(dims, dtype)


def whole(x):
    return pl.BlockSpec(x.shape, lambda i, s, r=len(x.shape): (0,) * r)


def call(kernel, scalars, args, specs, outs, est, scratch=()):
    return pl.pallas_call(
        kernel,
        grid_spec=pltpu.PrefetchScalarGridSpec(
            num_scalar_prefetch=1,
            grid=(1,),
            in_specs=specs,
            out_specs=[whole(o) for o in outs],
            scratch_shapes=list(scratch),
        ),
        out_shape=outs,
        compiler_params=params(),
        cost_estimate=est,
    )(scalars, *args)


def fold_kernel(n, s_ref, *refs):
    gens, cots, outs = refs[:n], refs[n : 2 * n], refs[2 * n :]
    for gen_ref, cot_ref, out in zip(gens, cots, outs):
        rows = gen_ref.shape[0] * gen_ref.shape[1]
        out[:rows, :] = gen_ref[...].reshape(rows, gen_ref.shape[2])
        cot = cot_ref[...].reshape(-1, cot_ref.shape[2])
        lanes = cot_ref.shape[2]
        per = out.shape[0] - rows
        for i in range(cot.shape[0] // per):
            out[rows:, i * lanes : (i + 1) * lanes] = cot[i * per : (i + 1) * per]


def forward_kernel(size, s_ref, gen_ref, cot_ref, center_ref, own_ref, oth_ref, *refs):
    g, c = s_ref[0], s_ref[1]
    recv, (a_ref, keep_ref, send_ref), parts = refs[: size - 1], refs[size - 1 : size + 2], refs[size + 2 :]
    boxes, per_gen, depth = gen_ref.shape
    rows = boxes * per_gen
    lanes = cot_ref.shape[2]
    for k in range(size):
        at = pl.ds(pl.multiple_of((g ^ k) * rows, rows), rows)
        if k == 0:
            a_ref[at, :] = gen_ref[...].reshape(rows, depth)
            keep_ref[at, :] = cot_ref[pl.ds(c * boxes, boxes)].reshape(rows, lanes)
            send_ref[at, :] = cot_ref[pl.ds((1 - c) * boxes, boxes)].reshape(rows, lanes)
        else:
            msg = recv[k - 1]
            a_ref[at, :] = msg[:rows, :]
            per = msg.shape[0] - rows
            cot = [msg[rows:, i * lanes : (i + 1) * lanes] for i in range(2 * rows // per)]
            low = jnp.concatenate(cot[: len(cot) // 2], 0)
            high = jnp.concatenate(cot[len(cot) // 2 :], 0)
            keep_ref[at, :] = jnp.where(c == 0, low, high)
            send_ref[at, :] = jnp.where(c == 0, high, low)
    mid = center_ref[...].astype(F32)
    mine = jnp.where(c == 0, mid[:boxes], mid[boxes:])
    pad = jnp.zeros((CENTER_ROWS - boxes, depth), F32)
    a_ref[size * rows :, :] = jnp.concatenate([mine, pad], 0).astype(BF)
    a = a_ref[...]
    for k in range(size):
        at = pl.ds(pl.multiple_of((g ^ k) * lanes, lanes), lanes)
        w = jnp.concatenate([own_ref[:, at], oth_ref[:, at]], 1)
        part = jnp.dot(a, w, preferred_element_type=F32)
        parts[k][...] = part[: parts[k].shape[0]]


def relax_kernel(size, boxes, s_ref, *refs):
    g = s_ref[0]
    parts, (keep_ref, got_ref, own_ref, oth_ref), outs = refs[:size], refs[size : size + 4], refs[size + 4 :]
    back_ref, go_ref, msgs = outs[0], outs[1], outs[2:-2]
    pre_ref, out_scratch = outs[-2], outs[-1]
    pre = parts[0][...]
    for p in parts[1:]:
        pre = pre + p[...]
    pre_ref[...] = pre
    rows = size * (go_ref.shape[0])
    per = go_ref.shape[0] // boxes
    cot = jnp.concatenate([keep_ref[...], got_ref[...]], 1).astype(F32)
    small = jnp.concatenate([own_ref[...], oth_ref[...]], 1)
    phase, center_cot, offset_cot = (small[i * boxes : (i + 1) * boxes] for i in range(3))
    bias = small[3 * boxes : 3 * boxes + 1]
    where = [[q * boxes * per + b * per for q in range(size)] for b in range(boxes)]
    radius, cross = [], []
    for b in range(boxes):
        radius.append(sum(jnp.sum(jnp.abs(pre[r : r + per]), 0, keepdims=True) for r in where[b]))
        cross.append(sum(jnp.sum(cot[r : r + per] * pre[r : r + per], 0, keepdims=True) for r in where[b]))
    radius, cross = jnp.concatenate(radius, 0), jnp.concatenate(cross, 0)
    center_pre = pre[rows : rows + boxes] + bias
    (slope, center_out, offset), pull = jax.vjp(lambda a, b: neuron(a, b, phase), center_pre, radius)
    g_center, g_radius = pull((cross, center_cot, offset_cot))
    for b in range(boxes):
        sl, gr = slope[b : b + 1], g_radius[b : b + 1]
        for r in where[b]:
            x = pre[r : r + per]
            sign = jnp.where(x > 0, gr, jnp.where(x < 0, -gr, 0.0))
            back_ref[r : r + per, :] = (sl * cot[r : r + per] + sign).astype(BF)
            out_scratch[r : r + per, :] = (sl * x).astype(BF)
    tail = []
    for value in (g_center, center_out, offset):
        high = value.astype(BF).astype(F32)
        tail += [high, value - high]
    tail.append(jnp.zeros((CENTER_ROWS - 6 * boxes, value.shape[1]), F32))
    back_ref[rows:, :] = jnp.concatenate(tail, 0).astype(BF)
    group = boxes * per
    go_ref[...] = out_scratch[pl.ds(pl.multiple_of(g * group, group), group), :]
    for k, msg in enumerate(msgs, 1):
        msg[: rows + CENTER_ROWS, :] = back_ref[...]
        at = pl.ds(pl.multiple_of((g ^ k) * group, group), group)
        msg[rows + CENTER_ROWS :, :] = out_scratch[at, :]


def spread_kernel(s_ref, back_ref, go_ref, *refs):
    g = s_ref[0]
    msgs, (own_ref, oth_ref) = refs[:-2], refs[-2:]
    rows, lanes = back_ref.shape[0], back_ref.shape[1] // 2
    for k in range(len(msgs) + 1):
        at = pl.ds(pl.multiple_of((g ^ k) * lanes, lanes), lanes)
        if k == 0:
            own_ref[:rows, at] = back_ref[:, :lanes]
            oth_ref[:rows, at] = back_ref[:, lanes:]
            own_ref[rows:, at] = go_ref[:, :lanes]
            oth_ref[rows:, at] = go_ref[:, lanes:]
        else:
            own_ref[:, at] = msgs[k - 1][:, :lanes]
            oth_ref[:, at] = msgs[k - 1][:, lanes:]


def input_grad_kernel(size, s_ref, own_ref, oth_ref, w_own_ref, w_oth_ref, *refs):
    n = s_ref[2]
    outs, res = refs[:-1], refs[-1]
    rows = res.shape[0]
    over = (((1,), (1,)), ((), ()))
    res[...] = lax.dot_general(
        own_ref[:rows, :], w_own_ref[...], over, preferred_element_type=F32
    ) + lax.dot_general(oth_ref[:rows, :], w_oth_ref[...], over, preferred_element_type=F32)
    group = (rows - CENTER_ROWS) // size
    tail = res[size * group : size * group + outs[0].shape[0] - group, :]
    for k, out in enumerate(outs):
        part = res[pl.ds(pl.multiple_of((n ^ k) * group, group), group), :]
        out[...] = jnp.concatenate([part, tail], 0).astype(BF)


def input_sum_kernel(s_ref, *refs):
    msgs, (grad_ref, center_ref) = refs[:-2], refs[-2:]
    c = s_ref[0] & 1
    boxes, per = grad_ref.shape[0] // 2, grad_ref.shape[1]
    group = boxes * per
    near = msgs[0][...].astype(F32) + msgs[2][...].astype(F32)
    far = msgs[1][...].astype(F32) + msgs[3][...].astype(F32)
    grad_ref[pl.ds(c * boxes, boxes)] = near[:group].reshape(boxes, per, -1)
    grad_ref[pl.ds((1 - c) * boxes, boxes)] = far[:group].reshape(boxes, per, -1)
    near, far = near[group : group + boxes], far[group : group + boxes]
    center_ref[...] = jnp.where(
        c == 0, jnp.concatenate([near, far], 0), jnp.concatenate([far, near], 0)
    )


def weight_grad_kernel(boxes, s_ref, *refs):
    lefts, rights, outs = refs[:4], refs[4:8], refs[8:]
    weight_ref, bias_ref, center_ref, offset_ref, gens_ref = outs
    rows = lefts[0].shape[0]
    total = None
    for left, right in zip(lefts, rights):
        part = lax.dot_general(
            left[...], right[:rows, :], (((0,), (0,)), ((), ())), preferred_element_type=F32
        )
        total = part if total is None else total + part
    weight_ref[...] = total

    @pl.when(pl.program_id(0) == 0)
    def _():
        c = s_ref[1]
        first = rows - CENTER_ROWS
        tails = [right[first:rows, :].astype(F32) for right in rights]
        bias_ref[...] = sum(jnp.sum(t[: 2 * boxes], 0, keepdims=True) for t in tails)
        for at, ref in ((2, center_ref), (4, offset_ref)):
            mine, other = (
                t[at * boxes : (at + 1) * boxes] + t[(at + 1) * boxes : (at + 2) * boxes] for t in tails[:2]
            )
            ref[...] = jnp.where(
                c == 0, jnp.concatenate([mine, other], 0), jnp.concatenate([other, mine], 0)
            )
        per = gens_ref.shape[1]
        gens_ref[pl.ds(c * boxes, boxes)] = rights[0][rows:, :].reshape(boxes, per, -1)
        gens_ref[pl.ds((1 - c) * boxes, boxes)] = rights[1][rows:, :].reshape(boxes, per, -1)


def square_body(size, gens, center, weight, bias, phase, gens_cot, center_cot, offset_cot):
    box_dev, per_gen, width = gens.shape
    depth, cols = weight.shape
    boxes = box_dev // 2
    group = boxes * per_gen
    rows = size * group
    lanes = cols // size
    g, n = lax.axis_index("gen"), lax.axis_index("neur")
    c = n % 2
    scalars = jnp.stack([g, c, n]).astype(jnp.int32)

    def over_gen(x, k):
        return lax.ppermute(x, "gen", [(i, i ^ k) for i in range(size)])

    def over_core(x):
        return lax.ppermute(x, "neur", [(i, i ^ 1) for i in range(size)])

    def over_box(x):
        return lax.ppermute(x, "box", [(0, 1), (1, 0)])

    def turned(x, k):
        pairs = [(i * size + j, (j ^ k) * size + i) for i in range(size) for j in range(size)]
        return lax.ppermute(x, ("gen", "neur"), pairs)

    def gens_spec(k):
        return pl.BlockSpec((boxes, per_gen, depth), lambda i, s: (s[1], 0, s[0] ^ k))

    def cot_spec(k):
        return pl.BlockSpec((box_dev, per_gen, lanes), lambda i, s: (0, 0, s[0] ^ k))

    others = range(1, size)
    with jax.named_scope("exchange_generators"):
        cot_rows = box_dev * per_gen * lanes // depth
        msgs = call(
            functools.partial(fold_kernel, size - 1),
            scalars,
            [gens] * (size - 1) + [gens_cot] * (size - 1),
            [gens_spec(k) for k in others] + [cot_spec(k) for k in others],
            [shape((group + cot_rows, depth), BF)] * (size - 1),
            cost(0, 1 << 20),
        )
        recv = [over_gen(m, k) for k, m in zip(others, msgs)]
    with jax.named_scope("swap_cores"):
        w_other = over_core(weight)
        stacked = jnp.stack([phase.astype(F32), center_cot, offset_cot])

        def small(core):
            part = lax.dynamic_slice_in_dim(stacked, core * boxes, boxes, 1)
            return jnp.concatenate(
                [part.reshape(3 * boxes, cols), bias[None], jnp.zeros((8 - 3 * boxes - 1, cols), F32)], 0
            )

        small_own = small(c)
        small_oth = over_core(small(1 - c))
    with jax.named_scope("forward"):
        res = call(
            functools.partial(forward_kernel, size),
            scalars,
            [gens, gens_cot, center, weight, w_other, *recv],
            [
                gens_spec(0),
                cot_spec(0),
                pl.BlockSpec((box_dev, depth), lambda i, s: (0, s[0])),
                whole(weight),
                whole(w_other),
                *[whole(r) for r in recv],
            ],
            [
                shape((rows + CENTER_ROWS, depth), BF),
                shape((rows, lanes), BF),
                shape((rows, lanes), BF),
                *[shape((rows + 8, 2 * lanes), F32)] * size,
            ],
            cost(2 * rows * depth * 2 * cols, 4 << 20),
        )
        a_own, cot_keep, cot_send, *parts = res
    with jax.named_scope("sum_products"):
        sums = [parts[0]] + [over_gen(parts[k], k) for k in others]
        cot_got = over_core(cot_send)
    with jax.named_scope("share_generators"):
        a_core = over_core(a_own)
        a_box = over_box(a_own)
        a_box_core = over_core(a_box)
    with jax.named_scope("relax"):
        small_spec = pl.BlockSpec((8, lanes), lambda i, s: (0, s[0]))
        back, go, *msgs = call(
            functools.partial(relax_kernel, size, boxes),
            scalars,
            [*sums, cot_keep, cot_got, small_own, small_oth],
            [*[whole(p) for p in sums], whole(cot_keep), whole(cot_got), small_spec, small_spec],
            [
                shape((rows + CENTER_ROWS, 2 * lanes), BF),
                shape((group, 2 * lanes), BF),
                *[shape((rows + CENTER_ROWS + group, 2 * lanes), BF)] * (size - 1),
            ],
            cost(rows * lanes * 20, 2 << 20),
            [pltpu.VMEM((rows + 8, 2 * lanes), F32), pltpu.VMEM((rows, 2 * lanes), BF)],
        )
    with jax.named_scope("exchange_back"):
        recv = [over_gen(m, k) for k, m in zip(others, msgs)]
        b_own, b_oth = call(
            spread_kernel,
            scalars,
            [back, go, *recv],
            [whole(back), whole(go), *[whole(r) for r in recv]],
            [shape((rows + CENTER_ROWS + group, cols), BF)] * 2,
            cost(0, 2 << 20),
        )
        b_core = over_core(b_oth)
        b_box = over_box(b_own[: rows + CENTER_ROWS])
        b_box_core = over_box(b_core[: rows + CENTER_ROWS])
    with jax.named_scope("input_gradient"):
        msgs = call(
            functools.partial(input_grad_kernel, size),
            scalars,
            [b_own, b_oth, weight, w_other],
            [whole(b_own), whole(b_oth), whole(weight), whole(w_other)],
            [shape((group + 8, depth), BF)] * size,
            cost(2 * rows * depth * 2 * cols, 4 << 20),
            [pltpu.VMEM((rows + CENTER_ROWS, depth), F32)],
        )
        recv = [turned(m, k) for k, m in enumerate(msgs)]
        gens_grad, center_grad = call(
            input_sum_kernel,
            scalars,
            recv,
            [whole(r) for r in recv],
            [shape((box_dev, per_gen, depth), F32), shape((box_dev, depth), F32)],
            cost(0, 2 << 20),
        )
    with jax.named_scope("weight_gradient"):
        blocks = 4
        lefts, rights = [a_own, a_core, a_box, a_box_core], [b_own, b_core, b_box, b_box_core]
        left_spec = pl.BlockSpec((rows + CENTER_ROWS, depth // blocks), lambda i, s: (0, i))
        weight_grad, bias_grad, center_out, offset, gens_out = pl.pallas_call(
            functools.partial(weight_grad_kernel, boxes),
            grid_spec=pltpu.PrefetchScalarGridSpec(
                num_scalar_prefetch=1,
                grid=(blocks,),
                in_specs=[left_spec] * 4 + [whole(r) for r in rights],
                out_specs=[
                    pl.BlockSpec((depth // blocks, cols), lambda i, s: (i, 0)),
                    whole(shape((1, cols), F32)),
                    whole(shape((box_dev, cols), F32)),
                    whole(shape((box_dev, cols), F32)),
                    whole(shape((box_dev, per_gen, cols), BF)),
                ],
            ),
            out_shape=[
                shape((depth, cols), F32),
                shape((1, cols), F32),
                shape((box_dev, cols), F32),
                shape((box_dev, cols), F32),
                shape((box_dev, per_gen, cols), BF),
            ],
            compiler_params=params(),
            cost_estimate=cost(2 * 4 * rows * depth * cols, 6 << 20),
        )(scalars, *lefts, *rights)
    return (
        center_out,
        gens_out,
        offset,
        weight_grad,
        bias_grad.reshape(cols),
        gens_grad,
        center_grad,
    )


def solution(mesh):
    sizes = dict(mesh.shape)

    def run(gens, center, weight, bias, phase, gens_cot, center_cot, offset_cot):
        size = sizes["gen"]
        box_dev = gens.shape[0] // sizes["box"]
        per_gen = gens.shape[1] // size
        cols = weight.shape[1] // sizes["neur"]
        square = (
            size == sizes["neur"] == 4
            and sizes["box"] == 2
            and box_dev == 4
            and per_gen % 16 == 0
            and cols % (128 * size) == 0
            and weight.shape[0] % (1024 * size) == 0
        )
        body = functools.partial(square_body, size) if square else general_body
        return jax.shard_map(
            body,
            mesh=mesh,
            in_specs=(
                P("box", "gen", None),
                P("box", None),
                P("gen", "neur"),
                P("neur"),
                P("box", "neur"),
                P("box", "gen", "neur"),
                P("box", "neur"),
                P("box", "neur"),
            ),
            out_specs=(
                P("box", "neur"),
                P("box", "gen", "neur"),
                P("box", "neur"),
                P("gen", "neur"),
                P("neur"),
                P("box", "gen", "neur"),
                P("box", "neur"),
            ),
            check_vma=False,
        )(gens, center, weight, bias, phase, gens_cot, center_cot, offset_cot)

    return run
```

time: 344 us -> 106 us (0.31)
  the two profiles are of different devices: /device:TPU:1 before, /device:TPU:2 now
where the time goes in v1:
time: 106 us; the launch traced here: 105 us
  waiting for transfers between devices  59.9 us (57%)
  starting transfers between devices  29.5 us (28%)
  Pallas kernels  12.7 us (12%)
  local copies, waits for them, and re-layouts  2.32 us (2%)
    ppermute x9, waiting for transfers between devices, over_gen(): return lax.ppermute(x, 'gen', [(i, i ^ k) for i in range(size)])  39.6 us
    ppermute x4, waiting for transfers between devices, turned(): return lax.ppermute(x, ('gen', 'neur'), pairs)  18 us
    ppermute x9, starting transfers between devices, over_gen(): return lax.ppermute(x, 'gen', [(i, i ^ k) for i in range(size)])  17.3 us
    pallas_call x6, Pallas kernels, call(): pl.pallas_call(kernel, grid_spec=pltpu.PrefetchScalarGridSpec(num_scalar_...  7.87 us
    ppermute x4, starting transfers between devices, turned(): return lax.ppermute(x, ('gen', 'neur'), pairs)  6.74 us
    pallas_call x1, Pallas kernels, square_body(): pl.pallas_call(functools.partial(weight_grad_kernel, boxes), grid_spec=pl...  4.81 us
    ppermute x3, starting transfers between devices, over_box(): return lax.ppermute(x, 'box', [(0, 1), (1, 0)])  4.54 us
    ppermute x6, waiting for transfers between devices, over_core(): return lax.ppermute(x, 'neur', [(i, i ^ 1) for i in range(size)])  2.27 us
  transfers between devices with their start and end apart: 22, of which 11 were waited for; matrix products, arithmetic and copies ran while one was open for 0% of the time, Pallas kernels for 5%

profile of v1, /device:TPU:2, one launch (start us, length us, event | category | flops | bytes accessed | tf_op | source)
XLA Modules:
  0.0 105.4 jit_solution(4740872921706264377)
XLA Ops:
  0.8 1.2 %copy-done = bf16[4,32,4096]{2,1,0:T(8,128)(2,1)S(1)} copy-done((bf16[4,32,4096]{2,1,0:T(8,128)(2,1)S(1)}, bf16[4,32,4096]{2,1,0:T(8,128)(2,1)}, u32[]{:S(2)}) %copy-start) | copy-done | bytes 1048600
  2.1 0.9 copy-done.3
  3.0 1.3 %exchange_generators.1 = (bf16[80,1024]{1,0:T(8,128)(2,1)}, bf16[80,1024]{1,0:T(8,128)(2,1)}, bf16[80,1024]{1,0:T(8,128)(2,1)}) custom-call(s32[3]{0:T(128)S(1)} %pad_add_fusion.s_ref, bf16[4,32,4096]{2,1,0:T(8,128)(2,1)S(1)} %copy-done, bf16[4,32,4096]{2,1,0:T(8,128)(2,1)S(1)} %copy-done, bf16[4,32,4096]{2,1,0:T(8,128)(2,1)S(1)} %copy-done, ...), custom_call_target="tpu_custom_call" | custom-call | bytes 1048576 | tf_op jit(solution)/shard_map/exchange_generators/pallas_call | solution.py:87
  4.3 1.6 %collective-permute-start.1 = (bf16[80,1024]{1,0:T(8,128)(2,1)}, bf16[80,1024]{1,0:T(8,128)(2,1)S(1)}, u32[]{:S(2)}, u32[]{:S(2)}) collective-permute-start(bf16[80,1024]{1,0:T(8,128)(2,1)} %get-tuple-element.35), channel_id=1, source_target_pairs={{0,8},{8,0},{16,24},{24,16},{1,9},{9,1},{17,25},{25,17},{2,10},{10... | collective-permute-start | bytes 491528 | tf_op jit(solution)/shard_map/exchange_generators/ppermute | solution.py:280
  5.9 2.6 %collective-permute-start.2 = (bf16[80,1024]{1,0:T(8,128)(2,1)}, bf16[80,1024]{1,0:T(8,128)(2,1)}, u32[]{:S(2)}, u32[]{:S(2)}) collective-permute-start(bf16[80,1024]{1,0:T(8,128)(2,1)} %get-tuple-element.36), channel_id=1, source_target_pairs={{0,16},{8,24},{16,0},{24,8},{1,17},{9,25},{17,1},{25,9},{2,18},{10... | collective-permute-start | bytes 491528 | tf_op jit(solution)/shard_map/exchange_generators/ppermute | solution.py:280
  8.9 5.3 %collective-permute-done.1.refs_0_ = bf16[80,1024]{1,0:T(8,128)(2,1)S(1)} collective-permute-done((bf16[80,1024]{1,0:T(8,128)(2,1)}, bf16[80,1024]{1,0:T(8,128)(2,1)S(1)}, u32[]{:S(2)}, u32[]{:S(2)}) %collective-permute-start.1) | collective-permute-done | bytes 163872 | tf_op jit(solution)/shard_map/exchange_generators/ppermute | solution.py:280
  14.2 7.0 %collective-permute-done.2.refs_1_ = bf16[80,1024]{1,0:T(8,128)(2,1)} collective-permute-done((bf16[80,1024]{1,0:T(8,128)(2,1)}, bf16[80,1024]{1,0:T(8,128)(2,1)}, u32[]{:S(2)}, u32[]{:S(2)}) %collective-permute-start.2) | collective-permute-done | bytes 163872 | tf_op jit(solution)/shard_map/exchange_generators/ppermute | solution.py:280
  21.3 2.3 %forward.1 = (bf16[272,1024]{1,0:T(8,128)(2,1)S(1)}, bf16[256,128]{1,0:T(8,128)(2,1)S(1)}, bf16[256,128]{1,0:T(8,128)(2,1)S(1)}, f32[264,256]{1,0:T(8,128)S(1)},...) custom-call(s32[3]{0:T(128)S(1)} %pad_add_fusion.s_ref, ...), custom_call_target="tpu_custom_call" | custom-call | flops 536870912 | bytes 4194304 | tf_op jit(solution)/shard_map/forward/pallas_call | solution.py:87
  23.6 3.4 %collective-permute-start.7 = (f32[264,256]{1,0:T(8,128)S(1)}, f32[264,256]{1,0:T(8,128)S(1)}, u32[]{:S(2)}, u32[]{:S(2)}) collective-permute-start(f32[264,256]{1,0:T(8,128)S(1)} %get-tuple-element.40), channel_id=1, source_target_pairs={{0,8},{8,0},{16,24},{24,16},{1,9},{9,1},{17,25},{25,17},{2,10},{10... | collective-permute-start | bytes 811016 | tf_op jit(solution)/shard_map/sum_products/ppermute | solution.py:280
  27.0 1.1 %collective-permute-start.8 = (f32[264,256]{1,0:T(8,128)S(1)}, f32[264,256]{1,0:T(8,128)S(1)}, u32[]{:S(2)}, u32[]{:S(2)}) collective-permute-start(f32[264,256]{1,0:T(8,128)S(1)} %get-tuple-element.41), channel_id=1, source_target_pairs={{0,16},{8,24},{16,0},{24,8},{1,17},{9,25},{17,1},{25,9},{2,18},{10... | collective-permute-start | bytes 811016 | tf_op jit(solution)/shard_map/sum_products/ppermute | solution.py:280
  28.1 1.4 %collective-permute-start.9 = (f32[264,256]{1,0:T(8,128)S(1)}, f32[264,256]{1,0:T(8,128)S(1)}, u32[]{:S(2)}, u32[]{:S(2)}) collective-permute-start(f32[264,256]{1,0:T(8,128)S(1)} %get-tuple-element.42), channel_id=1, source_target_pairs={{0,24},{8,16},{16,8},{24,0},{1,25},{9,17},{17,9},{25,1},{2,26},{10... | collective-permute-start | bytes 811016 | tf_op jit(solution)/shard_map/sum_products/ppermute | solution.py:280
  29.5 1.5 %collective-permute-start.5 = (bf16[272,1024]{1,0:T(8,128)(2,1)S(1)}, bf16[272,1024]{1,0:T(8,128)(2,1)S(1)}, u32[]{:S(2)}, u32[]{:S(2)}) collective-permute-start(bf16[272,1024]{1,0:T(8,128)(2,1)S(1)} %get-tuple-element.38.refs_0_), channel_id=1, source_target_pairs={{0,1},{1,0},{2,3},{3,2},{4,5},{5,4},{6,7},{7,6},{8,9},{9,8},{10,11... | collective-permute-start | bytes 1671176 | tf_op jit(solution)/shard_map/share_generators/ppermute | solution.py:286
  31.1 1.2 %collective-permute-done.11.refs_7_ = f32[8,512]{1,0:T(8,128)S(1)} collective-permute-done((f32[8,512]{1,0:T(8,128)S(1)}, f32[8,512]{1,0:T(8,128)S(1)}, u32[]{:S(2)}, u32[]{:S(2)}) %collective-permute-start.11) | collective-permute-done | bytes 16416 | tf_op jit(solution)/shard_map/swap_cores/ppermute | solution.py:283
  32.4 1.1 %collective-permute-done.10.refs_5_ = bf16[256,128]{1,0:T(8,128)(2,1)S(1)} collective-permute-done((bf16[256,128]{1,0:T(8,128)(2,1)S(1)}, bf16[256,128]{1,0:T(8,128)(2,1)S(1)}, u32[]{:S(2)}, u32[]{:S(2)}) %collective-permute-start.10) | collective-permute-done | bytes 65568 | tf_op jit(solution)/shard_map/sum_products/ppermute | solution.py:283
  33.5 4.3 %collective-permute-done.7.refs_1_ = f32[264,256]{1,0:T(8,128)S(1)} collective-permute-done((f32[264,256]{1,0:T(8,128)S(1)}, f32[264,256]{1,0:T(8,128)S(1)}, u32[]{:S(2)}, u32[]{:S(2)}) %collective-permute-start.7) | collective-permute-done | bytes 270368 | tf_op jit(solution)/shard_map/sum_products/ppermute | solution.py:280
  37.8 11.1 %collective-permute-done.8.refs_2_ = f32[264,256]{1,0:T(8,128)S(1)} collective-permute-done((f32[264,256]{1,0:T(8,128)S(1)}, f32[264,256]{1,0:T(8,128)S(1)}, u32[]{:S(2)}, u32[]{:S(2)}) %collective-permute-start.8) | collective-permute-done | bytes 270368 | tf_op jit(solution)/shard_map/sum_products/ppermute | solution.py:280
  48.9 0.8 relax.1
  49.7 4.5 %collective-permute-start.12 = (bf16[336,256]{1,0:T(8,128)(2,1)S(1)}, bf16[336,256]{1,0:T(8,128)(2,1)S(1)}, u32[]{:S(2)}, u32[]{:S(2)}) collective-permute-start(bf16[336,256]{1,0:T(8,128)(2,1)S(1)} %get-tuple-element.47), channel_id=1, source_target_pairs={{0,8},{8,0},{16,24},{24,16},{1,9},{9,1},{17,25},{25,17},{2,10},{10... | collective-permute-start | bytes 516104 | tf_op jit(solution)/shard_map/exchange_back/ppermute | solution.py:280
  54.2 1.1 %collective-permute-start.13 = (bf16[336,256]{1,0:T(8,128)(2,1)S(1)}, bf16[336,256]{1,0:T(8,128)(2,1)S(1)}, u32[]{:S(2)}, u32[]{:S(2)}) collective-permute-start(bf16[336,256]{1,0:T(8,128)(2,1)S(1)} %get-tuple-element.48), channel_id=1, source_target_pairs={{0,16},{8,24},{16,0},{24,8},{1,17},{9,25},{17,1},{25,9},{2,18},{10... | collective-permute-start | bytes 516104 | tf_op jit(solution)/shard_map/exchange_back/ppermute | solution.py:280
  55.3 1.4 %collective-permute-start.14 = (bf16[336,256]{1,0:T(8,128)(2,1)S(1)}, bf16[336,256]{1,0:T(8,128)(2,1)S(1)}, u32[]{:S(2)}, u32[]{:S(2)}) collective-permute-start(bf16[336,256]{1,0:T(8,128)(2,1)S(1)} %get-tuple-element.49), channel_id=1, source_target_pairs={{0,24},{8,16},{16,8},{24,0},{1,25},{9,17},{17,9},{25,1},{2,26},{10... | collective-permute-start | bytes 516104 | tf_op jit(solution)/shard_map/exchange_back/ppermute | solution.py:280
  56.7 2.8 %collective-permute-done.12.refs_0_ = bf16[336,256]{1,0:T(8,128)(2,1)S(1)} collective-permute-done((bf16[336,256]{1,0:T(8,128)(2,1)S(1)}, bf16[336,256]{1,0:T(8,128)(2,1)S(1)}, u32[]{:S(2)}, u32[]{:S(2)}) %collective-permute-start.12) | collective-permute-done | bytes 172064 | tf_op jit(solution)/shard_map/exchange_back/ppermute | solution.py:280
  59.5 9.1 %collective-permute-done.13.refs_1_ = bf16[336,256]{1,0:T(8,128)(2,1)S(1)} collective-permute-done((bf16[336,256]{1,0:T(8,128)(2,1)S(1)}, bf16[336,256]{1,0:T(8,128)(2,1)S(1)}, u32[]{:S(2)}, u32[]{:S(2)}) %collective-permute-start.13) | collective-permute-done | bytes 172064 | tf_op jit(solution)/shard_map/exchange_back/ppermute | solution.py:280
  69.9 1.4 %input_gradient.2 = (bf16[72,1024]{1,0:T(8,128)(2,1)S(1)}, bf16[72,1024]{1,0:T(8,128)(2,1)S(1)}, bf16[72,1024]{1,0:T(8,128)(2,1)S(1)}, bf16[72,1024]{1,0:T(8,128)(2,1)S(1)}) custom-call(s32[3]{0:T(128)S(1)} %pad_add_fusion.s_ref, bf16[336,512]{1,0:T(8,128)(2,1)S(1)} %get-tuple-element.50.refs_4_.own_ref, bf16[336,512]{1,0:T(8,128)(2,1)S(1)} %get-tuple-element.51.oth_ref, ...), custom_call_target="tpu_custom_call" | custom-call | flops 536870912 | bytes 4194304 | tf_op jit(solution)/shard_map/input_gradient/pallas_call | solution.py:87
  71.3 5.3 %collective-permute-start.18 = (bf16[72,1024]{1,0:T(8,128)(2,1)S(1)}, bf16[72,1024]{1,0:T(8,128)(2,1)S(1)}, u32[]{:S(2)}, u32[]{:S(2)}) collective-permute-start(bf16[72,1024]{1,0:T(8,128)(2,1)S(1)} %get-tuple-element.57), channel_id=1, source_target_pairs={{0,0},{2,8},{4,16},{6,24},{8,2},{10,10},{12,18},{14,26},{16,4},{18... | collective-permute-start | bytes 442376 | tf_op jit(solution)/shard_map/input_gradient/ppermute | solution.py:290
  76.6 1.4 %collective-permute-start.19 = (bf16[72,1024]{1,0:T(8,128)(2,1)S(1)}, bf16[72,1024]{1,0:T(8,128)(2,1)S(1)}, u32[]{:S(2)}, u32[]{:S(2)}) collective-permute-start(bf16[72,1024]{1,0:T(8,128)(2,1)S(1)} %get-tuple-element.58), channel_id=1, source_target_pairs={{0,8},{2,0},{4,24},{6,16},{8,10},{10,2},{12,26},{14,18},{16,12},{1... | collective-permute-start | bytes 442376 | tf_op jit(solution)/shard_map/input_gradient/ppermute | solution.py:290
  78.1 9.7 %collective-permute-done.18.refs_0_ = bf16[72,1024]{1,0:T(8,128)(2,1)S(1)} collective-permute-done((bf16[72,1024]{1,0:T(8,128)(2,1)S(1)}, bf16[72,1024]{1,0:T(8,128)(2,1)S(1)}, u32[]{:S(2)}, u32[]{:S(2)}) %collective-permute-start.18) | collective-permute-done | bytes 147488 | tf_op jit(solution)/shard_map/input_gradient/ppermute | solution.py:290
  87.7 1.5 %collective-permute-start.16 = (bf16[272,512]{1,0:T(8,128)(2,1)S(1)}, bf16[272,512]{1,0:T(8,128)(2,1)S(1)}, u32[]{:S(2)}, u32[]{:S(2)}) collective-permute-start(bf16[272,512]{1,0:T(8,128)(2,1)S(1)} %slice.6), channel_id=1, source_target_pairs={{0,1},{1,0},{2,3},{3,2},{4,5},{5,4},{6,7},{7,6},{8,9},{9,8},{10,11... | collective-permute-start | bytes 835592 | tf_op jit(solution)/shard_map/exchange_back/ppermute | solution.py:286
  89.3 1.9 %collective-permute-done.19.refs_1_ = bf16[72,1024]{1,0:T(8,128)(2,1)S(1)} collective-permute-done((bf16[72,1024]{1,0:T(8,128)(2,1)S(1)}, bf16[72,1024]{1,0:T(8,128)(2,1)S(1)}, u32[]{:S(2)}, u32[]{:S(2)}) %collective-permute-start.19) | collective-permute-done | bytes 147488 | tf_op jit(solution)/shard_map/input_gradient/ppermute | solution.py:290
  91.2 1.5 %collective-permute-start.17 = (bf16[272,512]{1,0:T(8,128)(2,1)S(1)}, bf16[272,512]{1,0:T(8,128)(2,1)S(1)}, u32[]{:S(2)}, u32[]{:S(2)}) collective-permute-start(bf16[272,512]{1,0:T(8,128)(2,1)S(1)} %slice.8), channel_id=1, source_target_pairs={{0,1},{1,0},{2,3},{3,2},{4,5},{5,4},{6,7},{7,6},{8,9},{9,8},{10,11... | collective-permute-start | bytes 835592 | tf_op jit(solution)/shard_map/exchange_back/ppermute | solution.py:286
  92.7 6.4 %collective-permute-done.21.refs_3_ = bf16[72,1024]{1,0:T(8,128)(2,1)S(1)} collective-permute-done((bf16[72,1024]{1,0:T(8,128)(2,1)S(1)}, bf16[72,1024]{1,0:T(8,128)(2,1)S(1)}, u32[]{:S(2)}, u32[]{:S(2)}) %collective-permute-start.21) | collective-permute-done | bytes 147488 | tf_op jit(solution)/shard_map/input_gradient/ppermute | solution.py:290
  99.1 1.4 %input_gradient.3 = (f32[4,32,1024]{2,1,0:T(8,128)}, f32[4,1024]{1,0:T(4,128)}) custom-call(s32[3]{0:T(128)S(1)} %pad_add_fusion.s_ref, bf16[72,1024]{1,0:T(8,128)(2,1)S(1)} %collective-permute-done.18.refs_0_, bf16[72,1024]{1,0:T(8,128)(2,1)S(1)} %collective-permute-done.19.refs_1_, bf16[72,1024]{1,0:T(8,128)(2,1)S(1)} %collective-permute-done.20.refs_2_, ...), custom_call_target="tpu_custom_call" | custom-call | bytes 2097152 | tf_op jit(solution)/shard_map/input_gradient/pallas_call | solution.py:87
  100.5 4.8 %weight_gradient.1 = (f32[1024,512]{1,0:T(8,128)}, f32[1,512]{1,0:T(1,128)}, f32[4,512]{1,0:T(4,128)}, f32[4,512]{1,0:T(4,128)}, bf16[4,32,512]{2,1,0:T(8,128)(2,1)}) custom-call(s32[3]{0:T(128)S(1)} %pad_add_fusion.s_ref, bf16[272,1024]{1,0:T(8,128)(2,1)S(1)} %get-tuple-element.38.refs_0_, bf16[272,1024]{1,0:T(8,128)(2,1)S(1)} %collective-permute-done.4.refs_1_, ...), custom_call_target="tpu_custom_call" | custom-call | flops 1073741824 | bytes 6291456 | tf_op jit(solution)/shard_map/weight_gradient/pallas_call | solution.py:402
  (49 shorter events, 2.2 us)
Async XLA Ops:
  0.6 8.1 %copy-start.6 = (s32[4,512]{1,0:T(4,128)S(1)}, s32[4,512]{1,0:T(4,128)}, u32[]{:S(2)}) copy-start(s32[4,512]{1,0:T(4,128)} %param.12) | copy-start | bytes 24580
  0.6 20.6 %copy-start.5 = (bf16[4,4096]{1,0:T(4,128)(2,1)S(1)}, bf16[4,4096]{1,0:T(4,128)(2,1)}, u32[]{:S(2)}) copy-start(bf16[4,4096]{1,0:T(4,128)(2,1)} %center_ref.1) | copy-start | bytes 98308
  0.7 20.6 %collective-permute-start = (bf16[1024,512]{1,0:T(8,128)(2,1)}, bf16[1024,512]{1,0:T(8,128)(2,1)S(1)}, u32[]{:S(2)}, u32[]{:S(2)}) collective-permute-start(bf16[1024,512]{1,0:T(8,128)(2,1)} %w_own_ref.1), channel_id=1, source_target_pairs={{0,2},{2,0},{4,6},{6,4},{1,3},{3,1},{5,7},{7,5},{8,10},{10,8},{12,... | collective-permute-start | bytes 3145736 | tf_op jit(solution)/shard_map/swap_cores/ppermute | solution.py:283
  0.8 1.2 %copy-start = (bf16[4,32,4096]{2,1,0:T(8,128)(2,1)S(1)}, bf16[4,32,4096]{2,1,0:T(8,128)(2,1)}, u32[]{:S(2)}) copy-start(bf16[4,32,4096]{2,1,0:T(8,128)(2,1)} %gen_ref.1) | copy-start | bytes 3145732
  2.0 0.9 copy-start.3
  3.0 5.8 %copy-start.7 = (f32[4,512]{1,0:T(4,128)S(1)}, f32[4,512]{1,0:T(4,128)}, u32[]{:S(2)}) copy-start(f32[4,512]{1,0:T(4,128)} %param.15) | copy-start | bytes 24580
  3.0 5.8 %copy-start.8 = (f32[4,512]{1,0:T(4,128)S(1)}, f32[4,512]{1,0:T(4,128)}, u32[]{:S(2)}) copy-start(f32[4,512]{1,0:T(4,128)} %param.14) | copy-start | bytes 24580
  3.0 18.3 %copy-start.1 = (bf16[4,32,4096]{2,1,0:T(8,128)(2,1)S(1)}, bf16[4,32,4096]{2,1,0:T(8,128)(2,1)}, u32[]{:S(2)}) copy-start(bf16[4,32,4096]{2,1,0:T(8,128)(2,1)} %gen_ref.1) | copy-start | bytes 3145732
  3.0 18.3 %copy-start.2 = (bf16[1024,512]{1,0:T(8,128)(2,1)S(1)}, bf16[1024,512]{1,0:T(8,128)(2,1)}, u32[]{:S(2)}) copy-start(bf16[1024,512]{1,0:T(8,128)(2,1)} %w_own_ref.1) | copy-start | bytes 3145732
  3.0 18.3 %copy-start.4 = (bf16[4,32,512]{2,1,0:T(8,128)(2,1)S(1)}, bf16[4,32,512]{2,1,0:T(8,128)(2,1)}, u32[]{:S(2)}) copy-start(bf16[4,32,512]{2,1,0:T(8,128)(2,1)} %cot_ref.1) | copy-start | bytes 393220
  4.3 26.7 %copy-start.9 = (f32[512]{0:T(512)S(1)}, f32[512]{0:T(512)}, u32[]{:S(2)}) copy-start(f32[512]{0:T(512)} %param.11) | copy-start | bytes 6148
  4.3 9.9 %collective-permute-start.1 = (bf16[80,1024]{1,0:T(8,128)(2,1)}, bf16[80,1024]{1,0:T(8,128)(2,1)S(1)}, u32[]{:S(2)}, u32[]{:S(2)}) collective-permute-start(bf16[80,1024]{1,0:T(8,128)(2,1)} %get-tuple-element.35), channel_id=1, source_target_pairs={{0,8},{8,0},{16,24},{24,16},{1,9},{9,1},{17,25},{25,17},{2,10},{10... | collective-permute-start | bytes 491528 | tf_op jit(solution)/shard_map/exchange_generators/ppermute | solution.py:280
  5.9 15.3 %collective-permute-start.2 = (bf16[80,1024]{1,0:T(8,128)(2,1)}, bf16[80,1024]{1,0:T(8,128)(2,1)}, u32[]{:S(2)}, u32[]{:S(2)}) collective-permute-start(bf16[80,1024]{1,0:T(8,128)(2,1)} %get-tuple-element.36), channel_id=1, source_target_pairs={{0,16},{8,24},{16,0},{24,8},{1,17},{9,25},{17,1},{25,9},{2,18},{10... | collective-permute-start | bytes 491528 | tf_op jit(solution)/shard_map/exchange_generators/ppermute | solution.py:280
  8.5 12.7 %collective-permute-start.3 = (bf16[80,1024]{1,0:T(8,128)(2,1)}, bf16[80,1024]{1,0:T(8,128)(2,1)}, u32[]{:S(2)}, u32[]{:S(2)}) collective-permute-start(bf16[80,1024]{1,0:T(8,128)(2,1)} %get-tuple-element.37), channel_id=1, source_target_pairs={{0,24},{8,16},{16,8},{24,0},{1,25},{9,17},{17,9},{25,1},{2,26},{10... | collective-permute-start | bytes 491528 | tf_op jit(solution)/shard_map/exchange_generators/ppermute | solution.py:280
  23.6 14.2 %collective-permute-start.7 = (f32[264,256]{1,0:T(8,128)S(1)}, f32[264,256]{1,0:T(8,128)S(1)}, u32[]{:S(2)}, u32[]{:S(2)}) collective-permute-start(f32[264,256]{1,0:T(8,128)S(1)} %get-tuple-element.40), channel_id=1, source_target_pairs={{0,8},{8,0},{16,24},{24,16},{1,9},{9,1},{17,25},{25,17},{2,10},{10... | collective-permute-start | bytes 811016 | tf_op jit(solution)/shard_map/sum_products/ppermute | solution.py:280
  27.0 21.9 %collective-permute-start.8 = (f32[264,256]{1,0:T(8,128)S(1)}, f32[264,256]{1,0:T(8,128)S(1)}, u32[]{:S(2)}, u32[]{:S(2)}) collective-permute-start(f32[264,256]{1,0:T(8,128)S(1)} %get-tuple-element.41), channel_id=1, source_target_pairs={{0,16},{8,24},{16,0},{24,8},{1,17},{9,25},{17,1},{25,9},{2,18},{10... | collective-permute-start | bytes 811016 | tf_op jit(solution)/shard_map/sum_products/ppermute | solution.py:280
  28.1 20.8 %collective-permute-start.9 = (f32[264,256]{1,0:T(8,128)S(1)}, f32[264,256]{1,0:T(8,128)S(1)}, u32[]{:S(2)}, u32[]{:S(2)}) collective-permute-start(f32[264,256]{1,0:T(8,128)S(1)} %get-tuple-element.42), channel_id=1, source_target_pairs={{0,24},{8,16},{16,8},{24,0},{1,25},{9,17},{17,9},{25,1},{2,26},{10... | collective-permute-start | bytes 811016 | tf_op jit(solution)/shard_map/sum_products/ppermute | solution.py:280
  29.5 40.4 %collective-permute-start.5 = (bf16[272,1024]{1,0:T(8,128)(2,1)S(1)}, bf16[272,1024]{1,0:T(8,128)(2,1)S(1)}, u32[]{:S(2)}, u32[]{:S(2)}) collective-permute-start(bf16[272,1024]{1,0:T(8,128)(2,1)S(1)} %get-tuple-element.38.refs_0_), channel_id=1, source_target_pairs={{0,1},{1,0},{2,3},{3,2},{4,5},{5,4},{6,7},{7,6},{8,9},{9,8},{10,11... | collective-permute-start | bytes 1671176 | tf_op jit(solution)/shard_map/share_generators/ppermute | solution.py:286
  31.1 1.2 %collective-permute-start.11 = (f32[8,512]{1,0:T(8,128)S(1)}, f32[8,512]{1,0:T(8,128)S(1)}, u32[]{:S(2)}, u32[]{:S(2)}) collective-permute-start(f32[8,512]{1,0:T(8,128)S(1)} %get-tuple-element.65), channel_id=1, source_target_pairs={{0,2},{2,0},{4,6},{6,4},{1,3},{3,1},{5,7},{7,5},{8,10},{10,8},{12,... | collective-permute-start | bytes 49160 | tf_op jit(solution)/shard_map/swap_cores/ppermute | solution.py:283
  32.3 1.3 %collective-permute-start.10 = (bf16[256,128]{1,0:T(8,128)(2,1)S(1)}, bf16[256,128]{1,0:T(8,128)(2,1)S(1)}, u32[]{:S(2)}, u32[]{:S(2)}) collective-permute-start(bf16[256,128]{1,0:T(8,128)(2,1)S(1)} %get-tuple-element.44), channel_id=1, source_target_pairs={{0,2},{2,0},{4,6},{6,4},{1,3},{3,1},{5,7},{7,5},{8,10},{10,8},{12,... | collective-permute-start | bytes 196616 | tf_op jit(solution)/shard_map/sum_products/ppermute | solution.py:283
  49.7 9.8 %collective-permute-start.12 = (bf16[336,256]{1,0:T(8,128)(2,1)S(1)}, bf16[336,256]{1,0:T(8,128)(2,1)S(1)}, u32[]{:S(2)}, u32[]{:S(2)}) collective-permute-start(bf16[336,256]{1,0:T(8,128)(2,1)S(1)} %get-tuple-element.47), channel_id=1, source_target_pairs={{0,8},{8,0},{16,24},{24,16},{1,9},{9,1},{17,25},{25,17},{2,10},{10... | collective-permute-start | bytes 516104 | tf_op jit(solution)/shard_map/exchange_back/ppermute | solution.py:280
  54.2 14.3 %collective-permute-start.13 = (bf16[336,256]{1,0:T(8,128)(2,1)S(1)}, bf16[336,256]{1,0:T(8,128)(2,1)S(1)}, u32[]{:S(2)}, u32[]{:S(2)}) collective-permute-start(bf16[336,256]{1,0:T(8,128)(2,1)S(1)} %get-tuple-element.48), channel_id=1, source_target_pairs={{0,16},{8,24},{16,0},{24,8},{1,17},{9,25},{17,1},{25,9},{2,18},{10... | collective-permute-start | bytes 516104 | tf_op jit(solution)/shard_map/exchange_back/ppermute | solution.py:280
  55.3 13.3 %collective-permute-start.14 = (bf16[336,256]{1,0:T(8,128)(2,1)S(1)}, bf16[336,256]{1,0:T(8,128)(2,1)S(1)}, u32[]{:S(2)}, u32[]{:S(2)}) collective-permute-start(bf16[336,256]{1,0:T(8,128)(2,1)S(1)} %get-tuple-element.49), channel_id=1, source_target_pairs={{0,24},{8,16},{16,8},{24,0},{1,25},{9,17},{17,9},{25,1},{2,26},{10... | collective-permute-start | bytes 516104 | tf_op jit(solution)/shard_map/exchange_back/ppermute | solution.py:280
  69.3 8.8 %collective-permute-start.15 = (bf16[336,512]{1,0:T(8,128)(2,1)S(1)}, bf16[336,512]{1,0:T(8,128)(2,1)S(1)}, u32[]{:S(2)}, u32[]{:S(2)}) collective-permute-start(bf16[336,512]{1,0:T(8,128)(2,1)S(1)} %get-tuple-element.51.oth_ref), channel_id=1, source_target_pairs={{0,2},{2,0},{4,6},{6,4},{1,3},{3,1},{5,7},{7,5},{8,10},{10,8},{12,... | collective-permute-start | bytes 1032200 | tf_op jit(solution)/shard_map/exchange_back/ppermute | solution.py:283
  69.3 31.2 %collective-permute-start.4 = (bf16[272,1024]{1,0:T(8,128)(2,1)S(1)}, bf16[272,1024]{1,0:T(8,128)(2,1)S(1)}, u32[]{:S(2)}, u32[]{:S(2)}) collective-permute-start(bf16[272,1024]{1,0:T(8,128)(2,1)S(1)} %get-tuple-element.38.refs_0_), channel_id=1, source_target_pairs={{0,2},{2,0},{4,6},{6,4},{1,3},{3,1},{5,7},{7,5},{8,10},{10,8},{12,... | collective-permute-start | bytes 1671176 | tf_op jit(solution)/shard_map/share_generators/ppermute | solution.py:283
  69.8 30.7 %collective-permute-start.6 = (bf16[272,1024]{1,0:T(8,128)(2,1)S(1)}, bf16[272,1024]{1,0:T(8,128)(2,1)S(1)}, u32[]{:S(2)}, u32[]{:S(2)}) collective-permute-start(bf16[272,1024]{1,0:T(8,128)(2,1)S(1)} %collective-permute-done.5.refs_2_), channel_id=1, source_target_pairs={{0,2},{2,0},{4,6},{6,4},{1,3},{3,1},{5,7},{7,5},{8,10},{10,8},{12,... | collective-permute-start | bytes 1671176 | tf_op jit(solution)/shard_map/share_generators/ppermute | solution.py:283
  71.3 16.5 %collective-permute-start.18 = (bf16[72,1024]{1,0:T(8,128)(2,1)S(1)}, bf16[72,1024]{1,0:T(8,128)(2,1)S(1)}, u32[]{:S(2)}, u32[]{:S(2)}) collective-permute-start(bf16[72,1024]{1,0:T(8,128)(2,1)S(1)} %get-tuple-element.57), channel_id=1, source_target_pairs={{0,0},{2,8},{4,16},{6,24},{8,2},{10,10},{12,18},{14,26},{16,4},{18... | collective-permute-start | bytes 442376 | tf_op jit(solution)/shard_map/input_gradient/ppermute | solution.py:290
  76.6 14.6 %collective-permute-start.19 = (bf16[72,1024]{1,0:T(8,128)(2,1)S(1)}, bf16[72,1024]{1,0:T(8,128)(2,1)S(1)}, u32[]{:S(2)}, u32[]{:S(2)}) collective-permute-start(bf16[72,1024]{1,0:T(8,128)(2,1)S(1)} %get-tuple-element.58), channel_id=1, source_target_pairs={{0,8},{2,0},{4,24},{6,16},{8,10},{10,2},{12,26},{14,18},{16,12},{1... | collective-permute-start | bytes 442376 | tf_op jit(solution)/shard_map/input_gradient/ppermute | solution.py:290
  78.0 14.7 %collective-permute-start.20 = (bf16[72,1024]{1,0:T(8,128)(2,1)S(1)}, bf16[72,1024]{1,0:T(8,128)(2,1)S(1)}, u32[]{:S(2)}, u32[]{:S(2)}) collective-permute-start(bf16[72,1024]{1,0:T(8,128)(2,1)S(1)} %get-tuple-element.59), channel_id=1, source_target_pairs={{0,16},{2,24},{4,0},{6,8},{8,18},{10,26},{12,2},{14,10},{16,20},{1... | collective-permute-start | bytes 442376 | tf_op jit(solution)/shard_map/input_gradient/ppermute | solution.py:290
  87.7 12.8 %collective-permute-start.16 = (bf16[272,512]{1,0:T(8,128)(2,1)S(1)}, bf16[272,512]{1,0:T(8,128)(2,1)S(1)}, u32[]{:S(2)}, u32[]{:S(2)}) collective-permute-start(bf16[272,512]{1,0:T(8,128)(2,1)S(1)} %slice.6), channel_id=1, source_target_pairs={{0,1},{1,0},{2,3},{3,2},{4,5},{5,4},{6,7},{7,6},{8,9},{9,8},{10,11... | collective-permute-start | bytes 835592 | tf_op jit(solution)/shard_map/exchange_back/ppermute | solution.py:286
  91.2 9.4 %collective-permute-start.17 = (bf16[272,512]{1,0:T(8,128)(2,1)S(1)}, bf16[272,512]{1,0:T(8,128)(2,1)S(1)}, u32[]{:S(2)}, u32[]{:S(2)}) collective-permute-start(bf16[272,512]{1,0:T(8,128)(2,1)S(1)} %slice.8), channel_id=1, source_target_pairs={{0,1},{1,0},{2,3},{3,2},{4,5},{5,4},{6,7},{7,6},{8,9},{9,8},{10,11... | collective-permute-start | bytes 835592 | tf_op jit(solution)/shard_map/exchange_back/ppermute | solution.py:286
  92.7 6.4 %collective-permute-start.21 = (bf16[72,1024]{1,0:T(8,128)(2,1)S(1)}, bf16[72,1024]{1,0:T(8,128)(2,1)S(1)}, u32[]{:S(2)}, u32[]{:S(2)}) collective-permute-start(bf16[72,1024]{1,0:T(8,128)(2,1)S(1)} %get-tuple-element.60), channel_id=1, source_target_pairs={{0,24},{2,16},{4,8},{6,0},{8,26},{10,18},{12,10},{14,2},{16,28},{1... | collective-permute-start | bytes 442376 | tf_op jit(solution)/shard_map/input_gradient/ppermute | solution.py:290

commit v2 on v1

v2 whole, which is shorter than its diff:
```python
import functools

import jax
import jax.numpy as jnp
from jax import lax
from jax.experimental import pallas as pl
from jax.experimental.pallas import tpu as pltpu
from jax.sharding import PartitionSpec as P

BF = jnp.bfloat16
F32 = jnp.float32
VMEM_LIMIT = 40 * 1024 * 1024


def neuron(center_pre, radius, phase):
    upper = center_pre + radius
    lower = center_pre - radius
    ratio = jnp.clip(upper / (upper - lower + 1e-05), 0.0, 1.0)
    active = (phase == 1).astype(center_pre.dtype)
    crossing = (phase == 2).astype(center_pre.dtype)
    slope = active + crossing * ratio
    offset = crossing * (-ratio * lower * 0.5)
    return (slope, slope * center_pre + offset, offset)


def general_body(gens, center, weight, bias, phase, gens_cot, center_cot, offset_cot):
    box_dev, gen_dev, width = gens.shape
    local_cols = weight.shape[1]
    local_rows = box_dev * gen_dev
    wide = jnp.concatenate([gens.reshape(local_rows, width), center], 0)
    full_weight = lax.all_gather(weight, "gen", axis=0, tiled=True)
    product = jnp.dot(wide, full_weight, preferred_element_type=F32)
    gen_pre = product[:local_rows].reshape(box_dev, gen_dev, local_cols)
    center_pre = product[local_rows:] + bias
    part_radius = jnp.sum(jnp.abs(gen_pre), axis=1)
    cot_wide = gens_cot.astype(F32)
    radius = lax.psum(part_radius, "gen")
    slope, center_out, offset = neuron(center_pre, radius, phase)
    gens_out = (slope[:, None, :] * gen_pre).astype(BF)
    intersection = lax.psum(jnp.sum(cot_wide * gen_pre, axis=1), "gen")
    unused, pull = jax.vjp(lambda a, b: neuron(a, b, phase), center_pre, radius)
    g_center, g_radius = pull((intersection, center_cot, offset_cot))
    gen_back = (slope[:, None, :] * cot_wide + jnp.sign(gen_pre) * g_radius[:, None, :]).astype(BF)
    center_back = g_center.astype(BF)
    back = jnp.concatenate([gen_back.reshape(local_rows, local_cols), center_back], 0)
    first_gen = (lax.axis_index("gen") == 0).astype(BF)
    back_owned = jnp.concatenate(
        [gen_back.reshape(local_rows, local_cols), center_back * first_gen], 0
    )
    shares = lax.psum_scatter(
        lax.dot_general(wide, back_owned, (((0,), (0,)), ((), ())), preferred_element_type=F32),
        ("gen", "box"),
        scatter_dimension=0,
        tiled=True,
    )
    weight_grad = lax.all_gather(shares, "box", axis=0, tiled=True)
    bias_grad = lax.psum(jnp.sum(g_center, axis=0), "box")
    partial_back = lax.dot_general(
        back, full_weight, (((1,), (1,)), ((), ())), preferred_element_type=F32
    )
    summed = lax.psum_scatter(partial_back, "neur", scatter_dimension=1, tiled=True)
    gens_grad = summed[:local_rows].reshape(box_dev, gen_dev, summed.shape[1])
    center_grad = summed[local_rows:]
    return (center_out, gens_out, offset, weight_grad, bias_grad, gens_grad, center_grad)


CENTER_ROWS = 16
HALVES = 2


def params():
    return pltpu.CompilerParams(vmem_limit_bytes=VMEM_LIMIT)


def cost(flops, nbytes):
    return pl.CostEstimate(flops=int(flops), bytes_accessed=int(nbytes), transcendentals=0)


def shape(dims, dtype):
    return jax.ShapeDtypeStruct(dims, dtype)


def whole(x):
    return pl.BlockSpec(x.shape, lambda i, s, r=len(x.shape): (0,) * r)


def call(kernel, scalars, args, specs, outs, est, scratch=()):
    return pl.pallas_call(
        kernel,
        grid_spec=pltpu.PrefetchScalarGridSpec(
            num_scalar_prefetch=1,
            grid=(1,),
            in_specs=specs,
            out_specs=[whole(o) for o in outs],
            scratch_shapes=list(scratch),
        ),
        out_shape=outs,
        compiler_params=params(),
        cost_estimate=est,
    )(scalars, *args)


def rows_at(index, size):
    return pl.ds(pl.multiple_of(index * size, size), size)


def fold_kernel(partners, s_ref, *refs):
    gens, cots, outs = refs[: partners * HALVES], refs[partners * HALVES : partners * (HALVES + 1)], refs[partners * (HALVES + 1) :]
    for gen_ref, out in zip(gens, outs):
        rows = gen_ref.shape[0] * gen_ref.shape[1]
        out[:rows, :] = gen_ref[...].reshape(rows, gen_ref.shape[2])
    for cot_ref, out in zip(cots, outs[partners * (HALVES - 1) :]):
        cot = cot_ref[...].reshape(-1, cot_ref.shape[2])
        lanes = cot_ref.shape[2]
        per = out.shape[0] - rows
        for i in range(cot.shape[0] // per):
            out[rows:, i * lanes : (i + 1) * lanes] = cot[i * per : (i + 1) * per]


def forward_kernel(size, part, s_ref, gen_ref, center_ref, own_ref, oth_ref, *refs):
    g, c = s_ref[0], s_ref[1]
    recv, refs = refs[: size - 1], refs[size - 1 :]
    boxes, per_gen, depth = gen_ref.shape
    rows = boxes * per_gen
    if part == HALVES - 1:
        cot_ref, a_ref, keep_ref, send_ref, *products = refs
    else:
        cot_ref, (a_ref, *products) = None, refs
    for k in range(size):
        at = rows_at(g ^ k, rows)
        a_ref[at, :] = gen_ref[...].reshape(rows, depth) if k == 0 else recv[k - 1][:rows, :]
    mid = center_ref[...].astype(F32)
    half = mid.shape[0] // 2
    mine = jnp.where(c == 0, mid[:half], mid[half:])[part * boxes : (part + 1) * boxes]
    pad = jnp.zeros((CENTER_ROWS - boxes, depth), F32)
    a_ref[size * rows :, :] = jnp.concatenate([mine, pad], 0).astype(BF)
    a = a_ref[...]
    lanes = products[0].shape[1] // 2
    for k in range(size):
        at = rows_at(g ^ k, lanes)
        w = jnp.concatenate([own_ref[:, at], oth_ref[:, at]], 1)
        product = jnp.dot(a, w, preferred_element_type=F32)
        products[k][...] = product[: products[k].shape[0]]
    if cot_ref is None:
        return
    for k in range(size):
        if k == 0:
            cot = cot_ref[...].reshape(-1, lanes)
        else:
            msg = recv[k - 1]
            cot = jnp.concatenate(
                [msg[rows:, i * lanes : (i + 1) * lanes] for i in range(depth // lanes)], 0
            )
        low, high = cot[: HALVES * rows], cot[HALVES * rows :]
        for ref, value in (
            (keep_ref, jnp.where(c == 0, low, high)),
            (send_ref, jnp.where(c == 0, high, low)),
        ):
            for h in range(HALVES):
                at = pl.ds(pl.multiple_of(h * size * rows + (g ^ k) * rows, rows), rows)
                ref[at, :] = value[h * rows : (h + 1) * rows]


def relax_kernel(size, boxes, part, s_ref, *refs):
    g = s_ref[0]
    sums, (keep_ref, got_ref, own_ref, oth_ref), outs = refs[:size], refs[size : size + 4], refs[size + 4 :]
    back_ref, go_ref, msgs, out_scratch = outs[0], outs[1], outs[2:-1], outs[-1]
    pre = sums[0][...]
    for p in sums[1:]:
        pre = pre + p[...]
    group = go_ref.shape[0]
    rows, per = size * group, group // boxes
    cot = jnp.concatenate([keep_ref[...], got_ref[...]], 1).astype(F32)
    small = jnp.concatenate([own_ref[...], oth_ref[...]], 1)
    step = HALVES * boxes
    phase, center_cot, offset_cot = (
        small[i * step + part * boxes : i * step + (part + 1) * boxes] for i in range(3)
    )
    bias = small[3 * step : 3 * step + 1]
    where = [[q * group + b * per for q in range(size)] for b in range(boxes)]
    radius, cross = [], []
    for b in range(boxes):
        radius.append(sum(jnp.sum(jnp.abs(pre[r : r + per]), 0, keepdims=True) for r in where[b]))
        cross.append(sum(jnp.sum(cot[r : r + per] * pre[r : r + per], 0, keepdims=True) for r in where[b]))
    radius, cross = jnp.concatenate(radius, 0), jnp.concatenate(cross, 0)
    center_pre = pre[rows : rows + boxes] + bias
    (slope, center_out, offset), pull = jax.vjp(lambda a, b: neuron(a, b, phase), center_pre, radius)
    g_center, g_radius = pull((cross, center_cot, offset_cot))
    for b in range(boxes):
        sl, gr = slope[b : b + 1], g_radius[b : b + 1]
        for r in where[b]:
            x = pre[r : r + per]
            sign = jnp.where(x > 0, gr, jnp.where(x < 0, -gr, 0.0))
            back_ref[r : r + per, :] = (sl * cot[r : r + per] + sign).astype(BF)
            out_scratch[r : r + per, :] = (sl * x).astype(BF)
    tail = []
    for value in (g_center, center_out, offset):
        high = value.astype(BF).astype(F32)
        tail += [high, value - high]
    tail.append(jnp.zeros((CENTER_ROWS - 6 * boxes, value.shape[1]), F32))
    back_ref[rows:, :] = jnp.concatenate(tail, 0).astype(BF)
    go_ref[...] = out_scratch[rows_at(g, group), :]
    for k, msg in enumerate(msgs, 1):
        msg[: rows + CENTER_ROWS, :] = back_ref[...]
        msg[rows + CENTER_ROWS :, :] = out_scratch[rows_at(g ^ k, group), :]


def spread_kernel(s_ref, back_ref, go_ref, *refs):
    g = s_ref[0]
    msgs, (own_ref, oth_ref) = refs[:-2], refs[-2:]
    rows, lanes = back_ref.shape[0], back_ref.shape[1] // 2
    for k in range(len(msgs) + 1):
        at = rows_at(g ^ k, lanes)
        if k == 0:
            own_ref[:rows, at] = back_ref[:, :lanes]
            oth_ref[:rows, at] = back_ref[:, lanes:]
            own_ref[rows:, at] = go_ref[:, :lanes]
            oth_ref[rows:, at] = go_ref[:, lanes:]
        else:
            own_ref[:, at] = msgs[k - 1][:, :lanes]
            oth_ref[:, at] = msgs[k - 1][:, lanes:]


def input_grad_kernel(size, s_ref, own_ref, oth_ref, w_own_ref, w_oth_ref, send_ref, keep_ref, res):
    x = s_ref[2] >> 1
    rows = res.shape[0]
    over = (((1,), (1,)), ((), ()))
    res[...] = lax.dot_general(
        own_ref[:rows, :], w_own_ref[...], over, preferred_element_type=F32
    ) + lax.dot_general(oth_ref[:rows, :], w_oth_ref[...], over, preferred_element_type=F32)
    group = (rows - CENTER_ROWS) // size
    tail = res[size * group : size * group + 8, :]
    for ref, at in ((send_ref, 1 - x), (keep_ref, x)):
        parts = [res[rows_at(at, group), :], res[rows_at(at + 2, group), :], tail]
        ref[...] = jnp.concatenate(parts, 0).astype(ref.dtype)


def input_pair_kernel(s_ref, keep_ref, got_ref, *refs):
    outs, total = refs[:-1], refs[-1]
    c = s_ref[1]
    total[...] = keep_ref[...] + got_ref[...].astype(F32)
    group = (total.shape[0] - 8) // 2
    tail = total[2 * group :, :]
    for k, out in enumerate(outs):
        out[...] = jnp.concatenate([total[rows_at(c ^ k, group), :], tail], 0).astype(BF)


def input_final_kernel(boxes, s_ref, *refs):
    msgs, (grad_ref, center_ref) = refs[: 2 * HALVES], refs[-2:]
    first = s_ref[0] >> 1
    per = grad_ref.shape[1]
    group = boxes * per
    rows = [[], []]
    for h in range(HALVES):
        for k in range(2):
            value = msgs[2 * h + k][...].astype(F32)
            at = (first ^ k) * (HALVES * boxes) + h * boxes
            grad_ref[pl.ds(at, boxes)] = value[:group].reshape(boxes, per, -1)
            rows[k].append(value[group : group + boxes])
    near, far = (jnp.concatenate(r, 0) for r in rows)
    center_ref[...] = jnp.where(
        first == 0, jnp.concatenate([near, far], 0), jnp.concatenate([far, near], 0)
    )


def stack_kernel(*refs):
    lefts, out = refs[:-1], refs[-1]
    rows = lefts[0].shape[0] // HALVES
    gens = rows - CENTER_ROWS
    tails = []
    for i in range(len(lefts) * HALVES):
        ref, h = lefts[i // HALVES], i % HALVES
        out[:, i * gens : (i + 1) * gens] = ref[h * rows : h * rows + gens, :].T
        tails.append(ref[h * rows + gens : (h + 1) * rows, :])
    out[:, len(tails) * gens :] = jnp.concatenate(tails, 0).T


def weight_grad_kernel(boxes, s_ref, left_ref, *refs):
    rights, refs = refs[: 4 * HALVES], refs[4 * HALVES :]
    weight_ref, bias_ref, center_ref, offset_ref, gens_ref, stack = refs
    per = gens_ref.shape[1]
    gens = (left_ref.shape[1] - len(rights) * CENTER_ROWS) // len(rights)

    @pl.when(pl.program_id(0) == 0)
    def _():
        c = s_ref[1]
        tails = []
        for i, right in enumerate(rights):
            stack[i * gens : (i + 1) * gens, :] = right[:gens, :]
            tail = right[gens : gens + CENTER_ROWS, :]
            at = len(rights) * gens + i * CENTER_ROWS
            stack[at : at + CENTER_ROWS, :] = tail
            tails.append(tail.astype(F32))
        bias_ref[...] = sum(jnp.sum(t[: 2 * boxes], 0, keepdims=True) for t in tails)
        for at, ref in ((2, center_ref), (4, offset_ref)):
            both = [
                t[at * boxes : (at + 1) * boxes] + t[(at + 1) * boxes : (at + 2) * boxes]
                for t in tails[: 2 * HALVES]
            ]
            mine, other = (jnp.concatenate(both[i * HALVES : (i + 1) * HALVES], 0) for i in range(2))
            ref[...] = jnp.where(
                c == 0, jnp.concatenate([mine, other], 0), jnp.concatenate([other, mine], 0)
            )
        for i in range(2):
            for h in range(HALVES):
                at = (c ^ i) * (HALVES * boxes) + h * boxes
                out = rights[i * HALVES + h][gens + CENTER_ROWS :, :]
                gens_ref[pl.ds(at, boxes)] = out.reshape(boxes, per, -1)

    weight_ref[...] = jnp.dot(left_ref[...], stack[...], preferred_element_type=F32)


def square_body(size, gens, center, weight, bias, phase, gens_cot, center_cot, offset_cot):
    box_dev, per_gen, width = gens.shape
    depth, cols = weight.shape
    core_boxes = box_dev // 2
    boxes = core_boxes // HALVES
    group = boxes * per_gen
    rows = size * group
    work = rows + CENTER_ROWS
    lanes = cols // size
    g, n = lax.axis_index("gen"), lax.axis_index("neur")
    c = n % 2
    scalars = jnp.stack([g, c, n]).astype(jnp.int32)
    halves, others = range(HALVES), range(1, size)

    def over_gen(x, k):
        return lax.ppermute(x, "gen", [(i, i ^ k) for i in range(size)])

    def over_core(x):
        return lax.ppermute(x, "neur", [(i, i ^ 1) for i in range(size)])

    def over_x(x):
        return lax.ppermute(x, "neur", [(i, i ^ 2) for i in range(size)])

    def over_box(x):
        return lax.ppermute(x, "box", [(0, 1), (1, 0)])

    def turned(x, k):
        pairs = [
            (i * size + j, ((j >> 1) + 2 * ((j & 1) ^ k)) * size + i)
            for i in range(size)
            for j in range(size)
        ]
        return lax.ppermute(x, ("gen", "neur"), pairs)

    def gens_spec(k, h):
        return pl.BlockSpec(
            (boxes, per_gen, depth), lambda i, s: (s[1] * HALVES + h, 0, s[0] ^ k)
        )

    def cot_spec(k):
        return pl.BlockSpec((box_dev, per_gen, lanes), lambda i, s: (0, 0, s[0] ^ k))

    with jax.named_scope("exchange_generators"):
        cot_rows = box_dev * per_gen * lanes // depth
        msgs = call(
            functools.partial(fold_kernel, size - 1),
            scalars,
            [gens] * ((size - 1) * HALVES) + [gens_cot] * (size - 1),
            [gens_spec(k, h) for h in halves for k in others] + [cot_spec(k) for k in others],
            [
                shape((group + (cot_rows if h == HALVES - 1 else 0), depth), BF)
                for h in halves
                for k in others
            ],
            cost(0, 1 << 20),
        )
        recv = [
            [over_gen(msgs[h * (size - 1) + k - 1], k) for k in others] for h in halves
        ]
    with jax.named_scope("swap_cores"):
        w_other = over_core(weight)
        stacked = jnp.stack([phase.astype(F32), center_cot, offset_cot])

        def small(core):
            part = lax.dynamic_slice_in_dim(stacked, core * core_boxes, core_boxes, 1)
            pad = jnp.zeros((8 - 3 * core_boxes - 1, cols), F32)
            return jnp.concatenate([part.reshape(3 * core_boxes, cols), bias[None], pad], 0)

        small_own = small(c)
        small_oth = over_core(small(1 - c))
    lefts, sums = [], []
    for h in halves:
        last = h == HALVES - 1
        with jax.named_scope("forward"):
            a_part, *res = call(
                functools.partial(forward_kernel, size, h),
                scalars,
                [gens, center, weight, w_other, *recv[h]] + [gens_cot] * last,
                [
                    gens_spec(0, h),
                    pl.BlockSpec((box_dev, depth), lambda i, s: (0, s[0])),
                    whole(weight),
                    whole(w_other),
                    *[whole(r) for r in recv[h]],
                ]
                + [cot_spec(0)] * last,
                [shape((work, depth), BF)]
                + [shape((HALVES * rows, lanes), BF)] * (2 * last)
                + [shape((rows + 8, 2 * lanes), F32)] * size,
                cost(2 * rows * depth * 2 * cols, 4 << 20),
            )
            if last:
                cot_keep, cot_send, *res = res
        lefts.append(a_part)
        with jax.named_scope("sum_products"):
            sums.append([res[0]] + [over_gen(res[k], k) for k in others])
    cot_got = over_core(cot_send)
    with jax.named_scope("share_generators"):
        a_own = jnp.concatenate(lefts, 0)
        a_core = over_core(a_own)
        a_box = over_box(a_own)
        a_box_core = over_core(a_box)
        pieces = [a_own, a_core, a_box, a_box_core]
        left = pl.pallas_call(
            stack_kernel,
            out_shape=shape((depth, 4 * HALVES * work), BF),
            compiler_params=params(),
            cost_estimate=cost(0, 5 << 20),
        )(*pieces)
    rights, finals = [[], [], [], []], []
    small_spec = pl.BlockSpec((8, lanes), lambda i, s: (0, s[0]))
    for h in halves:
        cot_part = pl.BlockSpec((rows, lanes), lambda i, s, h=h: (h, 0))
        with jax.named_scope("relax"):
            back, go, *msgs = call(
                functools.partial(relax_kernel, size, boxes, h),
                scalars,
                [*sums[h], cot_keep, cot_got, small_own, small_oth],
                [*[whole(p) for p in sums[h]], cot_part, cot_part, small_spec, small_spec],
                [
                    shape((work, 2 * lanes), BF),
                    shape((group, 2 * lanes), BF),
                    *[shape((work + group, 2 * lanes), BF)] * (size - 1),
                ],
                cost(rows * lanes * 20, 2 << 20),
                [pltpu.VMEM((rows, 2 * lanes), BF)],
            )
        with jax.named_scope("exchange_back"):
            got = [over_gen(m, k) for k, m in zip(others, msgs)]
            b_own, b_oth = call(
                spread_kernel,
                scalars,
                [back, go, *got],
                [whole(back), whole(go), *[whole(r) for r in got]],
                [shape((work + group, cols), BF)] * 2,
                cost(0, 2 << 20),
            )
            b_core = over_core(b_oth)
            b_box = over_box(b_own[:work])
            b_box_core = over_box(b_core[:work])
            for right, piece in zip(rights, (b_own, b_core, b_box, b_box_core)):
                right.append(piece)
        with jax.named_scope("input_gradient"):
            both = 2 * group + 8
            send, keep = call(
                functools.partial(input_grad_kernel, size),
                scalars,
                [b_own, b_oth, weight, w_other],
                [whole(b_own), whole(b_oth), whole(weight), whole(w_other)],
                [shape((both, depth), BF), shape((both, depth), F32)],
                cost(2 * rows * depth * 2 * cols, 4 << 20),
                [pltpu.VMEM((work, depth), F32)],
            )
            far = over_x(send)
            msgs = call(
                input_pair_kernel,
                scalars,
                [keep, far],
                [whole(keep), whole(far)],
                [shape((group + 8, depth), BF)] * 2,
                cost(0, 1 << 20),
                [pltpu.VMEM((both, depth), F32)],
            )
            finals += [turned(m, k) for k, m in enumerate(msgs)]
    with jax.named_scope("weight_gradient"):
        blocks = 4
        rights = [piece for right in rights for piece in right]
        out_shape = [
            shape((depth, cols), F32),
            shape((1, cols), F32),
            shape((box_dev, cols), F32),
            shape((box_dev, cols), F32),
            shape((box_dev, per_gen, cols), BF),
        ]
        weight_grad, bias_grad, center_out, offset, gens_out = pl.pallas_call(
            functools.partial(weight_grad_kernel, boxes),
            grid_spec=pltpu.PrefetchScalarGridSpec(
                num_scalar_prefetch=1,
                grid=(blocks,),
                in_specs=[pl.BlockSpec((depth // blocks, left.shape[1]), lambda i, s: (i, 0))]
                + [whole(r) for r in rights],
                out_specs=[pl.BlockSpec((depth // blocks, cols), lambda i, s: (i, 0))]
                + [whole(o) for o in out_shape[1:]],
                scratch_shapes=[pltpu.VMEM((left.shape[1], cols), BF)],
            ),
            out_shape=out_shape,
            compiler_params=params(),
            cost_estimate=cost(2 * left.shape[1] * depth * cols, 6 << 20),
        )(scalars, left, *rights)
    with jax.named_scope("input_gradient"):
        gens_grad, center_grad = call(
            functools.partial(input_final_kernel, boxes),
            scalars,
            [*finals, bias_grad],
            [*[whole(r) for r in finals], pl.BlockSpec(memory_space=pl.ANY)],
            [shape((box_dev, per_gen, depth), F32), shape((box_dev, depth), F32)],
            cost(0, 2 << 20),
        )
    return (
        center_out,
        gens_out,
        offset,
        weight_grad,
        bias_grad.reshape(cols),
        gens_grad,
        center_grad,
    )


def solution(mesh):
    sizes = dict(mesh.shape)

    def run(gens, center, weight, bias, phase, gens_cot, center_cot, offset_cot):
        size = sizes["gen"]
        box_dev = gens.shape[0] // sizes["box"]
        per_gen = gens.shape[1] // size
        cols = weight.shape[1] // sizes["neur"]
        square = (
            size == sizes["neur"] == 4
            and sizes["box"] == 2
            and box_dev == 4
            and per_gen % 16 == 0
            and cols % (128 * size) == 0
            and weight.shape[0] % (1024 * size) == 0
        )
        body = functools.partial(square_body, size) if square else general_body
        return jax.shard_map(
            body,
            mesh=mesh,
            in_specs=(
                P("box", "gen", None),
                P("box", None),
                P("gen", "neur"),
                P("neur"),
                P("box", "neur"),
                P("box", "gen", "neur"),
                P("box", "neur"),
                P("box", "neur"),
            ),
            out_specs=(
                P("box", "neur"),
                P("box", "gen", "neur"),
                P("box", "neur"),
                P("gen", "neur"),
                P("neur"),
                P("box", "gen", "neur"),
                P("box", "neur"),
            ),
            check_vma=False,
        )(gens, center, weight, bias, phase, gens_cot, center_cot, offset_cot)

    return run
```

time: 106 us -> 114 us (1.075)
  the two profiles are of different devices: /device:TPU:2 before, /device:TPU:1 now
where the time goes in v2:
time: 114 us; the launch traced here: 113 us
  starting transfers between devices  62.1 us (54%)
  waiting for transfers between devices  23 us (20%)
  Pallas kernels  15.1 us (13%)
  local copies, waits for them, and re-layouts  10.5 us (9%)
  other arithmetic  1.5 us (1%)
    ppermute x18, starting transfers between devices, over_gen(): return lax.ppermute(x, 'gen', [(i, i ^ k) for i in range(size)])  28.2 us
    ppermute x7, starting transfers between devices, over_core(): return lax.ppermute(x, 'neur', [(i, i ^ 1) for i in range(size)])  18.1 us
    ppermute x18, waiting for transfers between devices, over_gen(): return lax.ppermute(x, 'gen', [(i, i ^ k) for i in range(size)])  13 us
    pallas_call x12, Pallas kernels, call(): pl.pallas_call(kernel, grid_spec=pltpu.PrefetchScalarGridSpec(num_scalar_...  10.6 us
    ppermute x4, starting transfers between devices, turned(): return lax.ppermute(x, ('gen', 'neur'), pairs)  9.91 us
    unnamed x37, local copies, waits for them, and re-layouts  6.33 us
    ppermute x2, waiting for transfers between devices, over_x(): return lax.ppermute(x, 'neur', [(i, i ^ 2) for i in range(size)])  4.64 us
    ppermute x5, starting transfers between devices, over_box(): return lax.ppermute(x, 'box', [(0, 1), (1, 0)])  4.37 us
  transfers between devices with their start and end apart: 36, of which 10 were waited for; matrix products, arithmetic and copies ran while one was open for 5% of the time, Pallas kernels for 11%

profile of v2, /device:TPU:1, one launch (start us, length us, event | category | flops | bytes accessed | tf_op | source)
XLA Modules:
  0.0 113.2 jit_solution(7116687583829246806)
XLA Ops:
  3.6 2.8 %collective-permute-start.1 = (bf16[32,1024]{1,0:T(8,128)(2,1)S(1)}, bf16[32,1024]{1,0:T(8,128)(2,1)S(1)}, u32[]{:S(2)}, u32[]{:S(2)}) collective-permute-start(bf16[32,1024]{1,0:T(8,128)(2,1)S(1)} %get-tuple-element.54), channel_id=1, source_target_pairs={{0,8},{8,0},{16,24},{24,16},{1,9},{9,1},{17,25},{25,17},{2,10},{10... | collective-permute-start | bytes 196616 | tf_op jit(solution)/shard_map/exchange_generators/ppermute | solution.py:328
  6.4 2.3 %collective-permute-start.2 = (bf16[32,1024]{1,0:T(8,128)(2,1)S(1)}, bf16[32,1024]{1,0:T(8,128)(2,1)S(1)}, u32[]{:S(2)}, u32[]{:S(2)}) collective-permute-start(bf16[32,1024]{1,0:T(8,128)(2,1)S(1)} %get-tuple-element.55), channel_id=1, source_target_pairs={{0,16},{8,24},{16,0},{24,8},{1,17},{9,25},{17,1},{25,9},{2,18},{10... | collective-permute-start | bytes 196616 | tf_op jit(solution)/shard_map/exchange_generators/ppermute | solution.py:328
  9.1 3.3 %collective-permute-start.5 = (bf16[48,1024]{1,0:T(8,128)(2,1)S(1)}, bf16[48,1024]{1,0:T(8,128)(2,1)S(1)}, u32[]{:S(2)}, u32[]{:S(2)}) collective-permute-start(bf16[48,1024]{1,0:T(8,128)(2,1)S(1)} %get-tuple-element.59), channel_id=1, source_target_pairs={{0,16},{8,24},{16,0},{24,8},{1,17},{9,25},{17,1},{25,9},{2,18},{10... | collective-permute-start | bytes 294920 | tf_op jit(solution)/shard_map/exchange_generators/ppermute | solution.py:328
  16.9 4.7 %collective-permute-done.5.refs_1_ = bf16[48,1024]{1,0:T(8,128)(2,1)S(1)} collective-permute-done((bf16[48,1024]{1,0:T(8,128)(2,1)S(1)}, bf16[48,1024]{1,0:T(8,128)(2,1)S(1)}, u32[]{:S(2)}, u32[]{:S(2)}) %collective-permute-start.5) | collective-permute-done | bytes 98336 | tf_op jit(solution)/shard_map/exchange_generators/ppermute | solution.py:328
  23.4 1.2 %collective-permute-start.8 = (bf16[288,1024]{1,0:T(8,128)(2,1)S(1)}, bf16[288,1024]{1,0:T(8,128)(2,1)S(1)}, u32[]{:S(2)}, u32[]{:S(2)}) collective-permute-start(bf16[288,1024]{1,0:T(8,128)(2,1)S(1)} %constant_dynamic-update-slice_fusion.refs_0_), channel_id=1, source_target_pairs={{0,1},{1,0},{2,3},{3,2},{4,5},{5,4},{6,7},{7,6},{8,9},{9,8},{10,11... | collective-permute-start | bytes 1769480 | tf_op jit(solution)/shard_map/share_generators/ppermute | solution.py:337
  25.2 1.4 %constant_dynamic-slice_fusion = (f32[3,2,512]{2,1,0:T(2,128)}, f32[3,2,512]{2,1,0:T(2,128)}) fusion(f32[3,4,512]{2,1,0:T(4,128)} %pad_maximum_fusion, s32[]{:T(128)S(6)} %select_n.15, s32[]{:T(128)S(6)} %select_n.14), kind=kLoop, calls=%fused_computation.9 | loop fusion | bytes 49160 | tf_op jit(solution)/shard_map/swap_cores/dynamic_slice | solution.py:377
  26.7 1.3 %reshape.24 = f32[6,512]{1,0:T(8,128)} reshape(f32[3,2,512]{2,1,0:T(2,128)} %get-tuple-element.101) | data formatting | bytes 24576 | tf_op jit(solution)/shard_map/swap_cores/reshape | solution.py:379
  28.0 1.3 %reshape.23 = f32[6,512]{1,0:T(8,128)} reshape(f32[3,2,512]{2,1,0:T(2,128)} %get-tuple-element.102) | data formatting | bytes 24576 | tf_op jit(solution)/shard_map/swap_cores/reshape | solution.py:379
  29.4 2.4 %collective-permute-start.18 = (f32[136,256]{1,0:T(8,128)}, f32[136,256]{1,0:T(8,128)S(1)}, u32[]{:S(2)}, u32[]{:S(2)}) collective-permute-start(f32[136,256]{1,0:T(8,128)} %copy-done.13), channel_id=1, source_target_pairs={{0,8},{8,0},{16,24},{24,16},{1,9},{9,1},{17,25},{25,17},{2,10},{10... | collective-permute-start | bytes 417800 | tf_op jit(solution)/shard_map/sum_products/ppermute | solution.py:328
  32.4 1.4 %collective-permute-start.20 = (f32[136,256]{1,0:T(8,128)}, f32[136,256]{1,0:T(8,128)S(1)}, u32[]{:S(2)}, u32[]{:S(2)}) collective-permute-start(f32[136,256]{1,0:T(8,128)} %copy-done.11), channel_id=1, source_target_pairs={{0,24},{8,16},{16,8},{24,0},{1,25},{9,17},{17,9},{25,1},{2,26},{10... | collective-permute-start | bytes 417800 | tf_op jit(solution)/shard_map/sum_products/ppermute | solution.py:328
  34.7 1.7 %collective-permute-start.14 = (f32[8,512]{1,0:T(8,128)S(1)}, f32[8,512]{1,0:T(8,128)S(1)}, u32[]{:S(2)}, u32[]{:S(2)}) collective-permute-start(f32[8,512]{1,0:T(8,128)S(1)} %get-tuple-element.103), channel_id=1, source_target_pairs={{0,2},{2,0},{4,6},{6,4},{1,3},{3,1},{5,7},{7,5},{8,10},{10,8},{12,... | collective-permute-start | bytes 49160 | tf_op jit(solution)/shard_map/swap_cores/ppermute | solution.py:331
  39.9 1.7 %collective-permute-start.11 = (f32[136,256]{1,0:T(8,128)}, f32[136,256]{1,0:T(8,128)S(1)}, u32[]{:S(2)}, u32[]{:S(2)}) collective-permute-start(f32[136,256]{1,0:T(8,128)} %copy-done.9), channel_id=1, source_target_pairs={{0,16},{8,24},{16,0},{24,8},{1,17},{9,25},{17,1},{25,9},{2,18},{10... | collective-permute-start | bytes 417800 | tf_op jit(solution)/shard_map/sum_products/ppermute | solution.py:328
  41.8 1.8 %collective-permute-start.12 = (f32[136,256]{1,0:T(8,128)}, f32[136,256]{1,0:T(8,128)S(1)}, u32[]{:S(2)}, u32[]{:S(2)}) collective-permute-start(f32[136,256]{1,0:T(8,128)} %copy-done.8), channel_id=1, source_target_pairs={{0,24},{8,16},{16,8},{24,0},{1,25},{9,17},{17,9},{25,1},{2,26},{10... | collective-permute-start | bytes 417800 | tf_op jit(solution)/shard_map/sum_products/ppermute | solution.py:328
  45.1 1.5 %collective-permute-done.10.refs_1_ = f32[136,256]{1,0:T(8,128)S(1)} collective-permute-done((f32[136,256]{1,0:T(8,128)}, f32[136,256]{1,0:T(8,128)S(1)}, u32[]{:S(2)}, u32[]{:S(2)}) %collective-permute-start.10) | collective-permute-done | bytes 139296 | tf_op jit(solution)/shard_map/sum_products/ppermute | solution.py:328
  46.6 3.3 %collective-permute-start.21 = (bf16[176,256]{1,0:T(8,128)(2,1)S(1)}, bf16[176,256]{1,0:T(8,128)(2,1)S(1)}, u32[]{:S(2)}, u32[]{:S(2)}) collective-permute-start(bf16[176,256]{1,0:T(8,128)(2,1)S(1)} %get-tuple-element.80), channel_id=1, source_target_pairs={{0,8},{8,0},{16,24},{24,16},{1,9},{9,1},{17,25},{25,17},{2,10},{10... | collective-permute-start | bytes 270344 | tf_op jit(solution)/shard_map/exchange_back/ppermute | solution.py:328
  50.0 8.7 %collective-permute-start.9 = (bf16[288,1024]{1,0:T(8,128)(2,1)S(1)}, bf16[288,1024]{1,0:T(8,128)(2,1)S(1)}, u32[]{:S(2)}, u32[]{:S(2)}) collective-permute-start(bf16[288,1024]{1,0:T(8,128)(2,1)S(1)} %collective-permute-done.8.refs_2_), channel_id=1, source_target_pairs={{0,2},{2,0},{4,6},{6,4},{1,3},{3,1},{5,7},{7,5},{8,10},{10,8},{12,... | collective-permute-start | bytes 1769480 | tf_op jit(solution)/shard_map/share_generators/ppermute | solution.py:331
  58.7 1.9 %collective-permute-start.23 = (bf16[176,256]{1,0:T(8,128)(2,1)S(1)}, bf16[176,256]{1,0:T(8,128)(2,1)S(1)}, u32[]{:S(2)}, u32[]{:S(2)}) collective-permute-start(bf16[176,256]{1,0:T(8,128)(2,1)S(1)} %get-tuple-element.82), channel_id=1, source_target_pairs={{0,24},{8,16},{16,8},{24,0},{1,25},{9,17},{17,9},{25,1},{2,26},{10... | collective-permute-start | bytes 270344 | tf_op jit(solution)/shard_map/exchange_back/ppermute | solution.py:328
  62.1 5.5 %collective-permute-done.22.refs_1_ = bf16[176,256]{1,0:T(8,128)(2,1)S(1)} collective-permute-done((bf16[176,256]{1,0:T(8,128)(2,1)S(1)}, bf16[176,256]{1,0:T(8,128)(2,1)S(1)}, u32[]{:S(2)}, u32[]{:S(2)}) %collective-permute-start.22) | collective-permute-done | bytes 90144 | tf_op jit(solution)/shard_map/exchange_back/ppermute | solution.py:328
  68.2 1.4 %input_gradient.7 = (bf16[72,1024]{1,0:T(8,128)(2,1)S(1)}, f32[72,1024]{1,0:T(8,128)S(1)}) custom-call(s32[3]{0:T(128)S(1)} %pad_add_fusion.s_ref, bf16[176,512]{1,0:T(8,128)(2,1)S(1)} %get-tuple-element.83.refs_1_.own_ref, bf16[176,512]{1,0:T(8,128)(2,1)S(1)} %get-tuple-element.85.oth_ref, bf16[1024,512]{1,0:T(8,128)(2,1)S(1)} %copy-done.1, ...), custom_call_target="tpu_custom_call" | custom-call | flops 268435456 | bytes 4194304 | tf_op jit(solution)/shard_map/input_gradient/pallas_call | solution.py:88
  69.6 1.3 %collective-permute-start.33 = (bf16[72,1024]{1,0:T(8,128)(2,1)S(1)}, bf16[72,1024]{1,0:T(8,128)(2,1)S(1)}, u32[]{:S(2)}, u32[]{:S(2)}) collective-permute-start(bf16[72,1024]{1,0:T(8,128)(2,1)S(1)} %get-tuple-element.96), channel_id=1, source_target_pairs={{0,4},{2,6},{4,0},{6,2},{1,5},{3,7},{5,1},{7,3},{8,12},{10,14},{12... | collective-permute-start | bytes 442376 | tf_op jit(solution)/shard_map/input_gradient/ppermute | solution.py:334
  70.9 2.3 %collective-permute-start.16 = (bf16[176,256]{1,0:T(8,128)(2,1)S(1)}, bf16[176,256]{1,0:T(8,128)(2,1)S(1)}, u32[]{:S(2)}, u32[]{:S(2)}) collective-permute-start(bf16[176,256]{1,0:T(8,128)(2,1)S(1)} %get-tuple-element.71), channel_id=1, source_target_pairs={{0,16},{8,24},{16,0},{24,8},{1,17},{9,25},{17,1},{25,9},{2,18},{10... | collective-permute-start | bytes 270344 | tf_op jit(solution)/shard_map/exchange_back/ppermute | solution.py:328
  73.2 2.0 %collective-permute-start.17 = (bf16[176,256]{1,0:T(8,128)(2,1)S(1)}, bf16[176,256]{1,0:T(8,128)(2,1)S(1)}, u32[]{:S(2)}, u32[]{:S(2)}) collective-permute-start(bf16[176,256]{1,0:T(8,128)(2,1)S(1)} %get-tuple-element.72), channel_id=1, source_target_pairs={{0,24},{8,16},{16,8},{24,0},{1,25},{9,17},{17,9},{25,1},{2,26},{10... | collective-permute-start | bytes 270344 | tf_op jit(solution)/shard_map/exchange_back/ppermute | solution.py:328
  75.2 6.5 %collective-permute-start.25 = (bf16[176,512]{1,0:T(8,128)(2,1)S(1)}, bf16[176,512]{1,0:T(8,128)(2,1)S(1)}, u32[]{:S(2)}, u32[]{:S(2)}) collective-permute-start(bf16[176,512]{1,0:T(8,128)(2,1)S(1)} %get-tuple-element.85.oth_ref), channel_id=1, source_target_pairs={{0,2},{2,0},{4,6},{6,4},{1,3},{3,1},{5,7},{7,5},{8,10},{10,8},{12,... | collective-permute-start | bytes 540680 | tf_op jit(solution)/shard_map/exchange_back/ppermute | solution.py:331
  82.4 1.4 %input_gradient.5 = (bf16[72,1024]{1,0:T(8,128)(2,1)S(1)}, f32[72,1024]{1,0:T(8,128)S(1)}) custom-call(s32[3]{0:T(128)S(1)} %pad_add_fusion.s_ref, bf16[176,512]{1,0:T(8,128)(2,1)S(1)} %get-tuple-element.73.refs_0_.own_ref, bf16[176,512]{1,0:T(8,128)(2,1)S(1)} %get-tuple-element.84.oth_ref, bf16[1024,512]{1,0:T(8,128)(2,1)S(1)} %copy-done.1, ...), custom_call_target="tpu_custom_call" | custom-call | flops 268435456 | bytes 4194304 | tf_op jit(solution)/shard_map/input_gradient/pallas_call | solution.py:88
  84.2 4.6 %collective-permute-done.30.got_ref = bf16[72,1024]{1,0:T(8,128)(2,1)S(1)} collective-permute-done((bf16[72,1024]{1,0:T(8,128)(2,1)S(1)}, bf16[72,1024]{1,0:T(8,128)(2,1)S(1)}, u32[]{:S(2)}, u32[]{:S(2)}) %collective-permute-start.30) | collective-permute-done | bytes 147488 | tf_op jit(solution)/shard_map/input_gradient/ppermute | solution.py:334
  89.1 1.3 %collective-permute-start.26 = (bf16[144,512]{1,0:T(8,128)(2,1)S(1)}, bf16[144,512]{1,0:T(8,128)(2,1)S(1)}, u32[]{:S(2)}, u32[]{:S(2)}) collective-permute-start(bf16[144,512]{1,0:T(8,128)(2,1)S(1)} %slice.12), channel_id=1, source_target_pairs={{0,1},{1,0},{2,3},{3,2},{4,5},{5,4},{6,7},{7,6},{8,9},{9,8},{10,11... | collective-permute-start | bytes 442376 | tf_op jit(solution)/shard_map/exchange_back/ppermute | solution.py:337
  90.7 1.3 %collective-permute-start.28 = (bf16[144,512]{1,0:T(8,128)(2,1)S(1)}, bf16[144,512]{1,0:T(8,128)(2,1)S(1)}, u32[]{:S(2)}, u32[]{:S(2)}) collective-permute-start(bf16[144,512]{1,0:T(8,128)(2,1)S(1)} %slice.16), channel_id=1, source_target_pairs={{0,1},{1,0},{2,3},{3,2},{4,5},{5,4},{6,7},{7,6},{8,9},{9,8},{10,11... | collective-permute-start | bytes 442376 | tf_op jit(solution)/shard_map/exchange_back/ppermute | solution.py:337
  93.2 6.2 %collective-permute-start.34 = (bf16[40,1024]{1,0:T(8,128)(2,1)S(1)}, bf16[40,1024]{1,0:T(8,128)(2,1)S(1)}, u32[]{:S(2)}, u32[]{:S(2)}) collective-permute-start(bf16[40,1024]{1,0:T(8,128)(2,1)S(1)} %get-tuple-element.97), channel_id=1, source_target_pairs={{0,0},{2,16},{4,8},{6,24},{8,2},{10,18},{12,10},{14,26},{16,4},{18... | collective-permute-start | bytes 245768 | tf_op jit(solution)/shard_map/input_gradient/ppermute | solution.py:345
  100.1 3.6 %collective-permute-start.31 = (bf16[40,1024]{1,0:T(8,128)(2,1)S(1)}, bf16[40,1024]{1,0:T(8,128)(2,1)S(1)}, u32[]{:S(2)}, u32[]{:S(2)}) collective-permute-start(bf16[40,1024]{1,0:T(8,128)(2,1)S(1)} %get-tuple-element.93), channel_id=1, source_target_pairs={{0,0},{2,16},{4,8},{6,24},{8,2},{10,18},{12,10},{14,26},{16,4},{18... | collective-permute-start | bytes 245768 | tf_op jit(solution)/shard_map/input_gradient/ppermute | solution.py:345
  103.9 3.8 %weight_gradient.1 = (f32[1024,512]{1,0:T(8,128)}, f32[1,512]{1,0:T(1,128)}, f32[4,512]{1,0:T(4,128)}, f32[4,512]{1,0:T(4,128)}, bf16[4,32,512]{2,1,0:T(8,128)(2,1)}) custom-call(s32[3]{0:T(128)S(1)} %pad_add_fusion.s_ref, bf16[1024,1152]{1,0:T(8,128)(2,1)S(1)} %share_generators.1.left_ref, bf16[176,512]{1,0:T(8,128)(2,1)S(1)} %get-tuple-element.73.refs_0_.own_ref, ...), custom_call_target="tpu_custom_call" | custom-call | flops 1207959552 | bytes 6291456 | tf_op jit(solution)/shard_map/weight_gradient/pallas_call | solution.py:487
  107.7 3.2 %collective-permute-done.31.refs_0_ = bf16[40,1024]{1,0:T(8,128)(2,1)S(1)} collective-permute-done((bf16[40,1024]{1,0:T(8,128)(2,1)S(1)}, bf16[40,1024]{1,0:T(8,128)(2,1)S(1)}, u32[]{:S(2)}, u32[]{:S(2)}) %collective-permute-start.31) | collective-permute-done | bytes 81952 | tf_op jit(solution)/shard_map/input_gradient/ppermute | solution.py:345
  111.8 1.4 %input_gradient.9 = (f32[4,32,1024]{2,1,0:T(8,128)}, f32[4,1024]{1,0:T(4,128)}) custom-call(s32[3]{0:T(128)S(1)} %pad_add_fusion.s_ref, bf16[40,1024]{1,0:T(8,128)(2,1)S(1)} %collective-permute-done.31.refs_0_, bf16[40,1024]{1,0:T(8,128)(2,1)S(1)} %collective-permute-done.32.refs_1_, bf16[40,1024]{1,0:T(8,128)(2,1)S(1)} %collective-permute-done.34.refs_2_, ...), custom_call_target="tpu_custom_call" | custom-call | bytes 2097152 | tf_op jit(solution)/shard_map/input_gradient/pallas_call | solution.py:88
  (104 shorter events, 23.6 us)
Async XLA Ops:
  0.6 13.2 %collective-permute-start = (bf16[1024,512]{1,0:T(8,128)(2,1)}, bf16[1024,512]{1,0:T(8,128)(2,1)S(1)}, u32[]{:S(2)}, u32[]{:S(2)}) collective-permute-start(bf16[1024,512]{1,0:T(8,128)(2,1)} %w_own_ref.3), channel_id=1, source_target_pairs={{0,2},{2,0},{4,6},{6,4},{1,3},{3,1},{5,7},{7,5},{8,10},{10,8},{12,... | collective-permute-start | bytes 3145736 | tf_op jit(solution)/shard_map/swap_cores/ppermute | solution.py:331
  3.6 5.5 %collective-permute-start.1 = (bf16[32,1024]{1,0:T(8,128)(2,1)S(1)}, bf16[32,1024]{1,0:T(8,128)(2,1)S(1)}, u32[]{:S(2)}, u32[]{:S(2)}) collective-permute-start(bf16[32,1024]{1,0:T(8,128)(2,1)S(1)} %get-tuple-element.54), channel_id=1, source_target_pairs={{0,8},{8,0},{16,24},{24,16},{1,9},{9,1},{17,25},{25,17},{2,10},{10... | collective-permute-start | bytes 196616 | tf_op jit(solution)/shard_map/exchange_generators/ppermute | solution.py:328
  6.4 5.9 %collective-permute-start.2 = (bf16[32,1024]{1,0:T(8,128)(2,1)S(1)}, bf16[32,1024]{1,0:T(8,128)(2,1)S(1)}, u32[]{:S(2)}, u32[]{:S(2)}) collective-permute-start(bf16[32,1024]{1,0:T(8,128)(2,1)S(1)} %get-tuple-element.55), channel_id=1, source_target_pairs={{0,16},{8,24},{16,0},{24,8},{1,17},{9,25},{17,1},{25,9},{2,18},{10... | collective-permute-start | bytes 196616 | tf_op jit(solution)/shard_map/exchange_generators/ppermute | solution.py:328
  8.7 5.1 %collective-permute-start.3 = (bf16[32,1024]{1,0:T(8,128)(2,1)S(1)}, bf16[32,1024]{1,0:T(8,128)(2,1)S(1)}, u32[]{:S(2)}, u32[]{:S(2)}) collective-permute-start(bf16[32,1024]{1,0:T(8,128)(2,1)S(1)} %get-tuple-element.56), channel_id=1, source_target_pairs={{0,24},{8,16},{16,8},{24,0},{1,25},{9,17},{17,9},{25,1},{2,26},{10... | collective-permute-start | bytes 196616 | tf_op jit(solution)/shard_map/exchange_generators/ppermute | solution.py:328
  8.7 8.1 %collective-permute-start.4 = (bf16[48,1024]{1,0:T(8,128)(2,1)S(1)}, bf16[48,1024]{1,0:T(8,128)(2,1)S(1)}, u32[]{:S(2)}, u32[]{:S(2)}) collective-permute-start(bf16[48,1024]{1,0:T(8,128)(2,1)S(1)} %get-tuple-element.58), channel_id=1, source_target_pairs={{0,8},{8,0},{16,24},{24,16},{1,9},{9,1},{17,25},{25,17},{2,10},{10... | collective-permute-start | bytes 294920 | tf_op jit(solution)/shard_map/exchange_generators/ppermute | solution.py:328
  9.1 12.5 %collective-permute-start.5 = (bf16[48,1024]{1,0:T(8,128)(2,1)S(1)}, bf16[48,1024]{1,0:T(8,128)(2,1)S(1)}, u32[]{:S(2)}, u32[]{:S(2)}) collective-permute-start(bf16[48,1024]{1,0:T(8,128)(2,1)S(1)} %get-tuple-element.59), channel_id=1, source_target_pairs={{0,16},{8,24},{16,0},{24,8},{1,17},{9,25},{17,1},{25,9},{2,18},{10... | collective-permute-start | bytes 294920 | tf_op jit(solution)/shard_map/exchange_generators/ppermute | solution.py:328
  12.3 9.3 %collective-permute-start.6 = (bf16[48,1024]{1,0:T(8,128)(2,1)S(1)}, bf16[48,1024]{1,0:T(8,128)(2,1)S(1)}, u32[]{:S(2)}, u32[]{:S(2)}) collective-permute-start(bf16[48,1024]{1,0:T(8,128)(2,1)S(1)} %get-tuple-element.60), channel_id=1, source_target_pairs={{0,24},{8,16},{16,8},{24,0},{1,25},{9,17},{17,9},{25,1},{2,26},{10... | collective-permute-start | bytes 294920 | tf_op jit(solution)/shard_map/exchange_generators/ppermute | solution.py:328
  23.4 26.6 %collective-permute-start.8 = (bf16[288,1024]{1,0:T(8,128)(2,1)S(1)}, bf16[288,1024]{1,0:T(8,128)(2,1)S(1)}, u32[]{:S(2)}, u32[]{:S(2)}) collective-permute-start(bf16[288,1024]{1,0:T(8,128)(2,1)S(1)} %constant_dynamic-update-slice_fusion.refs_0_), channel_id=1, source_target_pairs={{0,1},{1,0},{2,3},{3,2},{4,5},{5,4},{6,7},{7,6},{8,9},{9,8},{10,11... | collective-permute-start | bytes 1769480 | tf_op jit(solution)/shard_map/share_generators/ppermute | solution.py:337
  29.4 9.9 %collective-permute-start.18 = (f32[136,256]{1,0:T(8,128)}, f32[136,256]{1,0:T(8,128)S(1)}, u32[]{:S(2)}, u32[]{:S(2)}) collective-permute-start(f32[136,256]{1,0:T(8,128)} %copy-done.13), channel_id=1, source_target_pairs={{0,8},{8,0},{16,24},{24,16},{1,9},{9,1},{17,25},{25,17},{2,10},{10... | collective-permute-start | bytes 417800 | tf_op jit(solution)/shard_map/sum_products/ppermute | solution.py:328
  31.8 8.1 %collective-permute-start.19 = (f32[136,256]{1,0:T(8,128)}, f32[136,256]{1,0:T(8,128)S(1)}, u32[]{:S(2)}, u32[]{:S(2)}) collective-permute-start(f32[136,256]{1,0:T(8,128)} %copy-done.12), channel_id=1, source_target_pairs={{0,16},{8,24},{16,0},{24,8},{1,17},{9,25},{17,1},{25,9},{2,18},{10... | collective-permute-start | bytes 417800 | tf_op jit(solution)/shard_map/sum_products/ppermute | solution.py:328
  32.4 9.3 %collective-permute-start.20 = (f32[136,256]{1,0:T(8,128)}, f32[136,256]{1,0:T(8,128)S(1)}, u32[]{:S(2)}, u32[]{:S(2)}) collective-permute-start(f32[136,256]{1,0:T(8,128)} %copy-done.11), channel_id=1, source_target_pairs={{0,24},{8,16},{16,8},{24,0},{1,25},{9,17},{17,9},{25,1},{2,26},{10... | collective-permute-start | bytes 417800 | tf_op jit(solution)/shard_map/sum_products/ppermute | solution.py:328
  38.5 8.2 %collective-permute-start.10 = (f32[136,256]{1,0:T(8,128)}, f32[136,256]{1,0:T(8,128)S(1)}, u32[]{:S(2)}, u32[]{:S(2)}) collective-permute-start(f32[136,256]{1,0:T(8,128)} %copy-done.10), channel_id=1, source_target_pairs={{0,8},{8,0},{16,24},{24,16},{1,9},{9,1},{17,25},{25,17},{2,10},{10... | collective-permute-start | bytes 417800 | tf_op jit(solution)/shard_map/sum_products/ppermute | solution.py:328
  39.3 51.4 %collective-permute-start.7 = (bf16[288,1024]{1,0:T(8,128)(2,1)S(1)}, bf16[288,1024]{1,0:T(8,128)(2,1)S(1)}, u32[]{:S(2)}, u32[]{:S(2)}) collective-permute-start(bf16[288,1024]{1,0:T(8,128)(2,1)S(1)} %constant_dynamic-update-slice_fusion.refs_0_), channel_id=1, source_target_pairs={{0,2},{2,0},{4,6},{6,4},{1,3},{3,1},{5,7},{7,5},{8,10},{10,8},{12,... | collective-permute-start | bytes 1769480 | tf_op jit(solution)/shard_map/share_generators/ppermute | solution.py:331
  39.9 18.8 %collective-permute-start.11 = (f32[136,256]{1,0:T(8,128)}, f32[136,256]{1,0:T(8,128)S(1)}, u32[]{:S(2)}, u32[]{:S(2)}) collective-permute-start(f32[136,256]{1,0:T(8,128)} %copy-done.9), channel_id=1, source_target_pairs={{0,16},{8,24},{16,0},{24,8},{1,17},{9,25},{17,1},{25,9},{2,18},{10... | collective-permute-start | bytes 417800 | tf_op jit(solution)/shard_map/sum_products/ppermute | solution.py:328
  41.8 16.9 %collective-permute-start.12 = (f32[136,256]{1,0:T(8,128)}, f32[136,256]{1,0:T(8,128)S(1)}, u32[]{:S(2)}, u32[]{:S(2)}) collective-permute-start(f32[136,256]{1,0:T(8,128)} %copy-done.8), channel_id=1, source_target_pairs={{0,24},{8,16},{16,8},{24,0},{1,25},{9,17},{17,9},{25,1},{2,26},{10... | collective-permute-start | bytes 417800 | tf_op jit(solution)/shard_map/sum_products/ppermute | solution.py:328
  46.6 14.6 %collective-permute-start.21 = (bf16[176,256]{1,0:T(8,128)(2,1)S(1)}, bf16[176,256]{1,0:T(8,128)(2,1)S(1)}, u32[]{:S(2)}, u32[]{:S(2)}) collective-permute-start(bf16[176,256]{1,0:T(8,128)(2,1)S(1)} %get-tuple-element.80), channel_id=1, source_target_pairs={{0,8},{8,0},{16,24},{24,16},{1,9},{9,1},{17,25},{25,17},{2,10},{10... | collective-permute-start | bytes 270344 | tf_op jit(solution)/shard_map/exchange_back/ppermute | solution.py:328
  50.0 43.2 %collective-permute-start.9 = (bf16[288,1024]{1,0:T(8,128)(2,1)S(1)}, bf16[288,1024]{1,0:T(8,128)(2,1)S(1)}, u32[]{:S(2)}, u32[]{:S(2)}) collective-permute-start(bf16[288,1024]{1,0:T(8,128)(2,1)S(1)} %collective-permute-done.8.refs_2_), channel_id=1, source_target_pairs={{0,2},{2,0},{4,6},{6,4},{1,3},{3,1},{5,7},{7,5},{8,10},{10,8},{12,... | collective-permute-start | bytes 1769480 | tf_op jit(solution)/shard_map/share_generators/ppermute | solution.py:331
  58.7 8.9 %collective-permute-start.22 = (bf16[176,256]{1,0:T(8,128)(2,1)S(1)}, bf16[176,256]{1,0:T(8,128)(2,1)S(1)}, u32[]{:S(2)}, u32[]{:S(2)}) collective-permute-start(bf16[176,256]{1,0:T(8,128)(2,1)S(1)} %get-tuple-element.81), channel_id=1, source_target_pairs={{0,16},{8,24},{16,0},{24,8},{1,17},{9,25},{17,1},{25,9},{2,18},{10... | collective-permute-start | bytes 270344 | tf_op jit(solution)/shard_map/exchange_back/ppermute | solution.py:328
  58.7 8.9 %collective-permute-start.23 = (bf16[176,256]{1,0:T(8,128)(2,1)S(1)}, bf16[176,256]{1,0:T(8,128)(2,1)S(1)}, u32[]{:S(2)}, u32[]{:S(2)}) collective-permute-start(bf16[176,256]{1,0:T(8,128)(2,1)S(1)} %get-tuple-element.82), channel_id=1, source_target_pairs={{0,24},{8,16},{16,8},{24,0},{1,25},{9,17},{17,9},{25,1},{2,26},{10... | collective-permute-start | bytes 270344 | tf_op jit(solution)/shard_map/exchange_back/ppermute | solution.py:328
  61.3 11.9 %collective-permute-start.15 = (bf16[176,256]{1,0:T(8,128)(2,1)S(1)}, bf16[176,256]{1,0:T(8,128)(2,1)S(1)}, u32[]{:S(2)}, u32[]{:S(2)}) collective-permute-start(bf16[176,256]{1,0:T(8,128)(2,1)S(1)} %get-tuple-element.70), channel_id=1, source_target_pairs={{0,8},{8,0},{16,24},{24,16},{1,9},{9,1},{17,25},{25,17},{2,10},{10... | collective-permute-start | bytes 270344 | tf_op jit(solution)/shard_map/exchange_back/ppermute | solution.py:328
  69.6 14.2 %collective-permute-start.33 = (bf16[72,1024]{1,0:T(8,128)(2,1)S(1)}, bf16[72,1024]{1,0:T(8,128)(2,1)S(1)}, u32[]{:S(2)}, u32[]{:S(2)}) collective-permute-start(bf16[72,1024]{1,0:T(8,128)(2,1)S(1)} %get-tuple-element.96), channel_id=1, source_target_pairs={{0,4},{2,6},{4,0},{6,2},{1,5},{3,7},{5,1},{7,3},{8,12},{10,14},{12... | collective-permute-start | bytes 442376 | tf_op jit(solution)/shard_map/input_gradient/ppermute | solution.py:334
  73.2 8.5 %collective-permute-start.17 = (bf16[176,256]{1,0:T(8,128)(2,1)S(1)}, bf16[176,256]{1,0:T(8,128)(2,1)S(1)}, u32[]{:S(2)}, u32[]{:S(2)}) collective-permute-start(bf16[176,256]{1,0:T(8,128)(2,1)S(1)} %get-tuple-element.72), channel_id=1, source_target_pairs={{0,24},{8,16},{16,8},{24,0},{1,25},{9,17},{17,9},{25,1},{2,26},{10... | collective-permute-start | bytes 270344 | tf_op jit(solution)/shard_map/exchange_back/ppermute | solution.py:328
  75.2 13.9 %collective-permute-start.25 = (bf16[176,512]{1,0:T(8,128)(2,1)S(1)}, bf16[176,512]{1,0:T(8,128)(2,1)S(1)}, u32[]{:S(2)}, u32[]{:S(2)}) collective-permute-start(bf16[176,512]{1,0:T(8,128)(2,1)S(1)} %get-tuple-element.85.oth_ref), channel_id=1, source_target_pairs={{0,2},{2,0},{4,6},{6,4},{1,3},{3,1},{5,7},{7,5},{8,10},{10,8},{12,... | collective-permute-start | bytes 540680 | tf_op jit(solution)/shard_map/exchange_back/ppermute | solution.py:331
  82.3 8.0 %collective-permute-start.24 = (bf16[176,512]{1,0:T(8,128)(2,1)S(1)}, bf16[176,512]{1,0:T(8,128)(2,1)S(1)}, u32[]{:S(2)}, u32[]{:S(2)}) collective-permute-start(bf16[176,512]{1,0:T(8,128)(2,1)S(1)} %get-tuple-element.84.oth_ref), channel_id=1, source_target_pairs={{0,2},{2,0},{4,6},{6,4},{1,3},{3,1},{5,7},{7,5},{8,10},{10,8},{12,... | collective-permute-start | bytes 540680 | tf_op jit(solution)/shard_map/exchange_back/ppermute | solution.py:331
  88.8 11.2 %collective-permute-start.27 = (bf16[144,512]{1,0:T(8,128)(2,1)S(1)}, bf16[144,512]{1,0:T(8,128)(2,1)S(1)}, u32[]{:S(2)}, u32[]{:S(2)}) collective-permute-start(bf16[144,512]{1,0:T(8,128)(2,1)S(1)} %slice.13), channel_id=1, source_target_pairs={{0,1},{1,0},{2,3},{3,2},{4,5},{5,4},{6,7},{7,6},{8,9},{9,8},{10,11... | collective-permute-start | bytes 442376 | tf_op jit(solution)/shard_map/exchange_back/ppermute | solution.py:337
  89.1 11.1 %collective-permute-start.26 = (bf16[144,512]{1,0:T(8,128)(2,1)S(1)}, bf16[144,512]{1,0:T(8,128)(2,1)S(1)}, u32[]{:S(2)}, u32[]{:S(2)}) collective-permute-start(bf16[144,512]{1,0:T(8,128)(2,1)S(1)} %slice.12), channel_id=1, source_target_pairs={{0,1},{1,0},{2,3},{3,2},{4,5},{5,4},{6,7},{7,6},{8,9},{9,8},{10,11... | collective-permute-start | bytes 442376 | tf_op jit(solution)/shard_map/exchange_back/ppermute | solution.py:337
  90.4 13.4 %collective-permute-start.29 = (bf16[144,512]{1,0:T(8,128)(2,1)S(1)}, bf16[144,512]{1,0:T(8,128)(2,1)S(1)}, u32[]{:S(2)}, u32[]{:S(2)}) collective-permute-start(bf16[144,512]{1,0:T(8,128)(2,1)S(1)} %slice.17), channel_id=1, source_target_pairs={{0,1},{1,0},{2,3},{3,2},{4,5},{5,4},{6,7},{7,6},{8,9},{9,8},{10,11... | collective-permute-start | bytes 442376 | tf_op jit(solution)/shard_map/exchange_back/ppermute | solution.py:337
  90.7 13.1 %collective-permute-start.28 = (bf16[144,512]{1,0:T(8,128)(2,1)S(1)}, bf16[144,512]{1,0:T(8,128)(2,1)S(1)}, u32[]{:S(2)}, u32[]{:S(2)}) collective-permute-start(bf16[144,512]{1,0:T(8,128)(2,1)S(1)} %slice.16), channel_id=1, source_target_pairs={{0,1},{1,0},{2,3},{3,2},{4,5},{5,4},{6,7},{7,6},{8,9},{9,8},{10,11... | collective-permute-start | bytes 442376 | tf_op jit(solution)/shard_map/exchange_back/ppermute | solution.py:337
  93.2 14.5 %collective-permute-start.34 = (bf16[40,1024]{1,0:T(8,128)(2,1)S(1)}, bf16[40,1024]{1,0:T(8,128)(2,1)S(1)}, u32[]{:S(2)}, u32[]{:S(2)}) collective-permute-start(bf16[40,1024]{1,0:T(8,128)(2,1)S(1)} %get-tuple-element.97), channel_id=1, source_target_pairs={{0,0},{2,16},{4,8},{6,24},{8,2},{10,18},{12,10},{14,26},{16,4},{18... | collective-permute-start | bytes 245768 | tf_op jit(solution)/shard_map/input_gradient/ppermute | solution.py:345
  100.1 7.6 %collective-permute-start.35 = (bf16[40,1024]{1,0:T(8,128)(2,1)S(1)}, bf16[40,1024]{1,0:T(8,128)(2,1)S(1)}, u32[]{:S(2)}, u32[]{:S(2)}) collective-permute-start(bf16[40,1024]{1,0:T(8,128)(2,1)S(1)} %get-tuple-element.98), channel_id=1, source_target_pairs={{0,16},{2,0},{4,24},{6,8},{8,18},{10,2},{12,26},{14,10},{16,20},{1... | collective-permute-start | bytes 245768 | tf_op jit(solution)/shard_map/input_gradient/ppermute | solution.py:345
  100.1 10.7 %collective-permute-start.31 = (bf16[40,1024]{1,0:T(8,128)(2,1)S(1)}, bf16[40,1024]{1,0:T(8,128)(2,1)S(1)}, u32[]{:S(2)}, u32[]{:S(2)}) collective-permute-start(bf16[40,1024]{1,0:T(8,128)(2,1)S(1)} %get-tuple-element.93), channel_id=1, source_target_pairs={{0,0},{2,16},{4,8},{6,24},{8,2},{10,18},{12,10},{14,26},{16,4},{18... | collective-permute-start | bytes 245768 | tf_op jit(solution)/shard_map/input_gradient/ppermute | solution.py:345
  103.8 7.4 %collective-permute-start.32 = (bf16[40,1024]{1,0:T(8,128)(2,1)S(1)}, bf16[40,1024]{1,0:T(8,128)(2,1)S(1)}, u32[]{:S(2)}, u32[]{:S(2)}) collective-permute-start(bf16[40,1024]{1,0:T(8,128)(2,1)S(1)} %get-tuple-element.94), channel_id=1, source_target_pairs={{0,16},{2,0},{4,24},{6,8},{8,18},{10,2},{12,26},{14,10},{16,20},{1... | collective-permute-start | bytes 245768 | tf_op jit(solution)/shard_map/input_gradient/ppermute | solution.py:345
  (22 other events, 103.5 us)

commit v3 on v2

v3 whole, which is shorter than its diff:
```python
import functools

import jax
import jax.numpy as jnp
from jax import lax
from jax.experimental import pallas as pl
from jax.experimental.pallas import tpu as pltpu
from jax.sharding import PartitionSpec as P

BF = jnp.bfloat16
F32 = jnp.float32
VMEM_LIMIT = 24 * 1024 * 1024


def neuron(center_pre, radius, phase):
    upper = center_pre + radius
    lower = center_pre - radius
    ratio = jnp.clip(upper / (upper - lower + 1e-05), 0.0, 1.0)
    active = (phase == 1).astype(center_pre.dtype)
    crossing = (phase == 2).astype(center_pre.dtype)
    slope = active + crossing * ratio
    offset = crossing * (-ratio * lower * 0.5)
    return (slope, slope * center_pre + offset, offset)


def general_body(gens, center, weight, bias, phase, gens_cot, center_cot, offset_cot):
    box_dev, gen_dev, width = gens.shape
    local_cols = weight.shape[1]
    local_rows = box_dev * gen_dev
    wide = jnp.concatenate([gens.reshape(local_rows, width), center], 0)
    full_weight = lax.all_gather(weight, "gen", axis=0, tiled=True)
    product = jnp.dot(wide, full_weight, preferred_element_type=F32)
    gen_pre = product[:local_rows].reshape(box_dev, gen_dev, local_cols)
    center_pre = product[local_rows:] + bias
    part_radius = jnp.sum(jnp.abs(gen_pre), axis=1)
    cot_wide = gens_cot.astype(F32)
    radius = lax.psum(part_radius, "gen")
    slope, center_out, offset = neuron(center_pre, radius, phase)
    gens_out = (slope[:, None, :] * gen_pre).astype(BF)
    intersection = lax.psum(jnp.sum(cot_wide * gen_pre, axis=1), "gen")
    unused, pull = jax.vjp(lambda a, b: neuron(a, b, phase), center_pre, radius)
    g_center, g_radius = pull((intersection, center_cot, offset_cot))
    gen_back = (slope[:, None, :] * cot_wide + jnp.sign(gen_pre) * g_radius[:, None, :]).astype(BF)
    center_back = g_center.astype(BF)
    back = jnp.concatenate([gen_back.reshape(local_rows, local_cols), center_back], 0)
    first_gen = (lax.axis_index("gen") == 0).astype(BF)
    back_owned = jnp.concatenate(
        [gen_back.reshape(local_rows, local_cols), center_back * first_gen], 0
    )
    shares = lax.psum_scatter(
        lax.dot_general(wide, back_owned, (((0,), (0,)), ((), ())), preferred_element_type=F32),
        ("gen", "box"),
        scatter_dimension=0,
        tiled=True,
    )
    weight_grad = lax.all_gather(shares, "box", axis=0, tiled=True)
    bias_grad = lax.psum(jnp.sum(g_center, axis=0), "box")
    partial_back = lax.dot_general(
        back, full_weight, (((1,), (1,)), ((), ())), preferred_element_type=F32
    )
    summed = lax.psum_scatter(partial_back, "neur", scatter_dimension=1, tiled=True)
    gens_grad = summed[:local_rows].reshape(box_dev, gen_dev, summed.shape[1])
    center_grad = summed[local_rows:]
    return (center_out, gens_out, offset, weight_grad, bias_grad, gens_grad, center_grad)


CENTER_ROWS = 16
HALVES = 1
ORDER = (0, 2, 3, 1)


def params():
    return pltpu.CompilerParams(vmem_limit_bytes=VMEM_LIMIT)


def shape(dims, dtype):
    return jax.ShapeDtypeStruct(dims, dtype)


def whole(x):
    return pl.BlockSpec(x.shape, lambda i, s, r=len(x.shape): (0,) * r)


def call(kernel, scalars, args, specs, outs, scratch=(), after=(), cost=(0, 1 << 20)):
    skip = len(after)

    def body(s_ref, *refs):
        kernel(s_ref, *refs[skip:])

    return pl.pallas_call(
        body,
        grid_spec=pltpu.PrefetchScalarGridSpec(
            num_scalar_prefetch=1,
            grid=(1,),
            in_specs=[pl.BlockSpec(memory_space=pl.ANY)] * skip + specs,
            out_specs=[whole(o) for o in outs],
            scratch_shapes=list(scratch),
        ),
        out_shape=outs,
        compiler_params=params(),
        cost_estimate=pl.CostEstimate(flops=cost[0], bytes_accessed=cost[1], transcendentals=0),
    )(scalars, *after, *args)


def rows_at(index, size):
    return pl.ds(pl.multiple_of(index * size, size), size)


def fold_kernel(size, s_ref, gens_ref, cot_ref, *refs):
    g, c = s_ref[0], s_ref[1]
    outs, cot, sems = refs[:size], refs[-2], refs[-1]
    core_boxes, per_gen = gens_ref.shape[0] // 2, gens_ref.shape[1]
    depth = outs[0].shape[1]
    copies = [pltpu.make_async_copy(cot_ref, cot, sems.at[0])]
    for k, out in zip(ORDER, outs):
        for b in range(core_boxes):
            source = gens_ref.at[c * core_boxes + b, :, rows_at(g ^ k, depth)]
            target = out.at[pl.ds(b * per_gen, per_gen), :]
            copies.append(pltpu.make_async_copy(source, target, sems.at[len(copies)]))
    for copy in copies:
        copy.start()
    for copy in copies:
        copy.wait()
    rows, lanes = core_boxes * per_gen, cot.shape[2] // size
    for k, out in zip(ORDER, outs):
        value = cot[:, :, rows_at(g ^ k, lanes)].reshape(-1, lanes)
        per = out.shape[0] - rows
        for i in range(value.shape[0] // per):
            out[rows:, i * lanes : (i + 1) * lanes] = value[i * per : (i + 1) * per]


def copy_kernel(s_ref, in_ref, out_ref):
    out_ref[...] = in_ref[...]


def forward_kernel(size, s_ref, center_ref, own_ref, oth_ref, *refs):
    g, c = s_ref[0], s_ref[1]
    recv, (a_ref, keep_ref, send_ref), products = refs[:size], refs[size : size + 3], refs[size + 3 :]
    work, depth = a_ref.shape[0] // HALVES, a_ref.shape[1]
    group = (work - CENTER_ROWS) // size
    mid = center_ref[...].astype(F32)
    core_boxes = mid.shape[0] // 2
    boxes = core_boxes // HALVES
    mid = jnp.where(c == 0, mid[:core_boxes], mid[core_boxes:])
    pad = jnp.zeros((CENTER_ROWS - boxes, depth), F32)
    lanes = products[0].shape[1] // 2
    for h in range(HALVES):
        for k, msg in zip(ORDER, recv):
            at = pl.ds(pl.multiple_of(h * work + (g ^ k) * group, CENTER_ROWS), group)
            a_ref[at, :] = msg[h * group : (h + 1) * group, :]
        tail = jnp.concatenate([mid[h * boxes : (h + 1) * boxes], pad], 0).astype(BF)
        a_ref[(h + 1) * work - CENTER_ROWS : (h + 1) * work, :] = tail
    a = a_ref[...]
    for i, k in enumerate(ORDER):
        at = rows_at(g ^ k, lanes)
        w = jnp.concatenate([own_ref[:, at], oth_ref[:, at]], 1)
        product = jnp.dot(a, w, preferred_element_type=F32)
        for h in range(HALVES):
            out = products[h * size + i]
            out[...] = product[h * work : h * work + out.shape[0]]
    rows = HALVES * group
    for k, msg in zip(ORDER, recv):
        cot = [msg[rows:, i * lanes : (i + 1) * lanes] for i in range(depth // lanes)]
        cot = jnp.concatenate(cot, 0)
        low, high = cot[:rows], cot[rows:]
        for ref, value in (
            (keep_ref, jnp.where(c == 0, low, high)),
            (send_ref, jnp.where(c == 0, high, low)),
        ):
            for h in range(HALVES):
                at = pl.ds(pl.multiple_of(h * size * group + (g ^ k) * group, group), group)
                ref[at, :] = value[h * group : (h + 1) * group]


def relax_kernel(size, boxes, part, s_ref, *refs):
    g = s_ref[0]
    sums, (keep_ref, got_ref, own_ref, oth_ref), outs = refs[:size], refs[size : size + 4], refs[size + 4 :]
    back_ref, go_ref, msgs, out_scratch = outs[0], outs[1], outs[2:-1], outs[-1]
    pre = sums[0][...]
    for p in sums[1:]:
        pre = pre + p[...]
    group = go_ref.shape[0]
    rows, per = size * group, group // boxes
    cot = jnp.concatenate([keep_ref[...], got_ref[...]], 1).astype(F32)
    small = jnp.concatenate([own_ref[...], oth_ref[...]], 1)
    step = HALVES * boxes
    phase, center_cot, offset_cot = (
        small[i * step + part * boxes : i * step + (part + 1) * boxes] for i in range(3)
    )
    bias = small[3 * step : 3 * step + 1]
    where = [[q * group + b * per for q in range(size)] for b in range(boxes)]
    radius, cross = [], []
    for b in range(boxes):
        radius.append(sum(jnp.sum(jnp.abs(pre[r : r + per]), 0, keepdims=True) for r in where[b]))
        cross.append(sum(jnp.sum(cot[r : r + per] * pre[r : r + per], 0, keepdims=True) for r in where[b]))
    radius, cross = jnp.concatenate(radius, 0), jnp.concatenate(cross, 0)
    center_pre = pre[rows : rows + boxes] + bias
    (slope, center_out, offset), pull = jax.vjp(lambda a, b: neuron(a, b, phase), center_pre, radius)
    g_center, g_radius = pull((cross, center_cot, offset_cot))
    for b in range(boxes):
        sl, gr = slope[b : b + 1], g_radius[b : b + 1]
        for r in where[b]:
            x = pre[r : r + per]
            sign = jnp.where(x > 0, gr, jnp.where(x < 0, -gr, 0.0))
            back_ref[r : r + per, :] = (sl * cot[r : r + per] + sign).astype(BF)
            out_scratch[r : r + per, :] = (sl * x).astype(BF)
    tail = []
    for value in (g_center, center_out, offset):
        high = value.astype(BF).astype(F32)
        tail += [high, value - high]
    tail.append(jnp.zeros((CENTER_ROWS - 6 * boxes, value.shape[1]), F32))
    back_ref[rows:, :] = jnp.concatenate(tail, 0).astype(BF)
    go_ref[...] = out_scratch[rows_at(g, group), :]
    for k, msg in zip(ORDER[1:], msgs):
        msg[: rows + CENTER_ROWS, :] = back_ref[...]
        msg[rows + CENTER_ROWS :, :] = out_scratch[rows_at(g ^ k, group), :]


def spread_kernel(s_ref, back_ref, go_ref, *refs):
    g = s_ref[0]
    msgs, (full_ref, oth_ref, out_ref) = refs[:-3], refs[-3:]
    rows, lanes = back_ref.shape[0], back_ref.shape[1] // 2
    cols = oth_ref.shape[1]
    for i, k in enumerate(ORDER):
        at = rows_at(g ^ k, lanes)
        right = pl.ds(pl.multiple_of(cols + (g ^ k) * lanes, lanes), lanes)
        back, out = (back_ref, go_ref[...]) if i == 0 else (msgs[i - 1], msgs[i - 1][rows:, :])
        full_ref[:, at] = back[:rows, :lanes]
        full_ref[:, right] = back[:rows, lanes:]
        oth_ref[:rows, at] = back[:rows, lanes:]
        oth_ref[rows:, at] = out[:, lanes:]
        out_ref[:, at] = out[:, :lanes]


def input_grad_kernel(size, s_ref, full_ref, w_own_ref, w_oth_ref, *refs):
    c, x = s_ref[1], s_ref[2] >> 1
    outs, res = refs[:-1], refs[-1]
    rows, cols = res.shape[0], w_own_ref.shape[1]
    over = (((1,), (1,)), ((), ()))
    res[...] = lax.dot_general(
        full_ref[:, :cols], w_own_ref[...], over, preferred_element_type=F32
    ) + lax.dot_general(full_ref[:, cols:], w_oth_ref[...], over, preferred_element_type=F32)
    group = (rows - CENTER_ROWS) // size
    tail = res[size * group : size * group + 8, :]
    for i, ref in enumerate(outs):
        at = (1 - x if i < 2 else x) + 2 * (c ^ (i % 2))
        ref[...] = jnp.concatenate([res[rows_at(at, group), :], tail], 0).astype(ref.dtype)


def input_pair_kernel(s_ref, keep_ref, far_ref, out_ref):
    out_ref[...] = (keep_ref[...] + far_ref[...].astype(F32)).astype(BF)


def input_final_kernel(boxes, s_ref, *refs):
    msgs, (grad_ref, center_ref) = refs[:-2], refs[-2:]
    first = s_ref[0] >> 1
    per = grad_ref.shape[1]
    group = boxes * per
    rows = [[], []]
    for h in range(HALVES):
        for k in range(2):
            value = msgs[k][h * (group + 8) : (h + 1) * (group + 8), :].astype(F32)
            at = (first ^ k) * (HALVES * boxes) + h * boxes
            grad_ref[pl.ds(at, boxes)] = value[:group].reshape(boxes, per, -1)
            rows[k].append(value[group : group + boxes])
    near, far = (jnp.concatenate(r, 0) for r in rows)
    center_ref[...] = jnp.where(
        first == 0, jnp.concatenate([near, far], 0), jnp.concatenate([far, near], 0)
    )


def stack_kernel(s_ref, *refs):
    lefts, out = refs[:-1], refs[-1]
    rows = lefts[0].shape[0] // HALVES
    gens = rows - CENTER_ROWS
    tails = []
    for i in range(len(lefts) * HALVES):
        ref, h = lefts[i // HALVES], i % HALVES
        out[:, i * gens : (i + 1) * gens] = ref[h * rows : h * rows + gens, :].T
        tails.append(ref[h * rows + gens : (h + 1) * rows, :])
    width = out.shape[1] - len(lefts) * HALVES * gens
    pad = jnp.zeros((width - len(tails) * CENTER_ROWS, out.shape[0]), BF)
    out[:, len(tails) * gens :] = jnp.concatenate(tails + [pad], 0).T


def weight_grad_kernel(boxes, s_ref, after_ref, left_ref, *refs):
    rights, keeps, refs = refs[: 4 * HALVES], refs[4 * HALVES : 5 * HALVES], refs[5 * HALVES :]
    weight_ref, bias_ref, center_ref, offset_ref, gens_ref, done_ref, stack = refs
    per = gens_ref.shape[1]
    cols = weight_ref.shape[1]
    gens = rights[-1].shape[0] - CENTER_ROWS

    @pl.when(pl.program_id(0) == 0)
    def _():
        c = s_ref[1]
        done_ref[...] = jnp.zeros(done_ref.shape, F32)
        tails = []
        for i, right in enumerate(rights):
            stack[i * gens : (i + 1) * gens, :] = right[:gens, :cols]
            tail = right[gens : gens + CENTER_ROWS, :cols]
            at = len(rights) * gens + i * CENTER_ROWS
            stack[at : at + CENTER_ROWS, :] = tail
            tails.append(tail.astype(F32))
        used = len(rights) * (gens + CENTER_ROWS)
        if used < stack.shape[0]:
            stack[used:, :] = jnp.zeros((stack.shape[0] - used, cols), BF)
        bias_ref[...] = sum(jnp.sum(t[: 2 * boxes], 0, keepdims=True) for t in tails)
        for at, ref in ((2, center_ref), (4, offset_ref)):
            both = [
                t[at * boxes : (at + 1) * boxes] + t[(at + 1) * boxes : (at + 2) * boxes]
                for t in tails[: 2 * HALVES]
            ]
            mine, other = (jnp.concatenate(both[i * HALVES : (i + 1) * HALVES], 0) for i in range(2))
            ref[...] = jnp.where(
                c == 0, jnp.concatenate([mine, other], 0), jnp.concatenate([other, mine], 0)
            )
        for h in range(HALVES):
            for at, out in ((c, keeps[h][...]), (1 - c, rights[HALVES + h][gens + CENTER_ROWS :, :])):
                at = at * (HALVES * boxes) + h * boxes
                gens_ref[pl.ds(at, boxes)] = out.reshape(boxes, per, -1)

    weight_ref[...] = jnp.dot(left_ref[...], stack[...], preferred_element_type=F32)


def square_body(size, gens, center, weight, bias, phase, gens_cot, center_cot, offset_cot):
    box_dev, per_gen, width = gens.shape
    depth, cols = weight.shape
    core_boxes = box_dev // 2
    boxes = core_boxes // HALVES
    group = boxes * per_gen
    rows = size * group
    work = rows + CENTER_ROWS
    lanes = cols // size
    g, n = lax.axis_index("gen"), lax.axis_index("neur")
    c = n % 2
    scalars = jnp.stack([g, c, n, lax.axis_index("box")]).astype(jnp.int32)
    halves = range(HALVES)

    def over_gen(pieces):
        return [pieces[0]] + [
            lax.ppermute(piece, "gen", [(i, i ^ k) for i in range(size)])
            for piece, k in zip(pieces[1:], ORDER[1:])
        ]

    def over_core(x):
        return lax.ppermute(x, "neur", [(i, i ^ 1) for i in range(size)])

    def over_x(x):
        return lax.ppermute(x, "neur", [(i, i ^ 2) for i in range(size)])

    def over_box(x):
        return lax.ppermute(x, "box", [(0, 1), (1, 0)])

    def turned(x, k):
        pairs = [
            (i * size + j, ((j >> 1) + 2 * ((j & 1) ^ k)) * size + i)
            for i in range(size)
            for j in range(size)
        ]
        return lax.ppermute(x, ("gen", "neur"), pairs)

    anywhere = pl.BlockSpec(memory_space=pl.ANY)
    with jax.named_scope("exchange_generators"):
        cot_rows = box_dev * per_gen * lanes // depth
        msgs = call(
            functools.partial(fold_kernel, size),
            scalars,
            [gens, gens_cot],
            [anywhere] * 2,
            [shape((core_boxes * per_gen + cot_rows, depth), BF)] * size,
            [pltpu.VMEM(gens_cot.shape, BF), pltpu.SemaphoreType.DMA((size * core_boxes + 1,))],
            cost=(0, 32 << 20),
        )
        recv = over_gen(msgs)
    with jax.named_scope("swap_cores"):
        w_other = over_core(weight)
        (w_back,) = call(
            copy_kernel, scalars, [w_other], [whole(w_other)], [shape(weight.shape, BF)], after=msgs[:1]
        )
        w_own = over_core(w_back)
        center = over_core(center)
        stacked = jnp.stack([phase.astype(F32), center_cot, offset_cot])

        def small(core):
            part = lax.dynamic_slice_in_dim(stacked, core * core_boxes, core_boxes, 1)
            pad = jnp.zeros((8 - 3 * core_boxes - 1, cols), F32)
            return jnp.concatenate([part.reshape(3 * core_boxes, cols), bias[None], pad], 0)

        small_own = small(c)
        small_oth = over_core(small(1 - c))
    with jax.named_scope("forward"):
        a_own, cot_keep, cot_send, *products = call(
            functools.partial(forward_kernel, size),
            scalars,
            [center, w_own, w_other, *recv],
            [
                pl.BlockSpec((box_dev, depth), lambda i, s: (0, s[0])),
                whole(w_own),
                whole(w_other),
                *[whole(r) for r in recv],
            ],
            [shape((HALVES * work, depth), BF)]
            + [shape((HALVES * rows, lanes), BF)] * 2
            + [shape((rows + 8, 2 * lanes), F32)] * (HALVES * size),
            cost=(2 * HALVES * rows * depth * 2 * cols, 4 << 20),
        )
    with jax.named_scope("sum_products"):
        sums = []
        for h in halves:
            sums.append(over_gen(products[h * size : (h + 1) * size]))
        cot_got = over_core(cot_send)
    with jax.named_scope("share_generators"):
        a_box = over_box(a_own)
        pieces = [a_own, over_core(a_own), a_box, over_core(a_box)]
        (left,) = call(
            stack_kernel,
            scalars,
            pieces,
            [whole(v) for v in pieces],
            [shape((depth, 4 * HALVES * rows + 128), BF)],
        )
    keeps, sends = [], []
    small_spec = pl.BlockSpec((8, lanes), lambda i, s: (0, s[0]))
    for h in halves:
        cot_part = pl.BlockSpec((rows, lanes), lambda i, s, h=h: (h, 0))
        with jax.named_scope("relax"):
            back, go, *msgs = call(
                functools.partial(relax_kernel, size, boxes, h),
                scalars,
                [*sums[h], cot_keep, cot_got, small_own, small_oth],
                [*[whole(p) for p in sums[h]], cot_part, cot_part, small_spec, small_spec],
                [
                    shape((work, 2 * lanes), BF),
                    shape((group, 2 * lanes), BF),
                    *[shape((work + group, 2 * lanes), BF)] * (size - 1),
                ],
                [pltpu.VMEM((rows, 2 * lanes), BF)],
            )
        with jax.named_scope("exchange_back"):
            got = over_gen([None, *msgs])[1:]
            full, oth, out_own = call(
                spread_kernel,
                scalars,
                [back, go, *got],
                [whole(back), whole(go), *[whole(r) for r in got]],
                [
                    shape((work, 2 * cols), BF),
                    shape((work + group, cols), BF),
                    shape((group, cols), BF),
                ],
                after=sends[-1][:1] if h else [],
            )
            full_box = over_box(full)
            core_part = over_core(oth)
            keeps.append(out_own)
        with jax.named_scope("input_gradient"):
            both = group + 8
            sends.append(
                call(
                    functools.partial(input_grad_kernel, size),
                    scalars,
                    [full, w_own, w_other],
                    [whole(full), whole(w_own), whole(w_other)],
                    [shape((both, depth), BF)] * 2 + [shape((both, depth), F32)] * 2,
                    [pltpu.VMEM((work, depth), F32)],
                    cost=(2 * rows * depth * 2 * cols, 4 << 20),
                )
            )
    with jax.named_scope("input_gradient"):
        (send_0, send_1, *keeps_f32), = sends
        fars = [over_x(send_0), over_x(send_1)]
        pairs = []
        for keep, far in zip(keeps_f32, fars):
            pairs += call(
                input_pair_kernel,
                scalars,
                [keep, far],
                [whole(keep), whole(far)],
                [shape((group + 8, depth), BF)],
                after=pairs[-1:],
            )
        finals = [turned(m, k) for k, m in enumerate(pairs)]
        (box_oth,) = call(
            copy_kernel,
            scalars,
            [full_box],
            [pl.BlockSpec((work, cols), lambda i, s: (0, 1))],
            [shape((work, cols), BF)],
            after=pairs[-1:],
        )
        rights = [full, core_part, full_box, over_core(box_oth)]
    with jax.named_scope("weight_gradient"):
        blocks = 4
        out_shape = [
            shape((depth, cols), F32),
            shape((1, cols), F32),
            shape((box_dev, cols), F32),
            shape((box_dev, cols), F32),
            shape((box_dev, per_gen, cols), BF),
            shape((8, 128), F32),
        ]
        weight_grad, bias_grad, center_out, offset, gens_out, done = pl.pallas_call(
            functools.partial(weight_grad_kernel, boxes),
            grid_spec=pltpu.PrefetchScalarGridSpec(
                num_scalar_prefetch=1,
                grid=(blocks,),
                in_specs=[anywhere, pl.BlockSpec((depth // blocks, left.shape[1]), lambda i, s: (i, 0))]
                + [whole(r) for r in rights + keeps],
                out_specs=[pl.BlockSpec((depth // blocks, cols), lambda i, s: (i, 0))]
                + [whole(o) for o in out_shape[1:]],
                scratch_shapes=[pltpu.VMEM((left.shape[1], cols), BF)],
            ),
            out_shape=out_shape,
            compiler_params=params(),
            cost_estimate=pl.CostEstimate(
                flops=2 * left.shape[1] * depth * cols, bytes_accessed=6 << 20, transcendentals=0
            ),
        )(scalars, pairs[-1], left, *rights, *keeps)
    with jax.named_scope("input_gradient"):
        gens_grad, center_grad = call(
            functools.partial(input_final_kernel, boxes),
            scalars,
            finals,
            [whole(r) for r in finals],
            [shape((box_dev, per_gen, depth), F32), shape((box_dev, depth), F32)],
            after=[done],
        )
    return (
        center_out,
        gens_out,
        offset,
        weight_grad,
        bias_grad.reshape(cols),
        gens_grad,
        center_grad,
    )


def solution(mesh):
    sizes = dict(mesh.shape)

    def run(gens, center, weight, bias, phase, gens_cot, center_cot, offset_cot):
        size = sizes["gen"]
        box_dev = gens.shape[0] // sizes["box"]
        per_gen = gens.shape[1] // size
        cols = weight.shape[1] // sizes["neur"]
        square = (
            size == sizes["neur"] == 4
            and sizes["box"] == 2
            and box_dev == 4
            and per_gen % 16 == 0
            and cols % (128 * size) == 0
            and weight.shape[0] % (1024 * size) == 0
        )
        body = functools.partial(square_body, size) if square else general_body
        return jax.shard_map(
            body,
            mesh=mesh,
            in_specs=(
                P("box", "gen", None),
                P("box", None),
                P("gen", "neur"),
                P("neur"),
                P("box", "neur"),
                P("box", "gen", "neur"),
                P("box", "neur"),
                P("box", "neur"),
            ),
            out_specs=(
                P("box", "neur"),
                P("box", "gen", "neur"),
                P("box", "neur"),
                P("gen", "neur"),
                P("neur"),
                P("box", "gen", "neur"),
                P("box", "neur"),
            ),
            check_vma=False,
        )(gens, center, weight, bias, phase, gens_cot, center_cot, offset_cot)

    return run
```

time: 114 us -> 98.6 us (0.86)
  starting transfers between devices: 62.1 us -> 43.7 us
  waiting for transfers between devices: 23 us -> 33.7 us
  local copies, waits for them, and re-layouts: 10.5 us -> 3.56 us
    ppermute x18 -> x9, waiting for transfers between devices: 13 us -> 28.1 us  [over_gen(): lax.ppermute(piece, 'gen', [(i, i ^ k) for i in range(size)])]
    ppermute x18 -> x9, starting transfers between devices: 28.2 us -> 19.8 us  [over_gen(): lax.ppermute(piece, 'gen', [(i, i ^ k) for i in range(size)])]
    ppermute x7 -> x9, starting transfers between devices: 18.1 us -> 10.7 us  [over_core(): return lax.ppermute(x, 'neur', [(i, i ^ 1) for i in range(size)])]
    unnamed x37 -> x10, local copies, waits for them, and re-layouts: 6.33 us -> 2.14 us
    ppermute x4 -> x2, waiting for transfers between devices: 3.5 us -> 0.1 us  [turned(): return lax.ppermute(x, ('gen', 'neur'), pairs)]
    reshape x2, local copies, waits for them, and re-layouts: 2.65 us -> 0.73 us  [small(): part.reshape(3 * core_boxes, cols)]
    ppermute x5 -> x2, starting transfers between devices: 4.37 us -> 2.54 us  [over_box(): return lax.ppermute(x, 'box', [(0, 1), (1, 0)])]
    ppermute x4 -> x2, starting transfers between devices: 9.91 us -> 9.18 us  [turned(): return lax.ppermute(x, ('gen', 'neur'), pairs)]
  transfers between devices with their start and end apart: 36 -> 24, of which waited for: 10 -> 10; matrix products, arithmetic and copies ran while one was open for 5% -> 2% of each run, Pallas kernels for 11% -> 12%
where the time goes in v3:
time: 98.6 us; the launch traced here: 98.3 us
  starting transfers between devices  43.7 us (44%)
  waiting for transfers between devices  33.7 us (34%)
  Pallas kernels  15.7 us (16%)
  local copies, waits for them, and re-layouts  3.56 us (4%)
    ppermute x9, waiting for transfers between devices, over_gen(): lax.ppermute(piece, 'gen', [(i, i ^ k) for i in range(size)])  28.1 us
    ppermute x9, starting transfers between devices, over_gen(): lax.ppermute(piece, 'gen', [(i, i ^ k) for i in range(size)])  19.8 us
    pallas_call x11, Pallas kernels, call(): pl.pallas_call(body, grid_spec=pltpu.PrefetchScalarGridSpec(num_scalar_pr...  11.9 us
    ppermute x9, starting transfers between devices, over_core(): return lax.ppermute(x, 'neur', [(i, i ^ 1) for i in range(size)])  10.7 us
    ppermute x2, starting transfers between devices, turned(): return lax.ppermute(x, ('gen', 'neur'), pairs)  9.18 us
    pallas_call x1, Pallas kernels, square_body(): pl.pallas_call(functools.partial(weight_grad_kernel, boxes), grid_spec=pl...  3.79 us
    ppermute x2, waiting for transfers between devices, over_x(): return lax.ppermute(x, 'neur', [(i, i ^ 2) for i in range(size)])  3.7 us
    ppermute x2, starting transfers between devices, over_box(): return lax.ppermute(x, 'box', [(0, 1), (1, 0)])  2.54 us
  transfers between devices with their start and end apart: 24, of which 10 were waited for; matrix products, arithmetic and copies ran while one was open for 2% of the time, Pallas kernels for 12%

profile of v3, /device:TPU:1, one launch (start us, length us, event | category | flops | bytes accessed | tf_op | source)
XLA Modules:
  0.0 98.3 jit_solution(5933835905966939568)
XLA Ops:
  0.9 1.2 %copy-done = bf16[4,32,4096]{2,1,0:T(8,128)(2,1)S(1)} copy-done((bf16[4,32,4096]{2,1,0:T(8,128)(2,1)S(1)}, bf16[4,32,4096]{2,1,0:T(8,128)(2,1)}, u32[]{:S(2)}) %copy-start) | copy-done | bytes 1048600
  2.1 0.9 copy-done.1
  3.0 1.8 %exchange_generators.1 = (bf16[80,1024]{1,0:T(8,128)(2,1)S(1)}, bf16[80,1024]{1,0:T(8,128)(2,1)}, bf16[80,1024]{1,0:T(8,128)(2,1)}, bf16[80,1024]{1,0:T(8,128)(2,1)}) custom-call(s32[4]{0:T(128)S(1)} %pad_add_fusion.s_ref, bf16[4,32,4096]{2,1,0:T(8,128)(2,1)S(1)} %copy-done, bf16[4,32,512]{2,1,0:T(8,128)(2,1)S(1)} %copy-done.1), custom_call_target="tpu_custom_call" | custom-call | bytes 33554432 | tf_op jit(solution)/shard_map/exchange_generators/pallas_call | solution.py:90
  5.9 3.4 %collective-permute-start.3 = (bf16[80,1024]{1,0:T(8,128)(2,1)}, bf16[80,1024]{1,0:T(8,128)(2,1)S(1)}, u32[]{:S(2)}, u32[]{:S(2)}) collective-permute-start(bf16[80,1024]{1,0:T(8,128)(2,1)} %get-tuple-element.39), channel_id=1, source_target_pairs={{0,16},{8,24},{16,0},{24,8},{1,17},{9,25},{17,1},{25,9},{2,18},{10... | collective-permute-start | bytes 491528 | tf_op jit(solution)/shard_map/exchange_generators/ppermute | solution.py:341
  9.3 1.1 %collective-permute-start.4 = (bf16[80,1024]{1,0:T(8,128)(2,1)}, bf16[80,1024]{1,0:T(8,128)(2,1)}, u32[]{:S(2)}, u32[]{:S(2)}) collective-permute-start(bf16[80,1024]{1,0:T(8,128)(2,1)} %get-tuple-element.40), channel_id=1, source_target_pairs={{0,24},{8,16},{16,8},{24,0},{1,25},{9,17},{17,9},{25,1},{2,26},{10... | collective-permute-start | bytes 491528 | tf_op jit(solution)/shard_map/exchange_generators/ppermute | solution.py:341
  10.6 1.0 %collective-permute-start = (bf16[4,4096]{1,0:T(4,128)(2,1)}, bf16[4,4096]{1,0:T(4,128)(2,1)S(1)}, u32[]{:S(2)}, u32[]{:S(2)}) collective-permute-start(bf16[4,4096]{1,0:T(4,128)(2,1)} %param.9), channel_id=1, source_target_pairs={{0,2},{2,0},{4,6},{6,4},{1,3},{3,1},{5,7},{7,5},{8,10},{10,8},{12,... | collective-permute-start | bytes 98312 | tf_op jit(solution)/shard_map/swap_cores/ppermute | solution.py:346
  13.1 7.7 %collective-permute-done.3.refs_4_ = bf16[80,1024]{1,0:T(8,128)(2,1)S(1)} collective-permute-done((bf16[80,1024]{1,0:T(8,128)(2,1)}, bf16[80,1024]{1,0:T(8,128)(2,1)S(1)}, u32[]{:S(2)}, u32[]{:S(2)}) %collective-permute-start.3) | collective-permute-done | bytes 163872 | tf_op jit(solution)/shard_map/exchange_generators/ppermute | solution.py:341
  20.8 2.4 %forward.1 = (bf16[272,1024]{1,0:T(8,128)(2,1)S(1)}, bf16[256,128]{1,0:T(8,128)(2,1)S(1)}, bf16[256,128]{1,0:T(8,128)(2,1)S(1)}, f32[264,256]{1,0:T(8,128)S(1)},...) custom-call(s32[4]{0:T(128)S(1)} %pad_add_fusion.s_ref, ...), custom_call_target="tpu_custom_call" | custom-call | flops 536870912 | bytes 4194304 | tf_op jit(solution)/shard_map/forward/pallas_call | solution.py:90
  23.1 6.5 %collective-permute-start.6 = (f32[264,256]{1,0:T(8,128)S(1)}, f32[264,256]{1,0:T(8,128)S(1)}, u32[]{:S(2)}, u32[]{:S(2)}) collective-permute-start(f32[264,256]{1,0:T(8,128)S(1)} %get-tuple-element.43), channel_id=1, source_target_pairs={{0,16},{8,24},{16,0},{24,8},{1,17},{9,25},{17,1},{25,9},{2,18},{10... | collective-permute-start | bytes 811016 | tf_op jit(solution)/shard_map/sum_products/ppermute | solution.py:341
  30.0 1.2 %collective-permute-start.17 = (bf16[272,1024]{1,0:T(8,128)(2,1)S(1)}, bf16[272,1024]{1,0:T(8,128)(2,1)S(1)}, u32[]{:S(2)}, u32[]{:S(2)}) collective-permute-start(bf16[272,1024]{1,0:T(8,128)(2,1)S(1)} %get-tuple-element.58.refs_0_), channel_id=1, source_target_pairs={{0,1},{1,0},{2,3},{3,2},{4,5},{5,4},{6,7},{7,6},{8,9},{9,8},{10,11... | collective-permute-start | bytes 1671176 | tf_op jit(solution)/shard_map/share_generators/ppermute | solution.py:352
  31.2 0.8 fusion.1
  32.0 1.3 %collective-permute-start.10 = (f32[8,512]{1,0:T(8,128)S(1)}, f32[8,512]{1,0:T(8,128)S(1)}, u32[]{:S(2)}, u32[]{:S(2)}) collective-permute-start(f32[8,512]{1,0:T(8,128)S(1)} %get-tuple-element.71), channel_id=1, source_target_pairs={{0,2},{2,0},{4,6},{6,4},{1,3},{3,1},{5,7},{7,5},{8,10},{10,8},{12,... | collective-permute-start | bytes 49160 | tf_op jit(solution)/shard_map/swap_cores/ppermute | solution.py:346
  33.3 0.8 collective-permute-done.10.refs_7_
  34.5 0.9 collective-permute-done.9.refs_5_
  35.4 12.6 %collective-permute-done.6.refs_1_ = f32[264,256]{1,0:T(8,128)S(1)} collective-permute-done((f32[264,256]{1,0:T(8,128)S(1)}, f32[264,256]{1,0:T(8,128)S(1)}, u32[]{:S(2)}, u32[]{:S(2)}) %collective-permute-start.6) | collective-permute-done | bytes 270368 | tf_op jit(solution)/shard_map/sum_products/ppermute | solution.py:341
  48.1 0.8 relax.1
  48.9 5.1 %collective-permute-start.11 = (bf16[336,256]{1,0:T(8,128)(2,1)S(1)}, bf16[336,256]{1,0:T(8,128)(2,1)S(1)}, u32[]{:S(2)}, u32[]{:S(2)}) collective-permute-start(bf16[336,256]{1,0:T(8,128)(2,1)S(1)} %get-tuple-element.50), channel_id=1, source_target_pairs={{0,16},{8,24},{16,0},{24,8},{1,17},{9,25},{17,1},{25,9},{2,18},{10... | collective-permute-start | bytes 516104 | tf_op jit(solution)/shard_map/exchange_back/ppermute | solution.py:341
  54.0 3.1 %collective-permute-start.12 = (bf16[336,256]{1,0:T(8,128)(2,1)S(1)}, bf16[336,256]{1,0:T(8,128)(2,1)S(1)}, u32[]{:S(2)}, u32[]{:S(2)}) collective-permute-start(bf16[336,256]{1,0:T(8,128)(2,1)S(1)} %get-tuple-element.51), channel_id=1, source_target_pairs={{0,24},{8,16},{16,8},{24,0},{1,25},{9,17},{17,9},{25,1},{2,26},{10... | collective-permute-start | bytes 516104 | tf_op jit(solution)/shard_map/exchange_back/ppermute | solution.py:341
  57.1 1.0 %collective-permute-done.11.refs_2_ = bf16[336,256]{1,0:T(8,128)(2,1)S(1)} collective-permute-done((bf16[336,256]{1,0:T(8,128)(2,1)S(1)}, bf16[336,256]{1,0:T(8,128)(2,1)S(1)}, u32[]{:S(2)}, u32[]{:S(2)}) %collective-permute-start.11) | collective-permute-done | bytes 172064 | tf_op jit(solution)/shard_map/exchange_back/ppermute | solution.py:341
  58.1 6.6 %collective-permute-done.12.refs_3_ = bf16[336,256]{1,0:T(8,128)(2,1)S(1)} collective-permute-done((bf16[336,256]{1,0:T(8,128)(2,1)S(1)}, bf16[336,256]{1,0:T(8,128)(2,1)S(1)}, u32[]{:S(2)}, u32[]{:S(2)}) %collective-permute-start.12) | collective-permute-done | bytes 172064 | tf_op jit(solution)/shard_map/exchange_back/ppermute | solution.py:341
  64.8 0.7 exchange_back.1
  65.6 1.3 %collective-permute-start.20 = (bf16[272,1024]{1,0:T(8,128)(2,1)S(1)}, bf16[272,1024]{1,0:T(8,128)(2,1)S(1)}, u32[]{:S(2)}, u32[]{:S(2)}) collective-permute-start(bf16[272,1024]{1,0:T(8,128)(2,1)S(1)} %get-tuple-element.53.refs_0_), channel_id=1, source_target_pairs={{0,1},{1,0},{2,3},{3,2},{4,5},{5,4},{6,7},{7,6},{8,9},{9,8},{10,11... | collective-permute-start | bytes 1671176 | tf_op jit(solution)/shard_map/exchange_back/ppermute | solution.py:352
  66.9 3.7 %collective-permute-start.16 = (bf16[272,1024]{1,0:T(8,128)(2,1)S(1)}, bf16[272,1024]{1,0:T(8,128)(2,1)S(1)}, u32[]{:S(2)}, u32[]{:S(2)}) collective-permute-start(bf16[272,1024]{1,0:T(8,128)(2,1)S(1)} %get-tuple-element.58.refs_0_), channel_id=1, source_target_pairs={{0,2},{2,0},{4,6},{6,4},{1,3},{3,1},{5,7},{7,5},{8,10},{10,8},{12,... | collective-permute-start | bytes 1671176 | tf_op jit(solution)/shard_map/share_generators/ppermute | solution.py:346
  70.6 1.4 %input_gradient.5 = (bf16[72,1024]{1,0:T(8,128)(2,1)S(1)}, bf16[72,1024]{1,0:T(8,128)(2,1)S(1)}, f32[72,1024]{1,0:T(8,128)S(1)}, f32[72,1024]{1,0:T(8,128)S(1)}) custom-call(s32[4]{0:T(128)S(1)} %pad_add_fusion.s_ref, bf16[272,1024]{1,0:T(8,128)(2,1)S(1)} %get-tuple-element.53.refs_0_, bf16[1024,512]{1,0:T(8,128)(2,1)S(1)} %collective-permute-done.2.refs_1_, ...), custom_call_target="tpu_custom_call" | custom-call | flops 536870912 | bytes 4194304 | tf_op jit(solution)/shard_map/input_gradient/pallas_call | solution.py:90
  71.9 1.3 %collective-permute-start.14 = (bf16[72,1024]{1,0:T(8,128)(2,1)S(1)}, bf16[72,1024]{1,0:T(8,128)(2,1)S(1)}, u32[]{:S(2)}, u32[]{:S(2)}) collective-permute-start(bf16[72,1024]{1,0:T(8,128)(2,1)S(1)} %get-tuple-element.55), channel_id=1, source_target_pairs={{0,4},{2,6},{4,0},{6,2},{1,5},{3,7},{5,1},{7,3},{8,12},{10,14},{12... | collective-permute-start | bytes 442376 | tf_op jit(solution)/shard_map/input_gradient/ppermute | solution.py:349
  73.5 3.4 %collective-permute-done.14.refs_1_ = bf16[72,1024]{1,0:T(8,128)(2,1)S(1)} collective-permute-done((bf16[72,1024]{1,0:T(8,128)(2,1)S(1)}, bf16[72,1024]{1,0:T(8,128)(2,1)S(1)}, u32[]{:S(2)}, u32[]{:S(2)}) %collective-permute-start.14) | collective-permute-done | bytes 147488 | tf_op jit(solution)/shard_map/input_gradient/ppermute | solution.py:349
  76.9 2.3 %collective-permute-start.19 = (bf16[336,512]{1,0:T(8,128)(2,1)S(1)}, bf16[336,512]{1,0:T(8,128)(2,1)S(1)}, u32[]{:S(2)}, u32[]{:S(2)}) collective-permute-start(bf16[336,512]{1,0:T(8,128)(2,1)S(1)} %get-tuple-element.59), channel_id=1, source_target_pairs={{0,2},{2,0},{4,6},{6,4},{1,3},{3,1},{5,7},{7,5},{8,10},{10,8},{12,... | collective-permute-start | bytes 1032200 | tf_op jit(solution)/shard_map/exchange_back/ppermute | solution.py:346
  81.2 1.4 %collective-permute-start.21 = (bf16[272,512]{1,0:T(8,128)(2,1)S(1)}, bf16[272,512]{1,0:T(8,128)(2,1)S(1)}, u32[]{:S(2)}, u32[]{:S(2)}) collective-permute-start(bf16[272,512]{1,0:T(8,128)(2,1)S(1)} %input_gradient.8), channel_id=1, source_target_pairs={{0,2},{2,0},{4,6},{6,4},{1,3},{3,1},{5,7},{7,5},{8,10},{10,8},{12,... | collective-permute-start | bytes 835592 | tf_op jit(solution)/shard_map/input_gradient/ppermute | solution.py:346
  82.7 9.1 %collective-permute-start.22 = (bf16[72,1024]{1,0:T(8,128)(2,1)S(1)}, bf16[72,1024]{1,0:T(8,128)(2,1)S(1)}, u32[]{:S(2)}, u32[]{:S(2)}) collective-permute-start(bf16[72,1024]{1,0:T(8,128)(2,1)S(1)} %input_gradient.6.refs_0_), channel_id=1, source_target_pairs={{0,0},{2,16},{4,8},{6,24},{8,2},{10,18},{12,10},{14,26},{16,4},{18... | collective-permute-start | bytes 442376 | tf_op jit(solution)/shard_map/input_gradient/ppermute | solution.py:360
  91.8 1.2 %share_generators.1.left_ref = bf16[1024,1152]{1,0:T(8,128)(2,1)S(1)} custom-call(s32[4]{0:T(128)S(1)} %pad_add_fusion.s_ref, bf16[272,1024]{1,0:T(8,128)(2,1)S(1)} %get-tuple-element.58.refs_0_, bf16[272,1024]{1,0:T(8,128)(2,1)S(1)} %collective-permute-done.16.refs_1_, bf16[272,1024]{1,0:T(8,128)(2,1)S(1)} %collective-permute-done.17.refs_2_, ...), custom_call_target="tpu_custom_call" | custom-call | bytes 1048576 | tf_op jit(solution)/shard_map/share_generators/pallas_call | solution.py:90
  93.1 3.8 %weight_gradient.1 = (f32[1024,512]{1,0:T(8,128)}, f32[1,512]{1,0:T(1,128)}, f32[4,512]{1,0:T(4,128)}, f32[4,512]{1,0:T(4,128)}, bf16[4,32,512]{2,1,0:T(8,128)(2,1)}, /*index=5*/f32[8,128]{1,0:T(8,128)S(1)}) custom-call(s32[4]{0:T(128)S(1)} %pad_add_fusion.s_ref, bf16[72,1024]{1,0:T(8,128)(2,1)S(1)} %input_gradient.7.refs_0_.after_ref, ...), custom_call_target="tpu_custom_call" | custom-call | flops 1207959552 | bytes 6291456 | tf_op jit(solution)/shard_map/weight_gradient/pallas_call | solution.py:502
  97.0 1.4 %input_gradient.9 = (f32[4,32,1024]{2,1,0:T(8,128)}, f32[4,1024]{1,0:T(4,128)}) custom-call(s32[4]{0:T(128)S(1)} %pad_add_fusion.s_ref, f32[8,128]{1,0:T(8,128)S(1)} %get-tuple-element.66.refs_0_, bf16[72,1024]{1,0:T(8,128)(2,1)S(1)} %collective-permute-done.22.refs_1_, bf16[72,1024]{1,0:T(8,128)(2,1)S(1)} %collective-permute-done.23.refs_2_), custom_call_target="tpu_custom_call" | custom-call | bytes 1048576 | tf_op jit(solution)/shard_map/input_gradient/pallas_call | solution.py:90
  (46 shorter events, 6.3 us)
Async XLA Ops:
  0.6 10.9 %copy-start.2 = (s32[4,512]{1,0:T(4,128)S(1)}, s32[4,512]{1,0:T(4,128)}, u32[]{:S(2)}) copy-start(s32[4,512]{1,0:T(4,128)} %param.12) | copy-start | bytes 24580
  0.6 10.9 %copy-start.4 = (f32[4,512]{1,0:T(4,128)S(1)}, f32[4,512]{1,0:T(4,128)}, u32[]{:S(2)}) copy-start(f32[4,512]{1,0:T(4,128)} %param.14) | copy-start | bytes 24580
  0.7 10.9 %copy-start.3 = (f32[4,512]{1,0:T(4,128)S(1)}, f32[4,512]{1,0:T(4,128)}, u32[]{:S(2)}) copy-start(f32[4,512]{1,0:T(4,128)} %param.15) | copy-start | bytes 24580
  0.7 4.1 %collective-permute-start.1 = (bf16[1024,512]{1,0:T(8,128)(2,1)}, bf16[1024,512]{1,0:T(8,128)(2,1)S(1)}, u32[]{:S(2)}, u32[]{:S(2)}) collective-permute-start(bf16[1024,512]{1,0:T(8,128)(2,1)} %param.10), channel_id=1, source_target_pairs={{0,2},{2,0},{4,6},{6,4},{1,3},{3,1},{5,7},{7,5},{8,10},{10,8},{12,... | collective-permute-start | bytes 3145736 | tf_op jit(solution)/shard_map/swap_cores/ppermute | solution.py:346
  0.9 1.2 %copy-start = (bf16[4,32,4096]{2,1,0:T(8,128)(2,1)S(1)}, bf16[4,32,4096]{2,1,0:T(8,128)(2,1)}, u32[]{:S(2)}) copy-start(bf16[4,32,4096]{2,1,0:T(8,128)(2,1)} %refs_0_.1) | copy-start | bytes 3145732
  2.1 0.9 copy-start.1
  5.4 15.4 %collective-permute-start.2 = (bf16[1024,512]{1,0:T(8,128)(2,1)S(1)}, bf16[1024,512]{1,0:T(8,128)(2,1)S(1)}, u32[]{:S(2)}, u32[]{:S(2)}) collective-permute-start(bf16[1024,512]{1,0:T(8,128)(2,1)S(1)} %swap_cores.1), channel_id=1, source_target_pairs={{0,2},{2,0},{4,6},{6,4},{1,3},{3,1},{5,7},{7,5},{8,10},{10,8},{12,... | collective-permute-start | bytes 3145736 | tf_op jit(solution)/shard_map/swap_cores/ppermute | solution.py:346
  5.9 14.9 %collective-permute-start.3 = (bf16[80,1024]{1,0:T(8,128)(2,1)}, bf16[80,1024]{1,0:T(8,128)(2,1)S(1)}, u32[]{:S(2)}, u32[]{:S(2)}) collective-permute-start(bf16[80,1024]{1,0:T(8,128)(2,1)} %get-tuple-element.39), channel_id=1, source_target_pairs={{0,16},{8,24},{16,0},{24,8},{1,17},{9,25},{17,1},{25,9},{2,18},{10... | collective-permute-start | bytes 491528 | tf_op jit(solution)/shard_map/exchange_generators/ppermute | solution.py:341
  9.3 11.5 %collective-permute-start.4 = (bf16[80,1024]{1,0:T(8,128)(2,1)}, bf16[80,1024]{1,0:T(8,128)(2,1)}, u32[]{:S(2)}, u32[]{:S(2)}) collective-permute-start(bf16[80,1024]{1,0:T(8,128)(2,1)} %get-tuple-element.40), channel_id=1, source_target_pairs={{0,24},{8,16},{16,8},{24,0},{1,25},{9,17},{17,9},{25,1},{2,26},{10... | collective-permute-start | bytes 491528 | tf_op jit(solution)/shard_map/exchange_generators/ppermute | solution.py:341
  10.4 10.4 %collective-permute-start.5 = (bf16[80,1024]{1,0:T(8,128)(2,1)}, bf16[80,1024]{1,0:T(8,128)(2,1)}, u32[]{:S(2)}, u32[]{:S(2)}) collective-permute-start(bf16[80,1024]{1,0:T(8,128)(2,1)} %get-tuple-element.41), channel_id=1, source_target_pairs={{0,8},{8,0},{16,24},{24,16},{1,9},{9,1},{17,25},{25,17},{2,10},{10... | collective-permute-start | bytes 491528 | tf_op jit(solution)/shard_map/exchange_generators/ppermute | solution.py:341
  10.6 2.5 %collective-permute-start = (bf16[4,4096]{1,0:T(4,128)(2,1)}, bf16[4,4096]{1,0:T(4,128)(2,1)S(1)}, u32[]{:S(2)}, u32[]{:S(2)}) collective-permute-start(bf16[4,4096]{1,0:T(4,128)(2,1)} %param.9), channel_id=1, source_target_pairs={{0,2},{2,0},{4,6},{6,4},{1,3},{3,1},{5,7},{7,5},{8,10},{10,8},{12,... | collective-permute-start | bytes 98312 | tf_op jit(solution)/shard_map/swap_cores/ppermute | solution.py:346
  23.1 24.9 %collective-permute-start.6 = (f32[264,256]{1,0:T(8,128)S(1)}, f32[264,256]{1,0:T(8,128)S(1)}, u32[]{:S(2)}, u32[]{:S(2)}) collective-permute-start(f32[264,256]{1,0:T(8,128)S(1)} %get-tuple-element.43), channel_id=1, source_target_pairs={{0,16},{8,24},{16,0},{24,8},{1,17},{9,25},{17,1},{25,9},{2,18},{10... | collective-permute-start | bytes 811016 | tf_op jit(solution)/shard_map/sum_products/ppermute | solution.py:341
  29.6 18.4 %collective-permute-start.7 = (f32[264,256]{1,0:T(8,128)S(1)}, f32[264,256]{1,0:T(8,128)S(1)}, u32[]{:S(2)}, u32[]{:S(2)}) collective-permute-start(f32[264,256]{1,0:T(8,128)S(1)} %get-tuple-element.44), channel_id=1, source_target_pairs={{0,24},{8,16},{16,8},{24,0},{1,25},{9,17},{17,9},{25,1},{2,26},{10... | collective-permute-start | bytes 811016 | tf_op jit(solution)/shard_map/sum_products/ppermute | solution.py:341
  29.8 18.3 %collective-permute-start.8 = (f32[264,256]{1,0:T(8,128)S(1)}, f32[264,256]{1,0:T(8,128)S(1)}, u32[]{:S(2)}, u32[]{:S(2)}) collective-permute-start(f32[264,256]{1,0:T(8,128)S(1)} %get-tuple-element.45), channel_id=1, source_target_pairs={{0,8},{8,0},{16,24},{24,16},{1,9},{9,1},{17,25},{25,17},{2,10},{10... | collective-permute-start | bytes 811016 | tf_op jit(solution)/shard_map/sum_products/ppermute | solution.py:341
  30.0 40.5 %collective-permute-start.17 = (bf16[272,1024]{1,0:T(8,128)(2,1)S(1)}, bf16[272,1024]{1,0:T(8,128)(2,1)S(1)}, u32[]{:S(2)}, u32[]{:S(2)}) collective-permute-start(bf16[272,1024]{1,0:T(8,128)(2,1)S(1)} %get-tuple-element.58.refs_0_), channel_id=1, source_target_pairs={{0,1},{1,0},{2,3},{3,2},{4,5},{5,4},{6,7},{7,6},{8,9},{9,8},{10,11... | collective-permute-start | bytes 1671176 | tf_op jit(solution)/shard_map/share_generators/ppermute | solution.py:352
  32.0 2.2 %collective-permute-start.10 = (f32[8,512]{1,0:T(8,128)S(1)}, f32[8,512]{1,0:T(8,128)S(1)}, u32[]{:S(2)}, u32[]{:S(2)}) collective-permute-start(f32[8,512]{1,0:T(8,128)S(1)} %get-tuple-element.71), channel_id=1, source_target_pairs={{0,2},{2,0},{4,6},{6,4},{1,3},{3,1},{5,7},{7,5},{8,10},{10,8},{12,... | collective-permute-start | bytes 49160 | tf_op jit(solution)/shard_map/swap_cores/ppermute | solution.py:346
  34.2 1.3 %collective-permute-start.9 = (bf16[256,128]{1,0:T(8,128)(2,1)S(1)}, bf16[256,128]{1,0:T(8,128)(2,1)S(1)}, u32[]{:S(2)}, u32[]{:S(2)}) collective-permute-start(bf16[256,128]{1,0:T(8,128)(2,1)S(1)} %get-tuple-element.47), channel_id=1, source_target_pairs={{0,2},{2,0},{4,6},{6,4},{1,3},{3,1},{5,7},{7,5},{8,10},{10,8},{12,... | collective-permute-start | bytes 196616 | tf_op jit(solution)/shard_map/sum_products/ppermute | solution.py:346
  48.9 9.2 %collective-permute-start.11 = (bf16[336,256]{1,0:T(8,128)(2,1)S(1)}, bf16[336,256]{1,0:T(8,128)(2,1)S(1)}, u32[]{:S(2)}, u32[]{:S(2)}) collective-permute-start(bf16[336,256]{1,0:T(8,128)(2,1)S(1)} %get-tuple-element.50), channel_id=1, source_target_pairs={{0,16},{8,24},{16,0},{24,8},{1,17},{9,25},{17,1},{25,9},{2,18},{10... | collective-permute-start | bytes 516104 | tf_op jit(solution)/shard_map/exchange_back/ppermute | solution.py:341
  54.0 10.7 %collective-permute-start.12 = (bf16[336,256]{1,0:T(8,128)(2,1)S(1)}, bf16[336,256]{1,0:T(8,128)(2,1)S(1)}, u32[]{:S(2)}, u32[]{:S(2)}) collective-permute-start(bf16[336,256]{1,0:T(8,128)(2,1)S(1)} %get-tuple-element.51), channel_id=1, source_target_pairs={{0,24},{8,16},{16,8},{24,0},{1,25},{9,17},{17,9},{25,1},{2,26},{10... | collective-permute-start | bytes 516104 | tf_op jit(solution)/shard_map/exchange_back/ppermute | solution.py:341
  57.1 7.7 %collective-permute-start.13 = (bf16[336,256]{1,0:T(8,128)(2,1)S(1)}, bf16[336,256]{1,0:T(8,128)(2,1)S(1)}, u32[]{:S(2)}, u32[]{:S(2)}) collective-permute-start(bf16[336,256]{1,0:T(8,128)(2,1)S(1)} %get-tuple-element.52), channel_id=1, source_target_pairs={{0,8},{8,0},{16,24},{24,16},{1,9},{9,1},{17,25},{25,17},{2,10},{10... | collective-permute-start | bytes 516104 | tf_op jit(solution)/shard_map/exchange_back/ppermute | solution.py:341
  65.6 15.1 %collective-permute-start.20 = (bf16[272,1024]{1,0:T(8,128)(2,1)S(1)}, bf16[272,1024]{1,0:T(8,128)(2,1)S(1)}, u32[]{:S(2)}, u32[]{:S(2)}) collective-permute-start(bf16[272,1024]{1,0:T(8,128)(2,1)S(1)} %get-tuple-element.53.refs_0_), channel_id=1, source_target_pairs={{0,1},{1,0},{2,3},{3,2},{4,5},{5,4},{6,7},{7,6},{8,9},{9,8},{10,11... | collective-permute-start | bytes 1671176 | tf_op jit(solution)/shard_map/exchange_back/ppermute | solution.py:352
  66.9 15.8 %collective-permute-start.16 = (bf16[272,1024]{1,0:T(8,128)(2,1)S(1)}, bf16[272,1024]{1,0:T(8,128)(2,1)S(1)}, u32[]{:S(2)}, u32[]{:S(2)}) collective-permute-start(bf16[272,1024]{1,0:T(8,128)(2,1)S(1)} %get-tuple-element.58.refs_0_), channel_id=1, source_target_pairs={{0,2},{2,0},{4,6},{6,4},{1,3},{3,1},{5,7},{7,5},{8,10},{10,8},{12,... | collective-permute-start | bytes 1671176 | tf_op jit(solution)/shard_map/share_generators/ppermute | solution.py:346
  70.6 21.3 %collective-permute-start.18 = (bf16[272,1024]{1,0:T(8,128)(2,1)S(1)}, bf16[272,1024]{1,0:T(8,128)(2,1)S(1)}, u32[]{:S(2)}, u32[]{:S(2)}) collective-permute-start(bf16[272,1024]{1,0:T(8,128)(2,1)S(1)} %collective-permute-done.17.refs_2_), channel_id=1, source_target_pairs={{0,2},{2,0},{4,6},{6,4},{1,3},{3,1},{5,7},{7,5},{8,10},{10,8},{12,... | collective-permute-start | bytes 1671176 | tf_op jit(solution)/shard_map/share_generators/ppermute | solution.py:346
  71.9 5.0 %collective-permute-start.14 = (bf16[72,1024]{1,0:T(8,128)(2,1)S(1)}, bf16[72,1024]{1,0:T(8,128)(2,1)S(1)}, u32[]{:S(2)}, u32[]{:S(2)}) collective-permute-start(bf16[72,1024]{1,0:T(8,128)(2,1)S(1)} %get-tuple-element.55), channel_id=1, source_target_pairs={{0,4},{2,6},{4,0},{6,2},{1,5},{3,7},{5,1},{7,3},{8,12},{10,14},{12... | collective-permute-start | bytes 442376 | tf_op jit(solution)/shard_map/input_gradient/ppermute | solution.py:349
  73.2 6.9 %collective-permute-start.15 = (bf16[72,1024]{1,0:T(8,128)(2,1)S(1)}, bf16[72,1024]{1,0:T(8,128)(2,1)S(1)}, u32[]{:S(2)}, u32[]{:S(2)}) collective-permute-start(bf16[72,1024]{1,0:T(8,128)(2,1)S(1)} %get-tuple-element.57), channel_id=1, source_target_pairs={{0,4},{2,6},{4,0},{6,2},{1,5},{3,7},{5,1},{7,3},{8,12},{10,14},{12... | collective-permute-start | bytes 442376 | tf_op jit(solution)/shard_map/input_gradient/ppermute | solution.py:349
  76.9 16.2 %collective-permute-start.19 = (bf16[336,512]{1,0:T(8,128)(2,1)S(1)}, bf16[336,512]{1,0:T(8,128)(2,1)S(1)}, u32[]{:S(2)}, u32[]{:S(2)}) collective-permute-start(bf16[336,512]{1,0:T(8,128)(2,1)S(1)} %get-tuple-element.59), channel_id=1, source_target_pairs={{0,2},{2,0},{4,6},{6,4},{1,3},{3,1},{5,7},{7,5},{8,10},{10,8},{12,... | collective-permute-start | bytes 1032200 | tf_op jit(solution)/shard_map/exchange_back/ppermute | solution.py:346
  81.2 11.9 %collective-permute-start.21 = (bf16[272,512]{1,0:T(8,128)(2,1)S(1)}, bf16[272,512]{1,0:T(8,128)(2,1)S(1)}, u32[]{:S(2)}, u32[]{:S(2)}) collective-permute-start(bf16[272,512]{1,0:T(8,128)(2,1)S(1)} %input_gradient.8), channel_id=1, source_target_pairs={{0,2},{2,0},{4,6},{6,4},{1,3},{3,1},{5,7},{7,5},{8,10},{10,8},{12,... | collective-permute-start | bytes 835592 | tf_op jit(solution)/shard_map/input_gradient/ppermute | solution.py:346
  82.6 14.2 %collective-permute-start.23 = (bf16[72,1024]{1,0:T(8,128)(2,1)S(1)}, bf16[72,1024]{1,0:T(8,128)(2,1)S(1)}, u32[]{:S(2)}, u32[]{:S(2)}) collective-permute-start(bf16[72,1024]{1,0:T(8,128)(2,1)S(1)} %input_gradient.7.refs_0_.after_ref), channel_id=1, source_target_pairs={{0,16},{2,0},{4,24},{6,8},{8,18},{10,2},{12,26},{14,10},{16,20},{1... | collective-permute-start | bytes 442376 | tf_op jit(solution)/shard_map/input_gradient/ppermute | solution.py:360
  82.7 14.3 %collective-permute-start.22 = (bf16[72,1024]{1,0:T(8,128)(2,1)S(1)}, bf16[72,1024]{1,0:T(8,128)(2,1)S(1)}, u32[]{:S(2)}, u32[]{:S(2)}) collective-permute-start(bf16[72,1024]{1,0:T(8,128)(2,1)S(1)} %input_gradient.6.refs_0_), channel_id=1, source_target_pairs={{0,0},{2,16},{4,8},{6,24},{8,2},{10,18},{12,10},{14,26},{16,4},{18... | collective-permute-start | bytes 442376 | tf_op jit(solution)/shard_map/input_gradient/ppermute | solution.py:360

commit v4 on v3

--- a/solution.py
+++ b/solution.py
@@ -9,7 +9,7 @@
 
 BF = jnp.bfloat16
 F32 = jnp.float32
-VMEM_LIMIT = 24 * 1024 * 1024
+VMEM_LIMIT = 32 * 1024 * 1024
 
 
 def neuron(center_pre, radius, phase):
@@ -66,7 +66,7 @@
 
 CENTER_ROWS = 16
 HALVES = 1
-ORDER = (0, 2, 3, 1)
+ORDER = (0, 3, 2, 1)
 
 
 def params():
@@ -81,7 +81,7 @@
     return pl.BlockSpec(x.shape, lambda i, s, r=len(x.shape): (0,) * r)
 
 
-def call(kernel, scalars, args, specs, outs, scratch=(), after=(), cost=(0, 1 << 20)):
+def call(kernel, scalars, args, specs, outs, scratch=(), after=(), cost=None):
     skip = len(after)
 
     def body(s_ref, *refs):
@@ -98,7 +98,7 @@
         ),
         out_shape=outs,
         compiler_params=params(),
-        cost_estimate=pl.CostEstimate(flops=cost[0], bytes_accessed=cost[1], transcendentals=0),
+        cost_estimate=cost and pl.CostEstimate(flops=cost[0], bytes_accessed=cost[1], transcendentals=0),
     )(scalars, *after, *args)
 
 
@@ -374,11 +374,9 @@
         recv = over_gen(msgs)
     with jax.named_scope("swap_cores"):
         w_other = over_core(weight)
-        (w_back,) = call(
-            copy_kernel, scalars, [w_other], [whole(w_other)], [shape(weight.shape, BF)], after=msgs[:1]
-        )
-        w_own = over_core(w_back)
-        center = over_core(center)
+        (w_near,) = call(
+            copy_kernel, scalars, [weight], [whole(weight)], [shape(weight.shape, BF)], after=[recv[1]]
+        )
         stacked = jnp.stack([phase.astype(F32), center_cot, offset_cot])
 
         def small(core):
@@ -392,10 +390,10 @@
         a_own, cot_keep, cot_send, *products = call(
             functools.partial(forward_kernel, size),
             scalars,
-            [center, w_own, w_other, *recv],
+            [center, w_near, w_other, *recv],
             [
                 pl.BlockSpec((box_dev, depth), lambda i, s: (0, s[0])),
-                whole(w_own),
+                whole(w_near),
                 whole(w_other),
                 *[whole(r) for r in recv],
             ],
@@ -448,9 +446,7 @@
                     shape((work + group, cols), BF),
                     shape((group, cols), BF),
                 ],
-                after=sends[-1][:1] if h else [],
             )
-            full_box = over_box(full)
             core_part = over_core(oth)
             keeps.append(out_own)
         with jax.named_scope("input_gradient"):
@@ -459,8 +455,8 @@
                 call(
                     functools.partial(input_grad_kernel, size),
                     scalars,
-                    [full, w_own, w_other],
-                    [whole(full), whole(w_own), whole(w_other)],
+                    [full, w_near, w_other],
+                    [whole(full), whole(w_near), whole(w_other)],
                     [shape((both, depth), BF)] * 2 + [shape((both, depth), F32)] * 2,
                     [pltpu.VMEM((work, depth), F32)],
                     cost=(2 * rows * depth * 2 * cols, 4 << 20),
@@ -468,25 +464,30 @@
             )
     with jax.named_scope("input_gradient"):
         (send_0, send_1, *keeps_f32), = sends
-        fars = [over_x(send_0), over_x(send_1)]
-        pairs = []
-        for keep, far in zip(keeps_f32, fars):
-            pairs += call(
+        def pair(keep, far, *after):
+            (out,) = call(
                 input_pair_kernel,
                 scalars,
                 [keep, far],
                 [whole(keep), whole(far)],
                 [shape((group + 8, depth), BF)],
-                after=pairs[-1:],
+                after=after,
             )
-        finals = [turned(m, k) for k, m in enumerate(pairs)]
+            return out
+
+        first = pair(keeps_f32[0], over_x(send_0))
+        full_box = over_box(full)
+        finals = [turned(first, 0)]
+        far_1 = over_x(send_1)
+        last = pair(keeps_f32[1], far_1, finals[0])
+        finals.append(turned(last, 1))
         (box_oth,) = call(
             copy_kernel,
             scalars,
             [full_box],
             [pl.BlockSpec((work, cols), lambda i, s: (0, 1))],
             [shape((work, cols), BF)],
-            after=pairs[-1:],
+            after=[last],
         )
         rights = [full, core_part, full_box, over_core(box_oth)]
     with jax.named_scope("weight_gradient"):
@@ -512,10 +513,7 @@
             ),
             out_shape=out_shape,
             compiler_params=params(),
-            cost_estimate=pl.CostEstimate(
-                flops=2 * left.shape[1] * depth * cols, bytes_accessed=6 << 20, transcendentals=0
-            ),
-        )(scalars, pairs[-1], left, *rights, *keeps)
+        )(scalars, last, left, *rights, *keeps)
     with jax.named_scope("input_gradient"):
         gens_grad, center_grad = call(
             functools.partial(input_final_kernel, boxes),

time: 98.6 us -> 93.9 us (0.952)
  the two profiles are of different devices: /device:TPU:1 before, /device:TPU:3 now
where the time goes in v4:
time: 93.9 us; the launch traced here: 93.5 us
  waiting for transfers between devices  38.2 us (41%)
  starting transfers between devices  35.6 us (38%)
  Pallas kernels  13.9 us (15%)
  local copies, waits for them, and re-layouts  3.48 us (4%)
  other arithmetic  1.57 us (2%)
    ppermute x9, waiting for transfers between devices, over_gen(): lax.ppermute(piece, 'gen', [(i, i ^ k) for i in range(size)])  33.7 us
    ppermute x7, starting transfers between devices, over_core(): return lax.ppermute(x, 'neur', [(i, i ^ 1) for i in range(size)])  11.4 us
    ppermute x9, starting transfers between devices, over_gen(): lax.ppermute(piece, 'gen', [(i, i ^ k) for i in range(size)])  11 us
    pallas_call x11, Pallas kernels, call(): pl.pallas_call(body, grid_spec=pltpu.PrefetchScalarGridSpec(num_scalar_pr...  10.2 us
    ppermute x2, starting transfers between devices, turned(): return lax.ppermute(x, ('gen', 'neur'), pairs)  9.16 us
    pallas_call x1, Pallas kernels, square_body(): pl.pallas_call(functools.partial(weight_grad_kernel, boxes), grid_spec=pl...  3.78 us
    unnamed x10, local copies, waits for them, and re-layouts  3.36 us
    ppermute x2, waiting for transfers between devices, turned(): return lax.ppermute(x, ('gen', 'neur'), pairs)  2.73 us
  transfers between devices with their start and end apart: 22, of which 10 were waited for; matrix products, arithmetic and copies ran while one was open for 2% of the time, Pallas kernels for 12%

profile of v4, /device:TPU:3, one launch (start us, length us, event | category | flops | bytes accessed | tf_op | source)
XLA Modules:
  0.0 93.5 jit_solution(9277378116964920022)
XLA Ops:
  1.5 1.2 %copy-done.1 = bf16[4,32,4096]{2,1,0:T(8,128)(2,1)S(1)} copy-done((bf16[4,32,4096]{2,1,0:T(8,128)(2,1)S(1)}, bf16[4,32,4096]{2,1,0:T(8,128)(2,1)}, u32[]{:S(2)}) %copy-start.1) | copy-done | bytes 1048600
  2.7 0.9 copy-done.2
  3.6 1.0 %exchange_generators.1 = (bf16[80,1024]{1,0:T(8,128)(2,1)S(1)}, bf16[80,1024]{1,0:T(8,128)(2,1)S(1)}, bf16[80,1024]{1,0:T(8,128)(2,1)S(1)}, bf16[80,1024]{1,0:T(8,128)(2,1)S(1)}) custom-call(s32[4]{0:T(128)S(1)} %pad_add_fusion.s_ref, bf16[4,32,4096]{2,1,0:T(8,128)(2,1)S(1)} %copy-done.1, bf16[4,32,512]{2,1,0:T(8,128)(2,1)S(1)} %copy-done.2), custom_call_target="tpu_custom_call" | custom-call | bytes 33554432 | tf_op jit(solution)/shard_map/exchange_generators/pallas_call | solution.py:90
  4.6 3.4 %collective-permute-start = (bf16[80,1024]{1,0:T(8,128)(2,1)S(1)}, bf16[80,1024]{1,0:T(8,128)(2,1)S(1)}, u32[]{:S(2)}, u32[]{:S(2)}) collective-permute-start(bf16[80,1024]{1,0:T(8,128)(2,1)S(1)} %get-tuple-element.38), channel_id=1, source_target_pairs={{0,24},{8,16},{16,8},{24,0},{1,25},{9,17},{17,9},{25,1},{2,26},{10... | collective-permute-start | bytes 491528 | tf_op jit(solution)/shard_map/exchange_generators/ppermute | solution.py:341
  9.9 2.5 %collective-permute-done.refs_0_.refs_4_ = bf16[80,1024]{1,0:T(8,128)(2,1)S(1)} collective-permute-done((bf16[80,1024]{1,0:T(8,128)(2,1)S(1)}, bf16[80,1024]{1,0:T(8,128)(2,1)S(1)}, u32[]{:S(2)}, u32[]{:S(2)}) %collective-permute-start) | collective-permute-done | bytes 163872 | tf_op jit(solution)/shard_map/exchange_generators/ppermute | solution.py:341
  12.4 1.2 %copy-done = bf16[1024,512]{1,0:T(8,128)(2,1)S(1)} copy-done((bf16[1024,512]{1,0:T(8,128)(2,1)S(1)}, bf16[1024,512]{1,0:T(8,128)(2,1)}, u32[]{:S(2)}) %copy-start) | copy-done | bytes 1048600
  14.3 7.7 %collective-permute-done.2.refs_5_ = bf16[80,1024]{1,0:T(8,128)(2,1)S(1)} collective-permute-done((bf16[80,1024]{1,0:T(8,128)(2,1)S(1)}, bf16[80,1024]{1,0:T(8,128)(2,1)S(1)}, u32[]{:S(2)}, u32[]{:S(2)}) %collective-permute-start.2) | collective-permute-done | bytes 163872 | tf_op jit(solution)/shard_map/exchange_generators/ppermute | solution.py:341
  22.0 1.4 %forward.1 = (bf16[272,1024]{1,0:T(8,128)(2,1)S(1)}, bf16[256,128]{1,0:T(8,128)(2,1)S(1)}, bf16[256,128]{1,0:T(8,128)(2,1)S(1)}, f32[264,256]{1,0:T(8,128)S(1)},...) custom-call(s32[4]{0:T(128)S(1)} %pad_add_fusion.s_ref, bf16[4,4096]{1,0:T(4,128)(2,1)S(1)} %copy-done.3, ...), custom_call_target="tpu_custom_call" | custom-call | flops 536870912 | bytes 4194304 | tf_op jit(solution)/shard_map/forward/pallas_call | solution.py:90
  23.4 2.3 %collective-permute-start.4 = (f32[264,256]{1,0:T(8,128)S(1)}, f32[264,256]{1,0:T(8,128)S(1)}, u32[]{:S(2)}, u32[]{:S(2)}) collective-permute-start(f32[264,256]{1,0:T(8,128)S(1)} %get-tuple-element.43), channel_id=1, source_target_pairs={{0,24},{8,16},{16,8},{24,0},{1,25},{9,17},{17,9},{25,1},{2,26},{10... | collective-permute-start | bytes 811016 | tf_op jit(solution)/shard_map/sum_products/ppermute | solution.py:341
  25.6 1.4 %collective-permute-start.6 = (f32[264,256]{1,0:T(8,128)S(1)}, f32[264,256]{1,0:T(8,128)S(1)}, u32[]{:S(2)}, u32[]{:S(2)}) collective-permute-start(f32[264,256]{1,0:T(8,128)S(1)} %get-tuple-element.45), channel_id=1, source_target_pairs={{0,8},{8,0},{16,24},{24,16},{1,9},{9,1},{17,25},{25,17},{2,10},{10... | collective-permute-start | bytes 811016 | tf_op jit(solution)/shard_map/sum_products/ppermute | solution.py:341
  27.0 1.2 %collective-permute-start.16 = (bf16[272,1024]{1,0:T(8,128)(2,1)S(1)}, bf16[272,1024]{1,0:T(8,128)(2,1)S(1)}, u32[]{:S(2)}, u32[]{:S(2)}) collective-permute-start(bf16[272,1024]{1,0:T(8,128)(2,1)S(1)} %get-tuple-element.58.refs_0_), channel_id=1, source_target_pairs={{0,1},{1,0},{2,3},{3,2},{4,5},{5,4},{6,7},{7,6},{8,9},{9,8},{10,11... | collective-permute-start | bytes 1671176 | tf_op jit(solution)/shard_map/share_generators/ppermute | solution.py:352
  28.3 1.9 %collective-permute-start.8 = (f32[8,512]{1,0:T(8,128)S(1)}, f32[8,512]{1,0:T(8,128)S(1)}, u32[]{:S(2)}, u32[]{:S(2)}) collective-permute-start(f32[8,512]{1,0:T(8,128)S(1)} %get-tuple-element.71), channel_id=1, source_target_pairs={{0,2},{2,0},{4,6},{6,4},{1,3},{3,1},{5,7},{7,5},{8,10},{10,8},{12,... | collective-permute-start | bytes 49160 | tf_op jit(solution)/shard_map/swap_cores/ppermute | solution.py:346
  30.3 0.8 collective-permute-done.8.refs_7_
  31.5 0.9 collective-permute-done.7.refs_5_
  32.6 14.6 %collective-permute-done.5.refs_2_ = f32[264,256]{1,0:T(8,128)S(1)} collective-permute-done((f32[264,256]{1,0:T(8,128)S(1)}, f32[264,256]{1,0:T(8,128)S(1)}, u32[]{:S(2)}, u32[]{:S(2)}) %collective-permute-start.5) | collective-permute-done | bytes 270368 | tf_op jit(solution)/shard_map/sum_products/ppermute | solution.py:341
  48.0 1.3 %collective-permute-start.11 = (bf16[336,256]{1,0:T(8,128)(2,1)S(1)}, bf16[336,256]{1,0:T(8,128)(2,1)S(1)}, u32[]{:S(2)}, u32[]{:S(2)}) collective-permute-start(bf16[336,256]{1,0:T(8,128)(2,1)S(1)} %get-tuple-element.52), channel_id=1, source_target_pairs={{0,8},{8,0},{16,24},{24,16},{1,9},{9,1},{17,25},{25,17},{2,10},{10... | collective-permute-start | bytes 516104 | tf_op jit(solution)/shard_map/exchange_back/ppermute | solution.py:341
  49.3 2.3 %collective-permute-start.9 = (bf16[336,256]{1,0:T(8,128)(2,1)S(1)}, bf16[336,256]{1,0:T(8,128)(2,1)S(1)}, u32[]{:S(2)}, u32[]{:S(2)}) collective-permute-start(bf16[336,256]{1,0:T(8,128)(2,1)S(1)} %get-tuple-element.50), channel_id=1, source_target_pairs={{0,24},{8,16},{16,8},{24,0},{1,25},{9,17},{17,9},{25,1},{2,26},{10... | collective-permute-start | bytes 516104 | tf_op jit(solution)/shard_map/exchange_back/ppermute | solution.py:341
  51.6 5.1 %collective-permute-done.10.refs_3_ = bf16[336,256]{1,0:T(8,128)(2,1)S(1)} collective-permute-done((bf16[336,256]{1,0:T(8,128)(2,1)S(1)}, bf16[336,256]{1,0:T(8,128)(2,1)S(1)}, u32[]{:S(2)}, u32[]{:S(2)}) %collective-permute-start.10) | collective-permute-done | bytes 172064 | tf_op jit(solution)/shard_map/exchange_back/ppermute | solution.py:341
  56.6 3.5 %collective-permute-done.9.refs_2_ = bf16[336,256]{1,0:T(8,128)(2,1)S(1)} collective-permute-done((bf16[336,256]{1,0:T(8,128)(2,1)S(1)}, bf16[336,256]{1,0:T(8,128)(2,1)S(1)}, u32[]{:S(2)}, u32[]{:S(2)}) %collective-permute-start.9) | collective-permute-done | bytes 172064 | tf_op jit(solution)/shard_map/exchange_back/ppermute | solution.py:341
  60.9 1.3 %collective-permute-start.19 = (bf16[272,1024]{1,0:T(8,128)(2,1)S(1)}, bf16[272,1024]{1,0:T(8,128)(2,1)S(1)}, u32[]{:S(2)}, u32[]{:S(2)}) collective-permute-start(bf16[272,1024]{1,0:T(8,128)(2,1)S(1)} %get-tuple-element.53.refs_0_), channel_id=1, source_target_pairs={{0,1},{1,0},{2,3},{3,2},{4,5},{5,4},{6,7},{7,6},{8,9},{9,8},{10,11... | collective-permute-start | bytes 1671176 | tf_op jit(solution)/shard_map/input_gradient/ppermute | solution.py:352
  62.2 1.4 %input_gradient.5 = (bf16[72,1024]{1,0:T(8,128)(2,1)S(1)}, bf16[72,1024]{1,0:T(8,128)(2,1)S(1)}, f32[72,1024]{1,0:T(8,128)S(1)}, f32[72,1024]{1,0:T(8,128)S(1)}) custom-call(s32[4]{0:T(128)S(1)} %pad_add_fusion.s_ref, bf16[272,1024]{1,0:T(8,128)(2,1)S(1)} %get-tuple-element.53.refs_0_, bf16[1024,512]{1,0:T(8,128)(2,1)S(1)} %swap_cores.1.refs_1_, ...), custom_call_target="tpu_custom_call" | custom-call | flops 536870912 | bytes 4194304 | tf_op jit(solution)/shard_map/input_gradient/pallas_call | solution.py:90
  63.9 3.2 %collective-permute-start.15 = (bf16[272,1024]{1,0:T(8,128)(2,1)S(1)}, bf16[272,1024]{1,0:T(8,128)(2,1)S(1)}, u32[]{:S(2)}, u32[]{:S(2)}) collective-permute-start(bf16[272,1024]{1,0:T(8,128)(2,1)S(1)} %get-tuple-element.58.refs_0_), channel_id=1, source_target_pairs={{0,2},{2,0},{4,6},{6,4},{1,3},{3,1},{5,7},{7,5},{8,10},{10,8},{12,... | collective-permute-start | bytes 1671176 | tf_op jit(solution)/shard_map/share_generators/ppermute | solution.py:346
  67.1 1.2 %collective-permute-start.14 = (bf16[72,1024]{1,0:T(8,128)(2,1)S(1)}, bf16[72,1024]{1,0:T(8,128)(2,1)S(1)}, u32[]{:S(2)}, u32[]{:S(2)}) collective-permute-start(bf16[72,1024]{1,0:T(8,128)(2,1)S(1)} %get-tuple-element.57), channel_id=1, source_target_pairs={{0,4},{2,6},{4,0},{6,2},{1,5},{3,7},{5,1},{7,3},{8,12},{10,14},{12... | collective-permute-start | bytes 442376 | tf_op jit(solution)/shard_map/input_gradient/ppermute | solution.py:349
  68.9 7.4 %collective-permute-start.13 = (bf16[72,1024]{1,0:T(8,128)(2,1)S(1)}, bf16[72,1024]{1,0:T(8,128)(2,1)S(1)}, u32[]{:S(2)}, u32[]{:S(2)}) collective-permute-start(bf16[72,1024]{1,0:T(8,128)(2,1)S(1)} %input_gradient.6), channel_id=1, source_target_pairs={{0,0},{2,16},{4,8},{6,24},{8,2},{10,18},{12,10},{14,26},{16,4},{18... | collective-permute-start | bytes 442376 | tf_op jit(solution)/shard_map/input_gradient/ppermute | solution.py:360
  76.3 1.6 %collective-permute-start.18 = (bf16[336,512]{1,0:T(8,128)(2,1)S(1)}, bf16[336,512]{1,0:T(8,128)(2,1)S(1)}, u32[]{:S(2)}, u32[]{:S(2)}) collective-permute-start(bf16[336,512]{1,0:T(8,128)(2,1)S(1)} %get-tuple-element.59), channel_id=1, source_target_pairs={{0,2},{2,0},{4,6},{6,4},{1,3},{3,1},{5,7},{7,5},{8,10},{10,8},{12,... | collective-permute-start | bytes 1032200 | tf_op jit(solution)/shard_map/exchange_back/ppermute | solution.py:346
  77.9 1.2 %collective-permute-done.13.refs_0_.refs_1_ = bf16[72,1024]{1,0:T(8,128)(2,1)S(1)} collective-permute-done((bf16[72,1024]{1,0:T(8,128)(2,1)S(1)}, bf16[72,1024]{1,0:T(8,128)(2,1)S(1)}, u32[]{:S(2)}, u32[]{:S(2)}) %collective-permute-start.13) | collective-permute-done | bytes 147488 | tf_op jit(solution)/shard_map/input_gradient/ppermute | solution.py:360
  80.3 3.6 %collective-permute-start.20 = (bf16[272,512]{1,0:T(8,128)(2,1)S(1)}, bf16[272,512]{1,0:T(8,128)(2,1)S(1)}, u32[]{:S(2)}, u32[]{:S(2)}) collective-permute-start(bf16[272,512]{1,0:T(8,128)(2,1)S(1)} %input_gradient.8), channel_id=1, source_target_pairs={{0,2},{2,0},{4,6},{6,4},{1,3},{3,1},{5,7},{7,5},{8,10},{10,8},{12,... | collective-permute-start | bytes 835592 | tf_op jit(solution)/shard_map/input_gradient/ppermute | solution.py:346
  83.9 1.7 %collective-permute-start.21 = (bf16[72,1024]{1,0:T(8,128)(2,1)S(1)}, bf16[72,1024]{1,0:T(8,128)(2,1)S(1)}, u32[]{:S(2)}, u32[]{:S(2)}) collective-permute-start(bf16[72,1024]{1,0:T(8,128)(2,1)S(1)} %input_gradient.7.refs_0_.after_ref), channel_id=1, source_target_pairs={{0,16},{2,0},{4,24},{6,8},{8,18},{10,2},{12,26},{14,10},{16,20},{1... | collective-permute-start | bytes 442376 | tf_op jit(solution)/shard_map/input_gradient/ppermute | solution.py:360
  85.7 1.2 %share_generators.1.left_ref = bf16[1024,1152]{1,0:T(8,128)(2,1)S(1)} custom-call(s32[4]{0:T(128)S(1)} %pad_add_fusion.s_ref, bf16[272,1024]{1,0:T(8,128)(2,1)S(1)} %get-tuple-element.58.refs_0_, bf16[272,1024]{1,0:T(8,128)(2,1)S(1)} %collective-permute-done.15.refs_1_, bf16[272,1024]{1,0:T(8,128)(2,1)S(1)} %collective-permute-done.16.refs_2_, ...), custom_call_target="tpu_custom_call" | custom-call | tf_op jit(solution)/shard_map/share_generators/pallas_call | solution.py:90
  86.9 3.8 %weight_gradient.1 = (f32[1024,512]{1,0:T(8,128)}, f32[1,512]{1,0:T(1,128)}, f32[4,512]{1,0:T(4,128)}, f32[4,512]{1,0:T(4,128)}, bf16[4,32,512]{2,1,0:T(8,128)(2,1)}, /*index=5*/f32[8,128]{1,0:T(8,128)S(1)}) custom-call(s32[4]{0:T(128)S(1)} %pad_add_fusion.s_ref, bf16[72,1024]{1,0:T(8,128)(2,1)S(1)} %input_gradient.7.refs_0_.after_ref, ...), custom_call_target="tpu_custom_call" | custom-call | tf_op jit(solution)/shard_map/weight_gradient/pallas_call | solution.py:503
  90.7 1.5 %collective-permute-done.21.refs_2_ = bf16[72,1024]{1,0:T(8,128)(2,1)S(1)} collective-permute-done((bf16[72,1024]{1,0:T(8,128)(2,1)S(1)}, bf16[72,1024]{1,0:T(8,128)(2,1)S(1)}, u32[]{:S(2)}, u32[]{:S(2)}) %collective-permute-start.21) | collective-permute-done | bytes 147488 | tf_op jit(solution)/shard_map/input_gradient/ppermute | solution.py:360
  92.2 1.4 %input_gradient.9 = (f32[4,32,1024]{2,1,0:T(8,128)}, f32[4,1024]{1,0:T(4,128)}) custom-call(s32[4]{0:T(128)S(1)} %pad_add_fusion.s_ref, f32[8,128]{1,0:T(8,128)S(1)} %get-tuple-element.66.refs_0_, bf16[72,1024]{1,0:T(8,128)(2,1)S(1)} %collective-permute-done.13.refs_0_.refs_1_, bf16[72,1024]{1,0:T(8,128)(2,1)S(1)} %collective-permute-done.21.refs_2_), custom_call_target="tpu_custom_call" | custom-call | tf_op jit(solution)/shard_map/input_gradient/pallas_call | solution.py:90
  (42 shorter events, 7.6 us)
Async XLA Ops:
  0.6 21.4 %copy-start.3 = (bf16[4,4096]{1,0:T(4,128)(2,1)S(1)}, bf16[4,4096]{1,0:T(4,128)(2,1)}, u32[]{:S(2)}) copy-start(bf16[4,4096]{1,0:T(4,128)(2,1)} %refs_0_.3) | copy-start | bytes 98308
  0.6 21.4 %collective-permute-start.1 = (bf16[1024,512]{1,0:T(8,128)(2,1)}, bf16[1024,512]{1,0:T(8,128)(2,1)S(1)}, u32[]{:S(2)}, u32[]{:S(2)}) collective-permute-start(bf16[1024,512]{1,0:T(8,128)(2,1)} %refs_1_.3), channel_id=1, source_target_pairs={{0,2},{2,0},{4,6},{6,4},{1,3},{3,1},{5,7},{7,5},{8,10},{10,8},{12,... | collective-permute-start | bytes 3145736 | tf_op jit(solution)/shard_map/swap_cores/ppermute | solution.py:346
  1.5 1.2 %copy-start.1 = (bf16[4,32,4096]{2,1,0:T(8,128)(2,1)S(1)}, bf16[4,32,4096]{2,1,0:T(8,128)(2,1)}, u32[]{:S(2)}) copy-start(bf16[4,32,4096]{2,1,0:T(8,128)(2,1)} %refs_0_.2) | copy-start | bytes 3145732
  2.7 0.9 copy-start.2
  4.6 7.8 %collective-permute-start = (bf16[80,1024]{1,0:T(8,128)(2,1)S(1)}, bf16[80,1024]{1,0:T(8,128)(2,1)S(1)}, u32[]{:S(2)}, u32[]{:S(2)}) collective-permute-start(bf16[80,1024]{1,0:T(8,128)(2,1)S(1)} %get-tuple-element.38), channel_id=1, source_target_pairs={{0,24},{8,16},{16,8},{24,0},{1,25},{9,17},{17,9},{25,1},{2,26},{10... | collective-permute-start | bytes 491528 | tf_op jit(solution)/shard_map/exchange_generators/ppermute | solution.py:341
  8.0 14.0 %collective-permute-start.2 = (bf16[80,1024]{1,0:T(8,128)(2,1)S(1)}, bf16[80,1024]{1,0:T(8,128)(2,1)S(1)}, u32[]{:S(2)}, u32[]{:S(2)}) collective-permute-start(bf16[80,1024]{1,0:T(8,128)(2,1)S(1)} %get-tuple-element.40), channel_id=1, source_target_pairs={{0,16},{8,24},{16,0},{24,8},{1,17},{9,25},{17,1},{25,9},{2,18},{10... | collective-permute-start | bytes 491528 | tf_op jit(solution)/shard_map/exchange_generators/ppermute | solution.py:341
  8.0 14.0 %collective-permute-start.3 = (bf16[80,1024]{1,0:T(8,128)(2,1)S(1)}, bf16[80,1024]{1,0:T(8,128)(2,1)S(1)}, u32[]{:S(2)}, u32[]{:S(2)}) collective-permute-start(bf16[80,1024]{1,0:T(8,128)(2,1)S(1)} %get-tuple-element.41), channel_id=1, source_target_pairs={{0,8},{8,0},{16,24},{24,16},{1,9},{9,1},{17,25},{25,17},{2,10},{10... | collective-permute-start | bytes 491528 | tf_op jit(solution)/shard_map/exchange_generators/ppermute | solution.py:341
  12.4 1.2 %copy-start = (bf16[1024,512]{1,0:T(8,128)(2,1)S(1)}, bf16[1024,512]{1,0:T(8,128)(2,1)}, u32[]{:S(2)}) copy-start(bf16[1024,512]{1,0:T(8,128)(2,1)} %refs_1_.3) | copy-start | bytes 3145732
  13.7 14.6 %copy-start.4 = (f32[512]{0:T(512)S(1)}, f32[512]{0:T(512)}, u32[]{:S(2)}) copy-start(f32[512]{0:T(512)} %param.11) | copy-start | bytes 6148
  23.4 9.2 %collective-permute-start.4 = (f32[264,256]{1,0:T(8,128)S(1)}, f32[264,256]{1,0:T(8,128)S(1)}, u32[]{:S(2)}, u32[]{:S(2)}) collective-permute-start(f32[264,256]{1,0:T(8,128)S(1)} %get-tuple-element.43), channel_id=1, source_target_pairs={{0,24},{8,16},{16,8},{24,0},{1,25},{9,17},{17,9},{25,1},{2,26},{10... | collective-permute-start | bytes 811016 | tf_op jit(solution)/shard_map/sum_products/ppermute | solution.py:341
  25.6 21.5 %collective-permute-start.5 = (f32[264,256]{1,0:T(8,128)S(1)}, f32[264,256]{1,0:T(8,128)S(1)}, u32[]{:S(2)}, u32[]{:S(2)}) collective-permute-start(f32[264,256]{1,0:T(8,128)S(1)} %get-tuple-element.44), channel_id=1, source_target_pairs={{0,16},{8,24},{16,0},{24,8},{1,17},{9,25},{17,1},{25,9},{2,18},{10... | collective-permute-start | bytes 811016 | tf_op jit(solution)/shard_map/sum_products/ppermute | solution.py:341
  25.6 21.5 %collective-permute-start.6 = (f32[264,256]{1,0:T(8,128)S(1)}, f32[264,256]{1,0:T(8,128)S(1)}, u32[]{:S(2)}, u32[]{:S(2)}) collective-permute-start(f32[264,256]{1,0:T(8,128)S(1)} %get-tuple-element.45), channel_id=1, source_target_pairs={{0,8},{8,0},{16,24},{24,16},{1,9},{9,1},{17,25},{25,17},{2,10},{10... | collective-permute-start | bytes 811016 | tf_op jit(solution)/shard_map/sum_products/ppermute | solution.py:341
  27.0 40.1 %collective-permute-start.16 = (bf16[272,1024]{1,0:T(8,128)(2,1)S(1)}, bf16[272,1024]{1,0:T(8,128)(2,1)S(1)}, u32[]{:S(2)}, u32[]{:S(2)}) collective-permute-start(bf16[272,1024]{1,0:T(8,128)(2,1)S(1)} %get-tuple-element.58.refs_0_), channel_id=1, source_target_pairs={{0,1},{1,0},{2,3},{3,2},{4,5},{5,4},{6,7},{7,6},{8,9},{9,8},{10,11... | collective-permute-start | bytes 1671176 | tf_op jit(solution)/shard_map/share_generators/ppermute | solution.py:352
  28.3 2.8 %collective-permute-start.8 = (f32[8,512]{1,0:T(8,128)S(1)}, f32[8,512]{1,0:T(8,128)S(1)}, u32[]{:S(2)}, u32[]{:S(2)}) collective-permute-start(f32[8,512]{1,0:T(8,128)S(1)} %get-tuple-element.71), channel_id=1, source_target_pairs={{0,2},{2,0},{4,6},{6,4},{1,3},{3,1},{5,7},{7,5},{8,10},{10,8},{12,... | collective-permute-start | bytes 49160 | tf_op jit(solution)/shard_map/swap_cores/ppermute | solution.py:346
  31.1 1.3 %collective-permute-start.7 = (bf16[256,128]{1,0:T(8,128)(2,1)S(1)}, bf16[256,128]{1,0:T(8,128)(2,1)S(1)}, u32[]{:S(2)}, u32[]{:S(2)}) collective-permute-start(bf16[256,128]{1,0:T(8,128)(2,1)S(1)} %get-tuple-element.47), channel_id=1, source_target_pairs={{0,2},{2,0},{4,6},{6,4},{1,3},{3,1},{5,7},{7,5},{8,10},{10,8},{12,... | collective-permute-start | bytes 196616 | tf_op jit(solution)/shard_map/sum_products/ppermute | solution.py:346
  47.9 8.7 %collective-permute-start.10 = (bf16[336,256]{1,0:T(8,128)(2,1)S(1)}, bf16[336,256]{1,0:T(8,128)(2,1)S(1)}, u32[]{:S(2)}, u32[]{:S(2)}) collective-permute-start(bf16[336,256]{1,0:T(8,128)(2,1)S(1)} %get-tuple-element.51), channel_id=1, source_target_pairs={{0,16},{8,24},{16,0},{24,8},{1,17},{9,25},{17,1},{25,9},{2,18},{10... | collective-permute-start | bytes 516104 | tf_op jit(solution)/shard_map/exchange_back/ppermute | solution.py:341
  48.0 8.6 %collective-permute-start.11 = (bf16[336,256]{1,0:T(8,128)(2,1)S(1)}, bf16[336,256]{1,0:T(8,128)(2,1)S(1)}, u32[]{:S(2)}, u32[]{:S(2)}) collective-permute-start(bf16[336,256]{1,0:T(8,128)(2,1)S(1)} %get-tuple-element.52), channel_id=1, source_target_pairs={{0,8},{8,0},{16,24},{24,16},{1,9},{9,1},{17,25},{25,17},{2,10},{10... | collective-permute-start | bytes 516104 | tf_op jit(solution)/shard_map/exchange_back/ppermute | solution.py:341
  49.3 10.9 %collective-permute-start.9 = (bf16[336,256]{1,0:T(8,128)(2,1)S(1)}, bf16[336,256]{1,0:T(8,128)(2,1)S(1)}, u32[]{:S(2)}, u32[]{:S(2)}) collective-permute-start(bf16[336,256]{1,0:T(8,128)(2,1)S(1)} %get-tuple-element.50), channel_id=1, source_target_pairs={{0,24},{8,16},{16,8},{24,0},{1,25},{9,17},{17,9},{25,1},{2,26},{10... | collective-permute-start | bytes 516104 | tf_op jit(solution)/shard_map/exchange_back/ppermute | solution.py:341
  60.9 18.8 %collective-permute-start.19 = (bf16[272,1024]{1,0:T(8,128)(2,1)S(1)}, bf16[272,1024]{1,0:T(8,128)(2,1)S(1)}, u32[]{:S(2)}, u32[]{:S(2)}) collective-permute-start(bf16[272,1024]{1,0:T(8,128)(2,1)S(1)} %get-tuple-element.53.refs_0_), channel_id=1, source_target_pairs={{0,1},{1,0},{2,3},{3,2},{4,5},{5,4},{6,7},{7,6},{8,9},{9,8},{10,11... | collective-permute-start | bytes 1671176 | tf_op jit(solution)/shard_map/input_gradient/ppermute | solution.py:352
  63.6 4.7 %collective-permute-start.12 = (bf16[72,1024]{1,0:T(8,128)(2,1)S(1)}, bf16[72,1024]{1,0:T(8,128)(2,1)S(1)}, u32[]{:S(2)}, u32[]{:S(2)}) collective-permute-start(bf16[72,1024]{1,0:T(8,128)(2,1)S(1)} %get-tuple-element.55), channel_id=1, source_target_pairs={{0,4},{2,6},{4,0},{6,2},{1,5},{3,7},{5,1},{7,3},{8,12},{10,14},{12... | collective-permute-start | bytes 442376 | tf_op jit(solution)/shard_map/input_gradient/ppermute | solution.py:349
  63.9 21.7 %collective-permute-start.15 = (bf16[272,1024]{1,0:T(8,128)(2,1)S(1)}, bf16[272,1024]{1,0:T(8,128)(2,1)S(1)}, u32[]{:S(2)}, u32[]{:S(2)}) collective-permute-start(bf16[272,1024]{1,0:T(8,128)(2,1)S(1)} %get-tuple-element.58.refs_0_), channel_id=1, source_target_pairs={{0,2},{2,0},{4,6},{6,4},{1,3},{3,1},{5,7},{7,5},{8,10},{10,8},{12,... | collective-permute-start | bytes 1671176 | tf_op jit(solution)/shard_map/share_generators/ppermute | solution.py:346
  67.1 18.6 %collective-permute-start.17 = (bf16[272,1024]{1,0:T(8,128)(2,1)S(1)}, bf16[272,1024]{1,0:T(8,128)(2,1)S(1)}, u32[]{:S(2)}, u32[]{:S(2)}) collective-permute-start(bf16[272,1024]{1,0:T(8,128)(2,1)S(1)} %collective-permute-done.16.refs_2_), channel_id=1, source_target_pairs={{0,2},{2,0},{4,6},{6,4},{1,3},{3,1},{5,7},{7,5},{8,10},{10,8},{12,... | collective-permute-start | bytes 1671176 | tf_op jit(solution)/shard_map/share_generators/ppermute | solution.py:346
  67.1 9.3 %collective-permute-start.14 = (bf16[72,1024]{1,0:T(8,128)(2,1)S(1)}, bf16[72,1024]{1,0:T(8,128)(2,1)S(1)}, u32[]{:S(2)}, u32[]{:S(2)}) collective-permute-start(bf16[72,1024]{1,0:T(8,128)(2,1)S(1)} %get-tuple-element.57), channel_id=1, source_target_pairs={{0,4},{2,6},{4,0},{6,2},{1,5},{3,7},{5,1},{7,3},{8,12},{10,14},{12... | collective-permute-start | bytes 442376 | tf_op jit(solution)/shard_map/input_gradient/ppermute | solution.py:349
  68.9 10.3 %collective-permute-start.13 = (bf16[72,1024]{1,0:T(8,128)(2,1)S(1)}, bf16[72,1024]{1,0:T(8,128)(2,1)S(1)}, u32[]{:S(2)}, u32[]{:S(2)}) collective-permute-start(bf16[72,1024]{1,0:T(8,128)(2,1)S(1)} %input_gradient.6), channel_id=1, source_target_pairs={{0,0},{2,16},{4,8},{6,24},{8,2},{10,18},{12,10},{14,26},{16,4},{18... | collective-permute-start | bytes 442376 | tf_op jit(solution)/shard_map/input_gradient/ppermute | solution.py:360
  76.3 10.5 %collective-permute-start.18 = (bf16[336,512]{1,0:T(8,128)(2,1)S(1)}, bf16[336,512]{1,0:T(8,128)(2,1)S(1)}, u32[]{:S(2)}, u32[]{:S(2)}) collective-permute-start(bf16[336,512]{1,0:T(8,128)(2,1)S(1)} %get-tuple-element.59), channel_id=1, source_target_pairs={{0,2},{2,0},{4,6},{6,4},{1,3},{3,1},{5,7},{7,5},{8,10},{10,8},{12,... | collective-permute-start | bytes 1032200 | tf_op jit(solution)/shard_map/exchange_back/ppermute | solution.py:346
  80.3 6.5 %collective-permute-start.20 = (bf16[272,512]{1,0:T(8,128)(2,1)S(1)}, bf16[272,512]{1,0:T(8,128)(2,1)S(1)}, u32[]{:S(2)}, u32[]{:S(2)}) collective-permute-start(bf16[272,512]{1,0:T(8,128)(2,1)S(1)} %input_gradient.8), channel_id=1, source_target_pairs={{0,2},{2,0},{4,6},{6,4},{1,3},{3,1},{5,7},{7,5},{8,10},{10,8},{12,... | collective-permute-start | bytes 835592 | tf_op jit(solution)/shard_map/input_gradient/ppermute | solution.py:346
  83.9 8.2 %collective-permute-start.21 = (bf16[72,1024]{1,0:T(8,128)(2,1)S(1)}, bf16[72,1024]{1,0:T(8,128)(2,1)S(1)}, u32[]{:S(2)}, u32[]{:S(2)}) collective-permute-start(bf16[72,1024]{1,0:T(8,128)(2,1)S(1)} %input_gradient.7.refs_0_.after_ref), channel_id=1, source_target_pairs={{0,16},{2,0},{4,24},{6,8},{8,18},{10,2},{12,26},{14,10},{16,20},{1... | collective-permute-start | bytes 442376 | tf_op jit(solution)/shard_map/input_gradient/ppermute | solution.py:360

commit v5 on v4

--- a/solution.py
+++ b/solution.py
@@ -67,6 +67,7 @@
 CENTER_ROWS = 16
 HALVES = 1
 ORDER = (0, 3, 2, 1)
+COSTS = {"fold": 1000000, "copy": 1000000000, "forward": 1000000000, "relax": 1000000000}
 
 
 def params():
@@ -81,8 +82,9 @@
     return pl.BlockSpec(x.shape, lambda i, s, r=len(x.shape): (0,) * r)
 
 
-def call(kernel, scalars, args, specs, outs, scratch=(), after=(), cost=None):
+def call(kernel, scalars, args, specs, outs, scratch=(), after=()):
     skip = len(after)
+    cost = COSTS.get(getattr(kernel, "func", kernel).__name__.replace("_kernel", ""))
 
     def body(s_ref, *refs):
         kernel(s_ref, *refs[skip:])
@@ -98,7 +100,7 @@
         ),
         out_shape=outs,
         compiler_params=params(),
-        cost_estimate=cost and pl.CostEstimate(flops=cost[0], bytes_accessed=cost[1], transcendentals=0),
+        cost_estimate=pl.CostEstimate(flops=cost, bytes_accessed=1 << 20, transcendentals=0) if cost else None,
     )(scalars, *after, *args)
 
 
@@ -129,11 +131,18 @@
             out[rows:, i * lanes : (i + 1) * lanes] = value[i * per : (i + 1) * per]
 
 
+def chunk_kernel(s_ref, own_ref, oth_ref, out_ref):
+    lanes = out_ref.shape[2] // 2
+    for j in range(out_ref.shape[0]):
+        out_ref[j, :, :lanes] = own_ref[:, j * lanes : (j + 1) * lanes]
+        out_ref[j, :, lanes:] = oth_ref[:, j * lanes : (j + 1) * lanes]
+
+
 def copy_kernel(s_ref, in_ref, out_ref):
     out_ref[...] = in_ref[...]
 
 
-def forward_kernel(size, s_ref, center_ref, own_ref, oth_ref, *refs):
+def forward_kernel(size, s_ref, center_ref, w_ref, *refs):
     g, c = s_ref[0], s_ref[1]
     recv, (a_ref, keep_ref, send_ref), products = refs[:size], refs[size : size + 3], refs[size + 3 :]
     work, depth = a_ref.shape[0] // HALVES, a_ref.shape[1]
@@ -152,9 +161,7 @@
         a_ref[(h + 1) * work - CENTER_ROWS : (h + 1) * work, :] = tail
     a = a_ref[...]
     for i, k in enumerate(ORDER):
-        at = rows_at(g ^ k, lanes)
-        w = jnp.concatenate([own_ref[:, at], oth_ref[:, at]], 1)
-        product = jnp.dot(a, w, preferred_element_type=F32)
+        product = jnp.dot(a, w_ref[g ^ k], preferred_element_type=F32)
         for h in range(HALVES):
             out = products[h * size + i]
             out[...] = product[h * work : h * work + out.shape[0]]
@@ -218,37 +225,43 @@
 
 def spread_kernel(s_ref, back_ref, go_ref, *refs):
     g = s_ref[0]
-    msgs, (full_ref, oth_ref, out_ref) = refs[:-3], refs[-3:]
+    msgs, (own_ref, oth_ref, far_ref, out_ref) = refs[:3], refs[3:]
     rows, lanes = back_ref.shape[0], back_ref.shape[1] // 2
-    cols = oth_ref.shape[1]
     for i, k in enumerate(ORDER):
         at = rows_at(g ^ k, lanes)
-        right = pl.ds(pl.multiple_of(cols + (g ^ k) * lanes, lanes), lanes)
         back, out = (back_ref, go_ref[...]) if i == 0 else (msgs[i - 1], msgs[i - 1][rows:, :])
-        full_ref[:, at] = back[:rows, :lanes]
-        full_ref[:, right] = back[:rows, lanes:]
+        own_ref[:, at] = back[:rows, :lanes]
         oth_ref[:rows, at] = back[:rows, lanes:]
+        far_ref[:, at] = back[:rows, lanes:]
         oth_ref[rows:, at] = out[:, lanes:]
         out_ref[:, at] = out[:, :lanes]
 
 
-def input_grad_kernel(size, s_ref, full_ref, w_own_ref, w_oth_ref, *refs):
-    c, x = s_ref[1], s_ref[2] >> 1
-    outs, res = refs[:-1], refs[-1]
-    rows, cols = res.shape[0], w_own_ref.shape[1]
+def input_grad_kernel(s_ref, back_ref, *refs):
+    g, c, x = s_ref[0], s_ref[1], s_ref[2] >> 1
+    msgs, w_ref, outs, res = refs[:3], refs[3], refs[4:-1], refs[-1]
+    rows = back_ref.shape[0]
     over = (((1,), (1,)), ((), ()))
-    res[...] = lax.dot_general(
-        full_ref[:, :cols], w_own_ref[...], over, preferred_element_type=F32
-    ) + lax.dot_general(full_ref[:, cols:], w_oth_ref[...], over, preferred_element_type=F32)
-    group = (rows - CENTER_ROWS) // size
-    tail = res[size * group : size * group + 8, :]
-    for i, ref in enumerate(outs):
-        at = (1 - x if i < 2 else x) + 2 * (c ^ (i % 2))
-        ref[...] = jnp.concatenate([res[rows_at(at, group), :], tail], 0).astype(ref.dtype)
-
-
-def input_pair_kernel(s_ref, keep_ref, far_ref, out_ref):
-    out_ref[...] = (keep_ref[...] + far_ref[...].astype(F32)).astype(BF)
+    total = None
+    for i, k in enumerate(ORDER):
+        back = back_ref[...] if i == 0 else msgs[i - 1][:rows, :]
+        part = lax.dot_general(back, w_ref[g ^ k], over, preferred_element_type=F32)
+        total = part if total is None else total + part
+    res[...] = total
+    group = (rows - CENTER_ROWS) // 4
+    tail = res[4 * group : 4 * group + 8, :]
+    for side, out in ((1 - x, outs[0]), (x, outs[1])):
+        first = res[rows_at(side + 2 * c, group), :]
+        second = res[rows_at(side + 2 * (1 - c), group), :]
+        out[...] = jnp.concatenate([first, second, tail], 0).astype(out.dtype)
+
+
+def input_both_kernel(s_ref, keep_ref, far_ref, first_ref, last_ref):
+    group = (keep_ref.shape[0] - 8) // 2
+    total = keep_ref[...] + far_ref[...].astype(F32)
+    tail = total[2 * group :]
+    first_ref[...] = jnp.concatenate([total[:group], tail], 0).astype(BF)
+    last_ref[...] = jnp.concatenate([total[group : 2 * group], tail], 0).astype(BF)
 
 
 def input_final_kernel(boxes, s_ref, *refs):
@@ -351,6 +364,10 @@
     def over_box(x):
         return lax.ppermute(x, "box", [(0, 1), (1, 0)])
 
+    def over_both(x):
+        pairs = [(i * 2 + j, (i ^ 1) * 2 + (j ^ 1)) for i in range(size) for j in range(2)]
+        return lax.ppermute(x, ("neur", "box"), pairs)
+
     def turned(x, k):
         pairs = [
             (i * size + j, ((j >> 1) + 2 * ((j & 1) ^ k)) * size + i)
@@ -360,6 +377,11 @@
         return lax.ppermute(x, ("gen", "neur"), pairs)
 
     anywhere = pl.BlockSpec(memory_space=pl.ANY)
+    def held(x, *after):
+        if not after:
+            return x
+        return call(copy_kernel, scalars, [x], [whole(x)], [shape(x.shape, x.dtype)], after=after)[0]
+
     with jax.named_scope("exchange_generators"):
         cot_rows = box_dev * per_gen * lanes // depth
         msgs = call(
@@ -369,13 +391,17 @@
             [anywhere] * 2,
             [shape((core_boxes * per_gen + cot_rows, depth), BF)] * size,
             [pltpu.VMEM(gens_cot.shape, BF), pltpu.SemaphoreType.DMA((size * core_boxes + 1,))],
-            cost=(0, 32 << 20),
         )
         recv = over_gen(msgs)
     with jax.named_scope("swap_cores"):
         w_other = over_core(weight)
-        (w_near,) = call(
-            copy_kernel, scalars, [weight], [whole(weight)], [shape(weight.shape, BF)], after=[recv[1]]
+        (w_chunks,) = call(
+            chunk_kernel,
+            scalars,
+            [weight, w_other],
+            [whole(weight), whole(w_other)],
+            [shape((size, depth, 2 * lanes), BF)],
+            after=[recv[1]],
         )
         stacked = jnp.stack([phase.astype(F32), center_cot, offset_cot])
 
@@ -390,17 +416,15 @@
         a_own, cot_keep, cot_send, *products = call(
             functools.partial(forward_kernel, size),
             scalars,
-            [center, w_near, w_other, *recv],
+            [center, w_chunks, *recv],
             [
                 pl.BlockSpec((box_dev, depth), lambda i, s: (0, s[0])),
-                whole(w_near),
-                whole(w_other),
+                whole(w_chunks),
                 *[whole(r) for r in recv],
             ],
             [shape((HALVES * work, depth), BF)]
             + [shape((HALVES * rows, lanes), BF)] * 2
             + [shape((rows + 8, 2 * lanes), F32)] * (HALVES * size),
-            cost=(2 * HALVES * rows * depth * 2 * cols, 4 << 20),
         )
     with jax.named_scope("sum_products"):
         sums = []
@@ -436,60 +460,43 @@
             )
         with jax.named_scope("exchange_back"):
             got = over_gen([None, *msgs])[1:]
-            full, oth, out_own = call(
+            both = group + 8
+            part = group + both
+            send, keep = call(
+                input_grad_kernel,
+                scalars,
+                [back, *got, w_chunks],
+                [whole(v) for v in (back, *got, w_chunks)],
+                [shape((part, depth), BF), shape((part, depth), F32)],
+                [pltpu.VMEM((work, depth), F32)],
+            )
+            own, oth, oth_back, out_own = call(
                 spread_kernel,
                 scalars,
                 [back, go, *got],
-                [whole(back), whole(go), *[whole(r) for r in got]],
+                [whole(v) for v in (back, go, *got)],
                 [
-                    shape((work, 2 * cols), BF),
+                    shape((work, cols), BF),
                     shape((work + group, cols), BF),
+                    shape((work, cols), BF),
                     shape((group, cols), BF),
                 ],
+                after=[send],
             )
             core_part = over_core(oth)
             keeps.append(out_own)
-        with jax.named_scope("input_gradient"):
-            both = group + 8
-            sends.append(
-                call(
-                    functools.partial(input_grad_kernel, size),
-                    scalars,
-                    [full, w_near, w_other],
-                    [whole(full), whole(w_near), whole(w_other)],
-                    [shape((both, depth), BF)] * 2 + [shape((both, depth), F32)] * 2,
-                    [pltpu.VMEM((work, depth), F32)],
-                    cost=(2 * rows * depth * 2 * cols, 4 << 20),
-                )
-            )
     with jax.named_scope("input_gradient"):
-        (send_0, send_1, *keeps_f32), = sends
-        def pair(keep, far, *after):
-            (out,) = call(
-                input_pair_kernel,
-                scalars,
-                [keep, far],
-                [whole(keep), whole(far)],
-                [shape((group + 8, depth), BF)],
-                after=after,
-            )
-            return out
-
-        first = pair(keeps_f32[0], over_x(send_0))
-        full_box = over_box(full)
-        finals = [turned(first, 0)]
-        far_1 = over_x(send_1)
-        last = pair(keeps_f32[1], far_1, finals[0])
-        finals.append(turned(last, 1))
-        (box_oth,) = call(
-            copy_kernel,
+
+        far = over_x(send)
+        first, last = call(
+            input_both_kernel,
             scalars,
-            [full_box],
-            [pl.BlockSpec((work, cols), lambda i, s: (0, 1))],
-            [shape((work, cols), BF)],
-            after=[last],
-        )
-        rights = [full, core_part, full_box, over_core(box_oth)]
+            [keep, far],
+            [whole(keep), whole(far)],
+            [shape((both, depth), BF)] * 2,
+        )
+        finals = [turned(first, 0), turned(last, 1)]
+        rights = [own, core_part, over_box(own), held(over_both(oth_back), last)]
     with jax.named_scope("weight_gradient"):
         blocks = 4
         out_shape = [

time: 93.9 us -> 90.2 us (0.961)
  the two profiles are of different devices: /device:TPU:3 before, /device:TPU:1 now
where the time goes in v5:
time: 90.2 us; the launch traced here: 89.9 us
  starting transfers between devices  36.4 us (40%)
  waiting for transfers between devices  35.2 us (39%)
  Pallas kernels  13.6 us (15%)
  local copies, waits for them, and re-layouts  2.36 us (3%)
  other arithmetic  1.57 us (2%)
    ppermute x9, waiting for transfers between devices, over_gen(): lax.ppermute(piece, 'gen', [(i, i ^ k) for i in range(size)])  31.4 us
    ppermute x9, starting transfers between devices, over_gen(): lax.ppermute(piece, 'gen', [(i, i ^ k) for i in range(size)])  12.3 us
    ppermute x2, starting transfers between devices, turned(): return lax.ppermute(x, ('gen', 'neur'), pairs)  11.5 us
    pallas_call x10, Pallas kernels, call(): pl.pallas_call(body, grid_spec=pltpu.PrefetchScalarGridSpec(num_scalar_pr...  9.82 us
    ppermute x6, starting transfers between devices, over_core(): return lax.ppermute(x, 'neur', [(i, i ^ 1) for i in range(size)])  8.6 us
    pallas_call x1, Pallas kernels, square_body(): pl.pallas_call(functools.partial(weight_grad_kernel, boxes), grid_spec=pl...  3.78 us
    unnamed x10, local copies, waits for them, and re-layouts  2.25 us
    ppermute x2, waiting for transfers between devices, turned(): return lax.ppermute(x, ('gen', 'neur'), pairs)  2.03 us
  transfers between devices with their start and end apart: 21, of which 8 were waited for; matrix products, arithmetic and copies ran while one was open for 2% of the time, Pallas kernels for 12%

profile of v5, /device:TPU:1, one launch (start us, length us, event | category | flops | bytes accessed | tf_op | source)
XLA Modules:
  0.0 89.9 jit_solution(4861282947414767543)
XLA Ops:
  0.8 1.3 %copy-done.1 = bf16[4,32,4096]{2,1,0:T(8,128)(2,1)S(1)} copy-done((bf16[4,32,4096]{2,1,0:T(8,128)(2,1)S(1)}, bf16[4,32,4096]{2,1,0:T(8,128)(2,1)}, u32[]{:S(2)}) %copy-start.1) | copy-done | bytes 1048600
  2.2 0.9 %copy-done.2 = bf16[4,32,512]{2,1,0:T(8,128)(2,1)S(1)} copy-done((bf16[4,32,512]{2,1,0:T(8,128)(2,1)S(1)}, bf16[4,32,512]{2,1,0:T(8,128)(2,1)}, u32[]{:S(2)}) %copy-start.2) | copy-done | bytes 131096
  3.1 1.0 %exchange_generators.1 = (bf16[80,1024]{1,0:T(8,128)(2,1)S(1)}, bf16[80,1024]{1,0:T(8,128)(2,1)S(1)}, bf16[80,1024]{1,0:T(8,128)(2,1)S(1)}, bf16[80,1024]{1,0:T(8,128)(2,1)S(1)}) custom-call(s32[4]{0:T(128)S(1)} %pad_add_fusion.s_ref, bf16[4,32,4096]{2,1,0:T(8,128)(2,1)S(1)} %copy-done.1, bf16[4,32,512]{2,1,0:T(8,128)(2,1)S(1)} %copy-done.2), custom_call_target="tpu_custom_call" | custom-call | flops 1000000 | bytes 1048576 | tf_op jit(solution)/shard_map/exchange_generators/pallas_call | solution.py:92
  4.1 4.7 %collective-permute-start = (bf16[80,1024]{1,0:T(8,128)(2,1)S(1)}, bf16[80,1024]{1,0:T(8,128)(2,1)S(1)}, u32[]{:S(2)}, u32[]{:S(2)}) collective-permute-start(bf16[80,1024]{1,0:T(8,128)(2,1)S(1)} %get-tuple-element.39), channel_id=1, source_target_pairs={{0,24},{8,16},{16,8},{24,0},{1,25},{9,17},{17,9},{25,1},{2,26},{10... | collective-permute-start | bytes 491528 | tf_op jit(solution)/shard_map/exchange_generators/ppermute | solution.py:354
  9.2 0.7 convert_bitcast_fusion
  9.9 0.7 pad_maximum_fusion
  10.7 2.6 %collective-permute-done.refs_0_.refs_3_ = bf16[80,1024]{1,0:T(8,128)(2,1)S(1)} collective-permute-done((bf16[80,1024]{1,0:T(8,128)(2,1)S(1)}, bf16[80,1024]{1,0:T(8,128)(2,1)S(1)}, u32[]{:S(2)}, u32[]{:S(2)}) %collective-permute-start) | collective-permute-done | bytes 163872 | tf_op jit(solution)/shard_map/exchange_generators/ppermute | solution.py:354
  13.3 0.9 %swap_cores.1.refs_1_.refs_4_ = bf16[4,1024,256]{2,1,0:T(8,128)(2,1)S(1)} custom-call(s32[4]{0:T(128)S(1)} %pad_add_fusion.s_ref, bf16[80,1024]{1,0:T(8,128)(2,1)S(1)} %collective-permute-done.refs_0_.refs_3_, bf16[1024,512]{1,0:T(8,128)(2,1)S(1)} %copy-done, bf16[1024,512]{1,0:T(8,128)(2,1)S(1)} %collective-permute-done.1.refs_2_), custom_call_target="tpu_custom_call" | custom-call | tf_op jit(solution)/shard_map/swap_cores/pallas_call | solution.py:92
  14.2 8.5 %collective-permute-done.2.refs_4_ = bf16[80,1024]{1,0:T(8,128)(2,1)S(1)} collective-permute-done((bf16[80,1024]{1,0:T(8,128)(2,1)S(1)}, bf16[80,1024]{1,0:T(8,128)(2,1)S(1)}, u32[]{:S(2)}, u32[]{:S(2)}) %collective-permute-start.2) | collective-permute-done | bytes 163872 | tf_op jit(solution)/shard_map/exchange_generators/ppermute | solution.py:354
  22.7 1.3 %forward.1 = (bf16[272,1024]{1,0:T(8,128)(2,1)S(1)}, bf16[256,128]{1,0:T(8,128)(2,1)S(1)}, bf16[256,128]{1,0:T(8,128)(2,1)S(1)}, f32[264,256]{1,0:T(8,128)S(1)},...) custom-call(s32[4]{0:T(128)S(1)} %pad_add_fusion.s_ref, bf16[4,4096]{1,0:T(4,128)(2,1)S(1)} %copy-done.3, ...), custom_call_target="tpu_custom_call" | custom-call | flops 1000000000 | bytes 1048576 | tf_op jit(solution)/shard_map/forward/pallas_call | solution.py:92
  24.0 2.3 %collective-permute-start.4 = (f32[264,256]{1,0:T(8,128)S(1)}, f32[264,256]{1,0:T(8,128)S(1)}, u32[]{:S(2)}, u32[]{:S(2)}) collective-permute-start(f32[264,256]{1,0:T(8,128)S(1)} %get-tuple-element.44), channel_id=1, source_target_pairs={{0,24},{8,16},{16,8},{24,0},{1,25},{9,17},{17,9},{25,1},{2,26},{10... | collective-permute-start | bytes 811016 | tf_op jit(solution)/shard_map/sum_products/ppermute | solution.py:354
  26.3 1.4 %collective-permute-start.6 = (f32[264,256]{1,0:T(8,128)S(1)}, f32[264,256]{1,0:T(8,128)S(1)}, u32[]{:S(2)}, u32[]{:S(2)}) collective-permute-start(f32[264,256]{1,0:T(8,128)S(1)} %get-tuple-element.46), channel_id=1, source_target_pairs={{0,8},{8,0},{16,24},{24,16},{1,9},{9,1},{17,25},{25,17},{2,10},{10... | collective-permute-start | bytes 811016 | tf_op jit(solution)/shard_map/sum_products/ppermute | solution.py:354
  27.6 1.2 %collective-permute-start.14 = (bf16[272,1024]{1,0:T(8,128)(2,1)S(1)}, bf16[272,1024]{1,0:T(8,128)(2,1)S(1)}, u32[]{:S(2)}, u32[]{:S(2)}) collective-permute-start(bf16[272,1024]{1,0:T(8,128)(2,1)S(1)} %get-tuple-element.56.refs_0_), channel_id=1, source_target_pairs={{0,1},{1,0},{2,3},{3,2},{4,5},{5,4},{6,7},{7,6},{8,9},{9,8},{10,11... | collective-permute-start | bytes 1671176 | tf_op jit(solution)/shard_map/share_generators/ppermute | solution.py:365
  29.0 2.1 %collective-permute-start.8 = (f32[8,512]{1,0:T(8,128)S(1)}, f32[8,512]{1,0:T(8,128)S(1)}, u32[]{:S(2)}, u32[]{:S(2)}) collective-permute-start(f32[8,512]{1,0:T(8,128)S(1)} %get-tuple-element.73), channel_id=1, source_target_pairs={{0,2},{2,0},{4,6},{6,4},{1,3},{3,1},{5,7},{7,5},{8,10},{10,8},{12,... | collective-permute-start | bytes 49160 | tf_op jit(solution)/shard_map/swap_cores/ppermute | solution.py:359
  31.0 0.8 collective-permute-done.8.refs_7_
  32.2 0.9 %collective-permute-done.7.refs_5_ = bf16[256,128]{1,0:T(8,128)(2,1)S(1)} collective-permute-done((bf16[256,128]{1,0:T(8,128)(2,1)S(1)}, bf16[256,128]{1,0:T(8,128)(2,1)S(1)}, u32[]{:S(2)}, u32[]{:S(2)}) %collective-permute-start.7) | collective-permute-done | bytes 65568 | tf_op jit(solution)/shard_map/sum_products/ppermute | solution.py:359
  33.1 14.5 %collective-permute-done.5.refs_2_ = f32[264,256]{1,0:T(8,128)S(1)} collective-permute-done((f32[264,256]{1,0:T(8,128)S(1)}, f32[264,256]{1,0:T(8,128)S(1)}, u32[]{:S(2)}, u32[]{:S(2)}) %collective-permute-start.5) | collective-permute-done | bytes 270368 | tf_op jit(solution)/shard_map/sum_products/ppermute | solution.py:354
  47.6 0.8 relax.1
  48.5 1.3 %collective-permute-start.11 = (bf16[336,256]{1,0:T(8,128)(2,1)S(1)}, bf16[336,256]{1,0:T(8,128)(2,1)S(1)}, u32[]{:S(2)}, u32[]{:S(2)}) collective-permute-start(bf16[336,256]{1,0:T(8,128)(2,1)S(1)} %get-tuple-element.52), channel_id=1, source_target_pairs={{0,8},{8,0},{16,24},{24,16},{1,9},{9,1},{17,25},{25,17},{2,10},{10... | collective-permute-start | bytes 516104 | tf_op jit(solution)/shard_map/exchange_back/ppermute | solution.py:354
  49.8 2.2 %collective-permute-start.9 = (bf16[336,256]{1,0:T(8,128)(2,1)S(1)}, bf16[336,256]{1,0:T(8,128)(2,1)S(1)}, u32[]{:S(2)}, u32[]{:S(2)}) collective-permute-start(bf16[336,256]{1,0:T(8,128)(2,1)S(1)} %get-tuple-element.50), channel_id=1, source_target_pairs={{0,24},{8,16},{16,8},{24,0},{1,25},{9,17},{17,9},{25,1},{2,26},{10... | collective-permute-start | bytes 516104 | tf_op jit(solution)/shard_map/exchange_back/ppermute | solution.py:354
  52.1 2.7 %collective-permute-start.13 = (bf16[272,1024]{1,0:T(8,128)(2,1)S(1)}, bf16[272,1024]{1,0:T(8,128)(2,1)S(1)}, u32[]{:S(2)}, u32[]{:S(2)}) collective-permute-start(bf16[272,1024]{1,0:T(8,128)(2,1)S(1)} %get-tuple-element.56.refs_0_), channel_id=1, source_target_pairs={{0,2},{2,0},{4,6},{6,4},{1,3},{3,1},{5,7},{7,5},{8,10},{10,8},{12,... | collective-permute-start | bytes 1671176 | tf_op jit(solution)/shard_map/share_generators/ppermute | solution.py:359
  54.8 2.9 %collective-permute-done.10.refs_2_.refs_4_ = bf16[336,256]{1,0:T(8,128)(2,1)S(1)} collective-permute-done((bf16[336,256]{1,0:T(8,128)(2,1)S(1)}, bf16[336,256]{1,0:T(8,128)(2,1)S(1)}, u32[]{:S(2)}, u32[]{:S(2)}) %collective-permute-start.10) | collective-permute-done | bytes 172064 | tf_op jit(solution)/shard_map/exchange_back/ppermute | solution.py:354
  57.6 3.0 %collective-permute-done.9.refs_1_.refs_3_ = bf16[336,256]{1,0:T(8,128)(2,1)S(1)} collective-permute-done((bf16[336,256]{1,0:T(8,128)(2,1)S(1)}, bf16[336,256]{1,0:T(8,128)(2,1)S(1)}, u32[]{:S(2)}, u32[]{:S(2)}) %collective-permute-start.9) | collective-permute-done | bytes 172064 | tf_op jit(solution)/shard_map/exchange_back/ppermute | solution.py:354
  60.6 1.4 %exchange_back.2 = (bf16[136,1024]{1,0:T(8,128)(2,1)S(1)}, f32[136,1024]{1,0:T(8,128)S(1)}) custom-call(s32[4]{0:T(128)S(1)} %pad_add_fusion.s_ref, bf16[272,256]{1,0:T(8,128)(2,1)S(1)} %get-tuple-element.49.refs_0_.refs_1_, bf16[336,256]{1,0:T(8,128)(2,1)S(1)} %collective-permute-done.9.refs_1_.refs_3_, ...), custom_call_target="tpu_custom_call" | custom-call | tf_op jit(solution)/shard_map/exchange_back/pallas_call | solution.py:92
  62.0 1.3 %collective-permute-start.12 = (bf16[136,1024]{1,0:T(8,128)(2,1)S(1)}, bf16[136,1024]{1,0:T(8,128)(2,1)S(1)}, u32[]{:S(2)}, u32[]{:S(2)}) collective-permute-start(bf16[136,1024]{1,0:T(8,128)(2,1)S(1)} %get-tuple-element.54.refs_0_), channel_id=1, source_target_pairs={{0,4},{2,6},{4,0},{6,2},{1,5},{3,7},{5,1},{7,3},{8,12},{10,14},{12... | collective-permute-start | bytes 835592 | tf_op jit(solution)/shard_map/input_gradient/ppermute | solution.py:362
  63.2 2.8 %collective-permute-start.15 = (bf16[272,1024]{1,0:T(8,128)(2,1)S(1)}, bf16[272,1024]{1,0:T(8,128)(2,1)S(1)}, u32[]{:S(2)}, u32[]{:S(2)}) collective-permute-start(bf16[272,1024]{1,0:T(8,128)(2,1)S(1)} %collective-permute-done.14.refs_2_), channel_id=1, source_target_pairs={{0,2},{2,0},{4,6},{6,4},{1,3},{3,1},{5,7},{7,5},{8,10},{10,8},{12,... | collective-permute-start | bytes 1671176 | tf_op jit(solution)/shard_map/share_generators/ppermute | solution.py:359
  66.8 1.2 %collective-permute-start.18 = (bf16[272,512]{1,0:T(8,128)(2,1)S(1)}, bf16[272,512]{1,0:T(8,128)(2,1)S(1)}, u32[]{:S(2)}, u32[]{:S(2)}) collective-permute-start(bf16[272,512]{1,0:T(8,128)(2,1)S(1)} %get-tuple-element.60), channel_id=1, source_target_pairs={{0,3},{1,2},{2,1},{3,0},{4,7},{5,6},{6,5},{7,4},{8,11},{9,10},{10,... | collective-permute-start | bytes 835592 | tf_op jit(solution)/shard_map/input_gradient/ppermute | solution.py:369
  69.3 11.5 %collective-permute-start.19 = (bf16[72,1024]{1,0:T(8,128)(2,1)S(1)}, bf16[72,1024]{1,0:T(8,128)(2,1)S(1)}, u32[]{:S(2)}, u32[]{:S(2)}) collective-permute-start(bf16[72,1024]{1,0:T(8,128)(2,1)S(1)} %get-tuple-element.68), channel_id=1, source_target_pairs={{0,0},{2,16},{4,8},{6,24},{8,2},{10,18},{12,10},{14,26},{16,4},{18... | collective-permute-start | bytes 442376 | tf_op jit(solution)/shard_map/input_gradient/ppermute | solution.py:377
  81.5 1.2 %share_generators.1.left_ref = bf16[1024,1152]{1,0:T(8,128)(2,1)S(1)} custom-call(s32[4]{0:T(128)S(1)} %pad_add_fusion.s_ref, bf16[272,1024]{1,0:T(8,128)(2,1)S(1)} %get-tuple-element.56.refs_0_, bf16[272,1024]{1,0:T(8,128)(2,1)S(1)} %collective-permute-done.13.refs_1_, bf16[272,1024]{1,0:T(8,128)(2,1)S(1)} %collective-permute-done.14.refs_2_, ...), custom_call_target="tpu_custom_call" | custom-call | tf_op jit(solution)/shard_map/share_generators/pallas_call | solution.py:92
  82.7 3.8 %weight_gradient.1 = (f32[1024,512]{1,0:T(8,128)}, f32[1,512]{1,0:T(1,128)}, f32[4,512]{1,0:T(4,128)}, f32[4,512]{1,0:T(4,128)}, bf16[4,32,512]{2,1,0:T(8,128)(2,1)}, /*index=5*/f32[8,128]{1,0:T(8,128)S(1)}) custom-call(s32[4]{0:T(128)S(1)} %pad_add_fusion.s_ref, bf16[72,1024]{1,0:T(8,128)(2,1)S(1)} %get-tuple-element.55.refs_0_.after_ref, ...), custom_call_target="tpu_custom_call" | custom-call | tf_op jit(solution)/shard_map/weight_gradient/pallas_call | solution.py:510
  86.5 2.0 %collective-permute-done.20.refs_2_ = bf16[72,1024]{1,0:T(8,128)(2,1)S(1)} collective-permute-done((bf16[72,1024]{1,0:T(8,128)(2,1)S(1)}, bf16[72,1024]{1,0:T(8,128)(2,1)S(1)}, u32[]{:S(2)}, u32[]{:S(2)}) %collective-permute-start.20) | collective-permute-done | bytes 147488 | tf_op jit(solution)/shard_map/input_gradient/ppermute | solution.py:377
  88.5 1.4 %input_gradient.5 = (f32[4,32,1024]{2,1,0:T(8,128)}, f32[4,1024]{1,0:T(4,128)}) custom-call(s32[4]{0:T(128)S(1)} %pad_add_fusion.s_ref, f32[8,128]{1,0:T(8,128)S(1)} %get-tuple-element.67.refs_0_, bf16[72,1024]{1,0:T(8,128)(2,1)S(1)} %collective-permute-done.19.refs_1_, bf16[72,1024]{1,0:T(8,128)(2,1)S(1)} %collective-permute-done.20.refs_2_), custom_call_target="tpu_custom_call" | custom-call | tf_op jit(solution)/shard_map/input_gradient/pallas_call | solution.py:92
  (39 shorter events, 3.9 us)
Async XLA Ops:
  0.6 12.7 %copy-start = (bf16[1024,512]{1,0:T(8,128)(2,1)S(1)}, bf16[1024,512]{1,0:T(8,128)(2,1)}, u32[]{:S(2)}) copy-start(bf16[1024,512]{1,0:T(8,128)(2,1)} %refs_1_.3) | copy-start | bytes 3145732
  0.6 12.7 %collective-permute-start.1 = (bf16[1024,512]{1,0:T(8,128)(2,1)}, bf16[1024,512]{1,0:T(8,128)(2,1)S(1)}, u32[]{:S(2)}, u32[]{:S(2)}) collective-permute-start(bf16[1024,512]{1,0:T(8,128)(2,1)} %refs_1_.3), channel_id=1, source_target_pairs={{0,2},{2,0},{4,6},{6,4},{1,3},{3,1},{5,7},{7,5},{8,10},{10,8},{12,... | collective-permute-start | bytes 3145736 | tf_op jit(solution)/shard_map/swap_cores/ppermute | solution.py:359
  0.8 1.3 %copy-start.1 = (bf16[4,32,4096]{2,1,0:T(8,128)(2,1)S(1)}, bf16[4,32,4096]{2,1,0:T(8,128)(2,1)}, u32[]{:S(2)}) copy-start(bf16[4,32,4096]{2,1,0:T(8,128)(2,1)} %refs_0_.2) | copy-start | bytes 3145732
  2.2 0.9 %copy-start.2 = (bf16[4,32,512]{2,1,0:T(8,128)(2,1)S(1)}, bf16[4,32,512]{2,1,0:T(8,128)(2,1)}, u32[]{:S(2)}) copy-start(bf16[4,32,512]{2,1,0:T(8,128)(2,1)} %refs_1_.2) | copy-start | bytes 393220
  4.1 9.2 %collective-permute-start = (bf16[80,1024]{1,0:T(8,128)(2,1)S(1)}, bf16[80,1024]{1,0:T(8,128)(2,1)S(1)}, u32[]{:S(2)}, u32[]{:S(2)}) collective-permute-start(bf16[80,1024]{1,0:T(8,128)(2,1)S(1)} %get-tuple-element.39), channel_id=1, source_target_pairs={{0,24},{8,16},{16,8},{24,0},{1,25},{9,17},{17,9},{25,1},{2,26},{10... | collective-permute-start | bytes 491528 | tf_op jit(solution)/shard_map/exchange_generators/ppermute | solution.py:354
  8.8 13.9 %collective-permute-start.2 = (bf16[80,1024]{1,0:T(8,128)(2,1)S(1)}, bf16[80,1024]{1,0:T(8,128)(2,1)S(1)}, u32[]{:S(2)}, u32[]{:S(2)}) collective-permute-start(bf16[80,1024]{1,0:T(8,128)(2,1)S(1)} %get-tuple-element.41), channel_id=1, source_target_pairs={{0,16},{8,24},{16,0},{24,8},{1,17},{9,25},{17,1},{25,9},{2,18},{10... | collective-permute-start | bytes 491528 | tf_op jit(solution)/shard_map/exchange_generators/ppermute | solution.py:354
  8.8 13.9 %collective-permute-start.3 = (bf16[80,1024]{1,0:T(8,128)(2,1)S(1)}, bf16[80,1024]{1,0:T(8,128)(2,1)S(1)}, u32[]{:S(2)}, u32[]{:S(2)}) collective-permute-start(bf16[80,1024]{1,0:T(8,128)(2,1)S(1)} %get-tuple-element.42), channel_id=1, source_target_pairs={{0,8},{8,0},{16,24},{24,16},{1,9},{9,1},{17,25},{25,17},{2,10},{10... | collective-permute-start | bytes 491528 | tf_op jit(solution)/shard_map/exchange_generators/ppermute | solution.py:354
  10.7 12.0 %copy-start.3 = (bf16[4,4096]{1,0:T(4,128)(2,1)S(1)}, bf16[4,4096]{1,0:T(4,128)(2,1)}, u32[]{:S(2)}) copy-start(bf16[4,4096]{1,0:T(4,128)(2,1)} %refs_0_.3) | copy-start | bytes 98308
  14.2 14.7 %copy-start.4 = (f32[512]{0:T(512)S(1)}, f32[512]{0:T(512)}, u32[]{:S(2)}) copy-start(f32[512]{0:T(512)} %param.11) | copy-start | bytes 6148
  24.0 9.1 %collective-permute-start.4 = (f32[264,256]{1,0:T(8,128)S(1)}, f32[264,256]{1,0:T(8,128)S(1)}, u32[]{:S(2)}, u32[]{:S(2)}) collective-permute-start(f32[264,256]{1,0:T(8,128)S(1)} %get-tuple-element.44), channel_id=1, source_target_pairs={{0,24},{8,16},{16,8},{24,0},{1,25},{9,17},{17,9},{25,1},{2,26},{10... | collective-permute-start | bytes 811016 | tf_op jit(solution)/shard_map/sum_products/ppermute | solution.py:354
  26.3 21.3 %collective-permute-start.5 = (f32[264,256]{1,0:T(8,128)S(1)}, f32[264,256]{1,0:T(8,128)S(1)}, u32[]{:S(2)}, u32[]{:S(2)}) collective-permute-start(f32[264,256]{1,0:T(8,128)S(1)} %get-tuple-element.45), channel_id=1, source_target_pairs={{0,16},{8,24},{16,0},{24,8},{1,17},{9,25},{17,1},{25,9},{2,18},{10... | collective-permute-start | bytes 811016 | tf_op jit(solution)/shard_map/sum_products/ppermute | solution.py:354
  26.3 21.3 %collective-permute-start.6 = (f32[264,256]{1,0:T(8,128)S(1)}, f32[264,256]{1,0:T(8,128)S(1)}, u32[]{:S(2)}, u32[]{:S(2)}) collective-permute-start(f32[264,256]{1,0:T(8,128)S(1)} %get-tuple-element.46), channel_id=1, source_target_pairs={{0,8},{8,0},{16,24},{24,16},{1,9},{9,1},{17,25},{25,17},{2,10},{10... | collective-permute-start | bytes 811016 | tf_op jit(solution)/shard_map/sum_products/ppermute | solution.py:354
  27.6 35.6 %collective-permute-start.14 = (bf16[272,1024]{1,0:T(8,128)(2,1)S(1)}, bf16[272,1024]{1,0:T(8,128)(2,1)S(1)}, u32[]{:S(2)}, u32[]{:S(2)}) collective-permute-start(bf16[272,1024]{1,0:T(8,128)(2,1)S(1)} %get-tuple-element.56.refs_0_), channel_id=1, source_target_pairs={{0,1},{1,0},{2,3},{3,2},{4,5},{5,4},{6,7},{7,6},{8,9},{9,8},{10,11... | collective-permute-start | bytes 1671176 | tf_op jit(solution)/shard_map/share_generators/ppermute | solution.py:365
  29.0 2.9 %collective-permute-start.8 = (f32[8,512]{1,0:T(8,128)S(1)}, f32[8,512]{1,0:T(8,128)S(1)}, u32[]{:S(2)}, u32[]{:S(2)}) collective-permute-start(f32[8,512]{1,0:T(8,128)S(1)} %get-tuple-element.73), channel_id=1, source_target_pairs={{0,2},{2,0},{4,6},{6,4},{1,3},{3,1},{5,7},{7,5},{8,10},{10,8},{12,... | collective-permute-start | bytes 49160 | tf_op jit(solution)/shard_map/swap_cores/ppermute | solution.py:359
  31.9 1.3 %collective-permute-start.7 = (bf16[256,128]{1,0:T(8,128)(2,1)S(1)}, bf16[256,128]{1,0:T(8,128)(2,1)S(1)}, u32[]{:S(2)}, u32[]{:S(2)}) collective-permute-start(bf16[256,128]{1,0:T(8,128)(2,1)S(1)} %get-tuple-element.48), channel_id=1, source_target_pairs={{0,2},{2,0},{4,6},{6,4},{1,3},{3,1},{5,7},{7,5},{8,10},{10,8},{12,... | collective-permute-start | bytes 196616 | tf_op jit(solution)/shard_map/sum_products/ppermute | solution.py:359
  48.4 9.2 %collective-permute-start.10 = (bf16[336,256]{1,0:T(8,128)(2,1)S(1)}, bf16[336,256]{1,0:T(8,128)(2,1)S(1)}, u32[]{:S(2)}, u32[]{:S(2)}) collective-permute-start(bf16[336,256]{1,0:T(8,128)(2,1)S(1)} %get-tuple-element.51), channel_id=1, source_target_pairs={{0,16},{8,24},{16,0},{24,8},{1,17},{9,25},{17,1},{25,9},{2,18},{10... | collective-permute-start | bytes 516104 | tf_op jit(solution)/shard_map/exchange_back/ppermute | solution.py:354
  48.5 9.1 %collective-permute-start.11 = (bf16[336,256]{1,0:T(8,128)(2,1)S(1)}, bf16[336,256]{1,0:T(8,128)(2,1)S(1)}, u32[]{:S(2)}, u32[]{:S(2)}) collective-permute-start(bf16[336,256]{1,0:T(8,128)(2,1)S(1)} %get-tuple-element.52), channel_id=1, source_target_pairs={{0,8},{8,0},{16,24},{24,16},{1,9},{9,1},{17,25},{25,17},{2,10},{10... | collective-permute-start | bytes 516104 | tf_op jit(solution)/shard_map/exchange_back/ppermute | solution.py:354
  49.8 10.8 %collective-permute-start.9 = (bf16[336,256]{1,0:T(8,128)(2,1)S(1)}, bf16[336,256]{1,0:T(8,128)(2,1)S(1)}, u32[]{:S(2)}, u32[]{:S(2)}) collective-permute-start(bf16[336,256]{1,0:T(8,128)(2,1)S(1)} %get-tuple-element.50), channel_id=1, source_target_pairs={{0,24},{8,16},{16,8},{24,0},{1,25},{9,17},{17,9},{25,1},{2,26},{10... | collective-permute-start | bytes 516104 | tf_op jit(solution)/shard_map/exchange_back/ppermute | solution.py:354
  52.1 17.3 %collective-permute-start.13 = (bf16[272,1024]{1,0:T(8,128)(2,1)S(1)}, bf16[272,1024]{1,0:T(8,128)(2,1)S(1)}, u32[]{:S(2)}, u32[]{:S(2)}) collective-permute-start(bf16[272,1024]{1,0:T(8,128)(2,1)S(1)} %get-tuple-element.56.refs_0_), channel_id=1, source_target_pairs={{0,2},{2,0},{4,6},{6,4},{1,3},{3,1},{5,7},{7,5},{8,10},{10,8},{12,... | collective-permute-start | bytes 1671176 | tf_op jit(solution)/shard_map/share_generators/ppermute | solution.py:359
  62.0 6.5 %collective-permute-start.12 = (bf16[136,1024]{1,0:T(8,128)(2,1)S(1)}, bf16[136,1024]{1,0:T(8,128)(2,1)S(1)}, u32[]{:S(2)}, u32[]{:S(2)}) collective-permute-start(bf16[136,1024]{1,0:T(8,128)(2,1)S(1)} %get-tuple-element.54.refs_0_), channel_id=1, source_target_pairs={{0,4},{2,6},{4,0},{6,2},{1,5},{3,7},{5,1},{7,3},{8,12},{10,14},{12... | collective-permute-start | bytes 835592 | tf_op jit(solution)/shard_map/input_gradient/ppermute | solution.py:362
  63.2 18.2 %collective-permute-start.15 = (bf16[272,1024]{1,0:T(8,128)(2,1)S(1)}, bf16[272,1024]{1,0:T(8,128)(2,1)S(1)}, u32[]{:S(2)}, u32[]{:S(2)}) collective-permute-start(bf16[272,1024]{1,0:T(8,128)(2,1)S(1)} %collective-permute-done.14.refs_2_), channel_id=1, source_target_pairs={{0,2},{2,0},{4,6},{6,4},{1,3},{3,1},{5,7},{7,5},{8,10},{10,8},{12,... | collective-permute-start | bytes 1671176 | tf_op jit(solution)/shard_map/share_generators/ppermute | solution.py:359
  66.8 14.0 %collective-permute-start.18 = (bf16[272,512]{1,0:T(8,128)(2,1)S(1)}, bf16[272,512]{1,0:T(8,128)(2,1)S(1)}, u32[]{:S(2)}, u32[]{:S(2)}) collective-permute-start(bf16[272,512]{1,0:T(8,128)(2,1)S(1)} %get-tuple-element.60), channel_id=1, source_target_pairs={{0,3},{1,2},{2,1},{3,0},{4,7},{5,6},{6,5},{7,4},{8,11},{9,10},{10,... | collective-permute-start | bytes 835592 | tf_op jit(solution)/shard_map/input_gradient/ppermute | solution.py:369
  68.0 14.7 %collective-permute-start.16 = (bf16[336,512]{1,0:T(8,128)(2,1)S(1)}, bf16[336,512]{1,0:T(8,128)(2,1)S(1)}, u32[]{:S(2)}, u32[]{:S(2)}) collective-permute-start(bf16[336,512]{1,0:T(8,128)(2,1)S(1)} %get-tuple-element.59), channel_id=1, source_target_pairs={{0,2},{2,0},{4,6},{6,4},{1,3},{3,1},{5,7},{7,5},{8,10},{10,8},{12,... | collective-permute-start | bytes 1032200 | tf_op jit(solution)/shard_map/exchange_back/ppermute | solution.py:359
  68.5 14.2 %collective-permute-start.17 = (bf16[272,512]{1,0:T(8,128)(2,1)S(1)}, bf16[272,512]{1,0:T(8,128)(2,1)S(1)}, u32[]{:S(2)}, u32[]{:S(2)}) collective-permute-start(bf16[272,512]{1,0:T(8,128)(2,1)S(1)} %get-tuple-element.58.refs_0_), channel_id=1, source_target_pairs={{0,1},{1,0},{2,3},{3,2},{4,5},{5,4},{6,7},{7,6},{8,9},{9,8},{10,11... | collective-permute-start | bytes 835592 | tf_op jit(solution)/shard_map/input_gradient/ppermute | solution.py:365
  69.3 17.2 %collective-permute-start.19 = (bf16[72,1024]{1,0:T(8,128)(2,1)S(1)}, bf16[72,1024]{1,0:T(8,128)(2,1)S(1)}, u32[]{:S(2)}, u32[]{:S(2)}) collective-permute-start(bf16[72,1024]{1,0:T(8,128)(2,1)S(1)} %get-tuple-element.68), channel_id=1, source_target_pairs={{0,0},{2,16},{4,8},{6,24},{8,2},{10,18},{12,10},{14,26},{16,4},{18... | collective-permute-start | bytes 442376 | tf_op jit(solution)/shard_map/input_gradient/ppermute | solution.py:377
  80.8 7.7 %collective-permute-start.20 = (bf16[72,1024]{1,0:T(8,128)(2,1)S(1)}, bf16[72,1024]{1,0:T(8,128)(2,1)S(1)}, u32[]{:S(2)}, u32[]{:S(2)}) collective-permute-start(bf16[72,1024]{1,0:T(8,128)(2,1)S(1)} %get-tuple-element.55.refs_0_.after_ref), channel_id=1, source_target_pairs={{0,16},{2,0},{4,24},{6,8},{8,18},{10,2},{12,26},{14,10},{16,20},{1... | collective-permute-start | bytes 442376 | tf_op jit(solution)/shard_map/input_gradient/ppermute | solution.py:377

commit v6 on v5

--- a/solution.py
+++ b/solution.py
@@ -67,7 +67,8 @@
 CENTER_ROWS = 16
 HALVES = 1
 ORDER = (0, 3, 2, 1)
-COSTS = {"fold": 1000000, "copy": 1000000000, "forward": 1000000000, "relax": 1000000000}
+BACK_ORDER = (0, 2, 3, 1)
+COSTS = {"fold": 1000000, "copy": 1000000000, "forward": 1000000000, "relax": 1000000000, "input_both": 300000000}
 
 
 def params():
@@ -218,7 +219,7 @@
     tail.append(jnp.zeros((CENTER_ROWS - 6 * boxes, value.shape[1]), F32))
     back_ref[rows:, :] = jnp.concatenate(tail, 0).astype(BF)
     go_ref[...] = out_scratch[rows_at(g, group), :]
-    for k, msg in zip(ORDER[1:], msgs):
+    for k, msg in zip(BACK_ORDER[1:], msgs):
         msg[: rows + CENTER_ROWS, :] = back_ref[...]
         msg[rows + CENTER_ROWS :, :] = out_scratch[rows_at(g ^ k, group), :]
 
@@ -227,7 +228,7 @@
     g = s_ref[0]
     msgs, (own_ref, oth_ref, far_ref, out_ref) = refs[:3], refs[3:]
     rows, lanes = back_ref.shape[0], back_ref.shape[1] // 2
-    for i, k in enumerate(ORDER):
+    for i, k in enumerate(BACK_ORDER):
         at = rows_at(g ^ k, lanes)
         back, out = (back_ref, go_ref[...]) if i == 0 else (msgs[i - 1], msgs[i - 1][rows:, :])
         own_ref[:, at] = back[:rows, :lanes]
@@ -243,7 +244,7 @@
     rows = back_ref.shape[0]
     over = (((1,), (1,)), ((), ()))
     total = None
-    for i, k in enumerate(ORDER):
+    for i, k in enumerate(BACK_ORDER):
         back = back_ref[...] if i == 0 else msgs[i - 1][:rows, :]
         part = lax.dot_general(back, w_ref[g ^ k], over, preferred_element_type=F32)
         total = part if total is None else total + part
@@ -349,10 +350,10 @@
     scalars = jnp.stack([g, c, n, lax.axis_index("box")]).astype(jnp.int32)
     halves = range(HALVES)
 
-    def over_gen(pieces):
+    def over_gen(pieces, order=ORDER):
         return [pieces[0]] + [
             lax.ppermute(piece, "gen", [(i, i ^ k) for i in range(size)])
-            for piece, k in zip(pieces[1:], ORDER[1:])
+            for piece, k in zip(pieces[1:], order[1:])
         ]
 
     def over_core(x):
@@ -459,7 +460,7 @@
                 [pltpu.VMEM((rows, 2 * lanes), BF)],
             )
         with jax.named_scope("exchange_back"):
-            got = over_gen([None, *msgs])[1:]
+            got = over_gen([None, *msgs], BACK_ORDER)[1:]
             both = group + 8
             part = group + both
             send, keep = call(

time: 90.2 us -> 89.4 us (level)
  starting transfers between devices: 36.4 us -> 30.8 us
  waiting for transfers between devices: 35.2 us -> 40 us
    ppermute x2, starting transfers between devices: 11.5 us -> 5.75 us  [turned(): return lax.ppermute(x, ('gen', 'neur'), pairs)]
    ppermute x2, waiting for transfers between devices: 0.01 us -> 3.18 us  [over_box(): return lax.ppermute(x, 'box', [(0, 1), (1, 0)])]
    ppermute x9, waiting for transfers between devices: 31.4 us -> 32.8 us  [over_gen(): lax.ppermute(piece, 'gen', [(i, i ^ k) for i in range(size)])]
  transfers between devices with their start and end apart: 21 -> 21, of which waited for: 8 -> 10; matrix products, arithmetic and copies ran while one was open for 2% -> 2% of each run, Pallas kernels for 12% -> 12%
where the time goes in v6:
time: 89.4 us; the launch traced here: 89.1 us
  waiting for transfers between devices  40 us (45%)
  starting transfers between devices  30.8 us (34%)
  Pallas kernels  13.6 us (15%)
  local copies, waits for them, and re-layouts  2.36 us (3%)
  other arithmetic  1.57 us (2%)
    ppermute x9, waiting for transfers between devices, over_gen(): lax.ppermute(piece, 'gen', [(i, i ^ k) for i in range(size)])  32.8 us
    ppermute x9, starting transfers between devices, over_gen(): lax.ppermute(piece, 'gen', [(i, i ^ k) for i in range(size)])  12.3 us
    pallas_call x10, Pallas kernels, call(): pl.pallas_call(body, grid_spec=pltpu.PrefetchScalarGridSpec(num_scalar_pr...  9.81 us
    ppermute x6, starting transfers between devices, over_core(): return lax.ppermute(x, 'neur', [(i, i ^ 1) for i in range(size)])  8.8 us
    ppermute x2, starting transfers between devices, turned(): return lax.ppermute(x, ('gen', 'neur'), pairs)  5.75 us
    pallas_call x1, Pallas kernels, square_body(): pl.pallas_call(functools.partial(weight_grad_kernel, boxes), grid_spec=pl...  3.78 us
    ppermute x2, waiting for transfers between devices, over_box(): return lax.ppermute(x, 'box', [(0, 1), (1, 0)])  3.18 us
    unnamed x10, local copies, waits for them, and re-layouts  2.25 us
  transfers between devices with their start and end apart: 21, of which 10 were waited for; matrix products, arithmetic and copies ran while one was open for 2% of the time, Pallas kernels for 12%

profile of v6, /device:TPU:1, one launch (start us, length us, event | category | flops | bytes accessed | tf_op | source)
XLA Modules:
  0.0 89.1 jit_solution(11127317324314492600)
XLA Ops:
  0.8 1.3 %copy-done.1 = bf16[4,32,4096]{2,1,0:T(8,128)(2,1)S(1)} copy-done((bf16[4,32,4096]{2,1,0:T(8,128)(2,1)S(1)}, bf16[4,32,4096]{2,1,0:T(8,128)(2,1)}, u32[]{:S(2)}) %copy-start.1) | copy-done | bytes 1048600
  2.2 0.9 %copy-done.2 = bf16[4,32,512]{2,1,0:T(8,128)(2,1)S(1)} copy-done((bf16[4,32,512]{2,1,0:T(8,128)(2,1)S(1)}, bf16[4,32,512]{2,1,0:T(8,128)(2,1)}, u32[]{:S(2)}) %copy-start.2) | copy-done | bytes 131096
  3.1 1.0 %exchange_generators.1 = (bf16[80,1024]{1,0:T(8,128)(2,1)S(1)}, bf16[80,1024]{1,0:T(8,128)(2,1)S(1)}, bf16[80,1024]{1,0:T(8,128)(2,1)S(1)}, bf16[80,1024]{1,0:T(8,128)(2,1)S(1)}) custom-call(s32[4]{0:T(128)S(1)} %pad_add_fusion.s_ref, bf16[4,32,4096]{2,1,0:T(8,128)(2,1)S(1)} %copy-done.1, bf16[4,32,512]{2,1,0:T(8,128)(2,1)S(1)} %copy-done.2), custom_call_target="tpu_custom_call" | custom-call | flops 1000000 | bytes 1048576 | tf_op jit(solution)/shard_map/exchange_generators/pallas_call | solution.py:93
  4.1 4.7 %collective-permute-start = (bf16[80,1024]{1,0:T(8,128)(2,1)S(1)}, bf16[80,1024]{1,0:T(8,128)(2,1)S(1)}, u32[]{:S(2)}, u32[]{:S(2)}) collective-permute-start(bf16[80,1024]{1,0:T(8,128)(2,1)S(1)} %get-tuple-element.39), channel_id=1, source_target_pairs={{0,24},{8,16},{16,8},{24,0},{1,25},{9,17},{17,9},{25,1},{2,26},{10... | collective-permute-start | bytes 491528 | tf_op jit(solution)/shard_map/exchange_generators/ppermute | solution.py:355
  9.9 0.7 pad_maximum_fusion
  10.7 2.6 %collective-permute-done.refs_0_.refs_3_ = bf16[80,1024]{1,0:T(8,128)(2,1)S(1)} collective-permute-done((bf16[80,1024]{1,0:T(8,128)(2,1)S(1)}, bf16[80,1024]{1,0:T(8,128)(2,1)S(1)}, u32[]{:S(2)}, u32[]{:S(2)}) %collective-permute-start) | collective-permute-done | bytes 163872 | tf_op jit(solution)/shard_map/exchange_generators/ppermute | solution.py:355
  13.3 0.9 %swap_cores.1.refs_1_.refs_4_ = bf16[4,1024,256]{2,1,0:T(8,128)(2,1)S(1)} custom-call(s32[4]{0:T(128)S(1)} %pad_add_fusion.s_ref, bf16[80,1024]{1,0:T(8,128)(2,1)S(1)} %collective-permute-done.refs_0_.refs_3_, bf16[1024,512]{1,0:T(8,128)(2,1)S(1)} %copy-done, bf16[1024,512]{1,0:T(8,128)(2,1)S(1)} %collective-permute-done.1.refs_2_), custom_call_target="tpu_custom_call" | custom-call | tf_op jit(solution)/shard_map/swap_cores/pallas_call | solution.py:93
  14.2 8.5 %collective-permute-done.2.refs_4_ = bf16[80,1024]{1,0:T(8,128)(2,1)S(1)} collective-permute-done((bf16[80,1024]{1,0:T(8,128)(2,1)S(1)}, bf16[80,1024]{1,0:T(8,128)(2,1)S(1)}, u32[]{:S(2)}, u32[]{:S(2)}) %collective-permute-start.2) | collective-permute-done | bytes 163872 | tf_op jit(solution)/shard_map/exchange_generators/ppermute | solution.py:355
  22.7 1.3 %forward.1 = (bf16[272,1024]{1,0:T(8,128)(2,1)S(1)}, bf16[256,128]{1,0:T(8,128)(2,1)S(1)}, bf16[256,128]{1,0:T(8,128)(2,1)S(1)}, f32[264,256]{1,0:T(8,128)S(1)},...) custom-call(s32[4]{0:T(128)S(1)} %pad_add_fusion.s_ref, bf16[4,4096]{1,0:T(4,128)(2,1)S(1)} %copy-done.3, ...), custom_call_target="tpu_custom_call" | custom-call | flops 1000000000 | bytes 1048576 | tf_op jit(solution)/shard_map/forward/pallas_call | solution.py:93
  24.0 2.3 %collective-permute-start.4 = (f32[264,256]{1,0:T(8,128)S(1)}, f32[264,256]{1,0:T(8,128)S(1)}, u32[]{:S(2)}, u32[]{:S(2)}) collective-permute-start(f32[264,256]{1,0:T(8,128)S(1)} %get-tuple-element.44), channel_id=1, source_target_pairs={{0,24},{8,16},{16,8},{24,0},{1,25},{9,17},{17,9},{25,1},{2,26},{10... | collective-permute-start | bytes 811016 | tf_op jit(solution)/shard_map/sum_products/ppermute | solution.py:355
  26.3 1.4 %collective-permute-start.6 = (f32[264,256]{1,0:T(8,128)S(1)}, f32[264,256]{1,0:T(8,128)S(1)}, u32[]{:S(2)}, u32[]{:S(2)}) collective-permute-start(f32[264,256]{1,0:T(8,128)S(1)} %get-tuple-element.46), channel_id=1, source_target_pairs={{0,8},{8,0},{16,24},{24,16},{1,9},{9,1},{17,25},{25,17},{2,10},{10... | collective-permute-start | bytes 811016 | tf_op jit(solution)/shard_map/sum_products/ppermute | solution.py:355
  27.6 1.2 %collective-permute-start.14 = (bf16[272,1024]{1,0:T(8,128)(2,1)S(1)}, bf16[272,1024]{1,0:T(8,128)(2,1)S(1)}, u32[]{:S(2)}, u32[]{:S(2)}) collective-permute-start(bf16[272,1024]{1,0:T(8,128)(2,1)S(1)} %get-tuple-element.56.refs_0_), channel_id=1, source_target_pairs={{0,1},{1,0},{2,3},{3,2},{4,5},{5,4},{6,7},{7,6},{8,9},{9,8},{10,11... | collective-permute-start | bytes 1671176 | tf_op jit(solution)/shard_map/share_generators/ppermute | solution.py:366
  29.0 2.1 %collective-permute-start.8 = (f32[8,512]{1,0:T(8,128)S(1)}, f32[8,512]{1,0:T(8,128)S(1)}, u32[]{:S(2)}, u32[]{:S(2)}) collective-permute-start(f32[8,512]{1,0:T(8,128)S(1)} %get-tuple-element.73), channel_id=1, source_target_pairs={{0,2},{2,0},{4,6},{6,4},{1,3},{3,1},{5,7},{7,5},{8,10},{10,8},{12,... | collective-permute-start | bytes 49160 | tf_op jit(solution)/shard_map/swap_cores/ppermute | solution.py:360
  31.0 0.8 collective-permute-done.8.refs_7_
  32.2 0.9 %collective-permute-done.7.refs_5_ = bf16[256,128]{1,0:T(8,128)(2,1)S(1)} collective-permute-done((bf16[256,128]{1,0:T(8,128)(2,1)S(1)}, bf16[256,128]{1,0:T(8,128)(2,1)S(1)}, u32[]{:S(2)}, u32[]{:S(2)}) %collective-permute-start.7) | collective-permute-done | bytes 65568 | tf_op jit(solution)/shard_map/sum_products/ppermute | solution.py:360
  33.1 14.5 %collective-permute-done.5.refs_2_ = f32[264,256]{1,0:T(8,128)S(1)} collective-permute-done((f32[264,256]{1,0:T(8,128)S(1)}, f32[264,256]{1,0:T(8,128)S(1)}, u32[]{:S(2)}, u32[]{:S(2)}) %collective-permute-start.5) | collective-permute-done | bytes 270368 | tf_op jit(solution)/shard_map/sum_products/ppermute | solution.py:355
  47.6 0.8 relax.1
  48.4 1.1 %collective-permute-start.10 = (bf16[336,256]{1,0:T(8,128)(2,1)S(1)}, bf16[336,256]{1,0:T(8,128)(2,1)S(1)}, u32[]{:S(2)}, u32[]{:S(2)}) collective-permute-start(bf16[336,256]{1,0:T(8,128)(2,1)S(1)} %get-tuple-element.51), channel_id=1, source_target_pairs={{0,24},{8,16},{16,8},{24,0},{1,25},{9,17},{17,9},{25,1},{2,26},{10... | collective-permute-start | bytes 516104 | tf_op jit(solution)/shard_map/exchange_back/ppermute | solution.py:355
  49.5 2.5 %collective-permute-start.9 = (bf16[336,256]{1,0:T(8,128)(2,1)S(1)}, bf16[336,256]{1,0:T(8,128)(2,1)S(1)}, u32[]{:S(2)}, u32[]{:S(2)}) collective-permute-start(bf16[336,256]{1,0:T(8,128)(2,1)S(1)} %get-tuple-element.50), channel_id=1, source_target_pairs={{0,16},{8,24},{16,0},{24,8},{1,17},{9,25},{17,1},{25,9},{2,18},{10... | collective-permute-start | bytes 516104 | tf_op jit(solution)/shard_map/exchange_back/ppermute | solution.py:355
  52.1 2.7 %collective-permute-start.13 = (bf16[272,1024]{1,0:T(8,128)(2,1)S(1)}, bf16[272,1024]{1,0:T(8,128)(2,1)S(1)}, u32[]{:S(2)}, u32[]{:S(2)}) collective-permute-start(bf16[272,1024]{1,0:T(8,128)(2,1)S(1)} %get-tuple-element.56.refs_0_), channel_id=1, source_target_pairs={{0,2},{2,0},{4,6},{6,4},{1,3},{3,1},{5,7},{7,5},{8,10},{10,8},{12,... | collective-permute-start | bytes 1671176 | tf_op jit(solution)/shard_map/share_generators/ppermute | solution.py:360
  54.8 6.5 %collective-permute-done.11.refs_3_.refs_5_ = bf16[336,256]{1,0:T(8,128)(2,1)S(1)} collective-permute-done((bf16[336,256]{1,0:T(8,128)(2,1)S(1)}, bf16[336,256]{1,0:T(8,128)(2,1)S(1)}, u32[]{:S(2)}, u32[]{:S(2)}) %collective-permute-start.11) | collective-permute-done | bytes 172064 | tf_op jit(solution)/shard_map/exchange_back/ppermute | solution.py:355
  61.3 0.7 collective-permute-done.9.refs_1_.refs_3_
  62.0 1.4 %exchange_back.2 = (bf16[136,1024]{1,0:T(8,128)(2,1)S(1)}, f32[136,1024]{1,0:T(8,128)S(1)}) custom-call(s32[4]{0:T(128)S(1)} %pad_add_fusion.s_ref, bf16[272,256]{1,0:T(8,128)(2,1)S(1)} %get-tuple-element.49.refs_0_.refs_1_, bf16[336,256]{1,0:T(8,128)(2,1)S(1)} %collective-permute-done.9.refs_1_.refs_3_, ...), custom_call_target="tpu_custom_call" | custom-call | tf_op jit(solution)/shard_map/exchange_back/pallas_call | solution.py:93
  63.4 1.3 %collective-permute-start.12 = (bf16[136,1024]{1,0:T(8,128)(2,1)S(1)}, bf16[136,1024]{1,0:T(8,128)(2,1)S(1)}, u32[]{:S(2)}, u32[]{:S(2)}) collective-permute-start(bf16[136,1024]{1,0:T(8,128)(2,1)S(1)} %get-tuple-element.54.refs_0_), channel_id=1, source_target_pairs={{0,4},{2,6},{4,0},{6,2},{1,5},{3,7},{5,1},{7,3},{8,12},{10,14},{12... | collective-permute-start | bytes 835592 | tf_op jit(solution)/shard_map/input_gradient/ppermute | solution.py:363
  64.7 3.0 %collective-permute-start.15 = (bf16[272,1024]{1,0:T(8,128)(2,1)S(1)}, bf16[272,1024]{1,0:T(8,128)(2,1)S(1)}, u32[]{:S(2)}, u32[]{:S(2)}) collective-permute-start(bf16[272,1024]{1,0:T(8,128)(2,1)S(1)} %collective-permute-done.14.refs_2_), channel_id=1, source_target_pairs={{0,2},{2,0},{4,6},{6,4},{1,3},{3,1},{5,7},{7,5},{8,10},{10,8},{12,... | collective-permute-start | bytes 1671176 | tf_op jit(solution)/shard_map/share_generators/ppermute | solution.py:360
  68.4 1.2 %collective-permute-start.18 = (bf16[272,512]{1,0:T(8,128)(2,1)S(1)}, bf16[272,512]{1,0:T(8,128)(2,1)S(1)}, u32[]{:S(2)}, u32[]{:S(2)}) collective-permute-start(bf16[272,512]{1,0:T(8,128)(2,1)S(1)} %get-tuple-element.60), channel_id=1, source_target_pairs={{0,3},{1,2},{2,1},{3,0},{4,7},{5,6},{6,5},{7,4},{8,11},{9,10},{10,... | collective-permute-start | bytes 835592 | tf_op jit(solution)/shard_map/input_gradient/ppermute | solution.py:370
  71.0 5.8 %collective-permute-start.19 = (bf16[72,1024]{1,0:T(8,128)(2,1)S(1)}, bf16[72,1024]{1,0:T(8,128)(2,1)S(1)}, u32[]{:S(2)}, u32[]{:S(2)}) collective-permute-start(bf16[72,1024]{1,0:T(8,128)(2,1)S(1)} %get-tuple-element.68), channel_id=1, source_target_pairs={{0,0},{2,16},{4,8},{6,24},{8,2},{10,18},{12,10},{14,26},{16,4},{18... | collective-permute-start | bytes 442376 | tf_op jit(solution)/shard_map/input_gradient/ppermute | solution.py:378
  78.0 1.2 %share_generators.1.left_ref = bf16[1024,1152]{1,0:T(8,128)(2,1)S(1)} custom-call(s32[4]{0:T(128)S(1)} %pad_add_fusion.s_ref, bf16[272,1024]{1,0:T(8,128)(2,1)S(1)} %get-tuple-element.56.refs_0_, bf16[272,1024]{1,0:T(8,128)(2,1)S(1)} %collective-permute-done.13.refs_1_, bf16[272,1024]{1,0:T(8,128)(2,1)S(1)} %collective-permute-done.14.refs_2_, ...), custom_call_target="tpu_custom_call" | custom-call | tf_op jit(solution)/shard_map/share_generators/pallas_call | solution.py:93
  79.2 3.2 %collective-permute-done.17.refs_2_ = bf16[272,512]{1,0:T(8,128)(2,1)S(1)} collective-permute-done((bf16[272,512]{1,0:T(8,128)(2,1)S(1)}, bf16[272,512]{1,0:T(8,128)(2,1)S(1)}, u32[]{:S(2)}, u32[]{:S(2)}) %collective-permute-start.17) | collective-permute-done | bytes 278560 | tf_op jit(solution)/shard_map/input_gradient/ppermute | solution.py:366
  82.4 3.8 %weight_gradient.1 = (f32[1024,512]{1,0:T(8,128)}, f32[1,512]{1,0:T(1,128)}, f32[4,512]{1,0:T(4,128)}, f32[4,512]{1,0:T(4,128)}, bf16[4,32,512]{2,1,0:T(8,128)(2,1)}, /*index=5*/f32[8,128]{1,0:T(8,128)S(1)}) custom-call(s32[4]{0:T(128)S(1)} %pad_add_fusion.s_ref, bf16[72,1024]{1,0:T(8,128)(2,1)S(1)} %get-tuple-element.55.refs_0_.after_ref, ...), custom_call_target="tpu_custom_call" | custom-call | tf_op jit(solution)/shard_map/weight_gradient/pallas_call | solution.py:511
  86.2 1.6 %collective-permute-done.20.refs_2_ = bf16[72,1024]{1,0:T(8,128)(2,1)S(1)} collective-permute-done((bf16[72,1024]{1,0:T(8,128)(2,1)S(1)}, bf16[72,1024]{1,0:T(8,128)(2,1)S(1)}, u32[]{:S(2)}, u32[]{:S(2)}) %collective-permute-start.20) | collective-permute-done | bytes 147488 | tf_op jit(solution)/shard_map/input_gradient/ppermute | solution.py:378
  87.7 1.4 %input_gradient.5 = (f32[4,32,1024]{2,1,0:T(8,128)}, f32[4,1024]{1,0:T(4,128)}) custom-call(s32[4]{0:T(128)S(1)} %pad_add_fusion.s_ref, f32[8,128]{1,0:T(8,128)S(1)} %get-tuple-element.67.refs_0_, bf16[72,1024]{1,0:T(8,128)(2,1)S(1)} %collective-permute-done.19.refs_1_, bf16[72,1024]{1,0:T(8,128)(2,1)S(1)} %collective-permute-done.20.refs_2_), custom_call_target="tpu_custom_call" | custom-call | tf_op jit(solution)/shard_map/input_gradient/pallas_call | solution.py:93
  (39 shorter events, 5.1 us)
Async XLA Ops:
  0.6 12.7 %copy-start = (bf16[1024,512]{1,0:T(8,128)(2,1)S(1)}, bf16[1024,512]{1,0:T(8,128)(2,1)}, u32[]{:S(2)}) copy-start(bf16[1024,512]{1,0:T(8,128)(2,1)} %refs_1_.3) | copy-start | bytes 3145732
  0.6 12.7 %collective-permute-start.1 = (bf16[1024,512]{1,0:T(8,128)(2,1)}, bf16[1024,512]{1,0:T(8,128)(2,1)S(1)}, u32[]{:S(2)}, u32[]{:S(2)}) collective-permute-start(bf16[1024,512]{1,0:T(8,128)(2,1)} %refs_1_.3), channel_id=1, source_target_pairs={{0,2},{2,0},{4,6},{6,4},{1,3},{3,1},{5,7},{7,5},{8,10},{10,8},{12,... | collective-permute-start | bytes 3145736 | tf_op jit(solution)/shard_map/swap_cores/ppermute | solution.py:360
  0.8 1.3 %copy-start.1 = (bf16[4,32,4096]{2,1,0:T(8,128)(2,1)S(1)}, bf16[4,32,4096]{2,1,0:T(8,128)(2,1)}, u32[]{:S(2)}) copy-start(bf16[4,32,4096]{2,1,0:T(8,128)(2,1)} %refs_0_.2) | copy-start | bytes 3145732
  2.2 0.9 %copy-start.2 = (bf16[4,32,512]{2,1,0:T(8,128)(2,1)S(1)}, bf16[4,32,512]{2,1,0:T(8,128)(2,1)}, u32[]{:S(2)}) copy-start(bf16[4,32,512]{2,1,0:T(8,128)(2,1)} %refs_1_.2) | copy-start | bytes 393220
  4.1 9.2 %collective-permute-start = (bf16[80,1024]{1,0:T(8,128)(2,1)S(1)}, bf16[80,1024]{1,0:T(8,128)(2,1)S(1)}, u32[]{:S(2)}, u32[]{:S(2)}) collective-permute-start(bf16[80,1024]{1,0:T(8,128)(2,1)S(1)} %get-tuple-element.39), channel_id=1, source_target_pairs={{0,24},{8,16},{16,8},{24,0},{1,25},{9,17},{17,9},{25,1},{2,26},{10... | collective-permute-start | bytes 491528 | tf_op jit(solution)/shard_map/exchange_generators/ppermute | solution.py:355
  8.8 13.9 %collective-permute-start.2 = (bf16[80,1024]{1,0:T(8,128)(2,1)S(1)}, bf16[80,1024]{1,0:T(8,128)(2,1)S(1)}, u32[]{:S(2)}, u32[]{:S(2)}) collective-permute-start(bf16[80,1024]{1,0:T(8,128)(2,1)S(1)} %get-tuple-element.41), channel_id=1, source_target_pairs={{0,16},{8,24},{16,0},{24,8},{1,17},{9,25},{17,1},{25,9},{2,18},{10... | collective-permute-start | bytes 491528 | tf_op jit(solution)/shard_map/exchange_generators/ppermute | solution.py:355
  8.8 13.9 %collective-permute-start.3 = (bf16[80,1024]{1,0:T(8,128)(2,1)S(1)}, bf16[80,1024]{1,0:T(8,128)(2,1)S(1)}, u32[]{:S(2)}, u32[]{:S(2)}) collective-permute-start(bf16[80,1024]{1,0:T(8,128)(2,1)S(1)} %get-tuple-element.42), channel_id=1, source_target_pairs={{0,8},{8,0},{16,24},{24,16},{1,9},{9,1},{17,25},{25,17},{2,10},{10... | collective-permute-start | bytes 491528 | tf_op jit(solution)/shard_map/exchange_generators/ppermute | solution.py:355
  10.7 12.0 %copy-start.3 = (bf16[4,4096]{1,0:T(4,128)(2,1)S(1)}, bf16[4,4096]{1,0:T(4,128)(2,1)}, u32[]{:S(2)}) copy-start(bf16[4,4096]{1,0:T(4,128)(2,1)} %refs_0_.3) | copy-start | bytes 98308
  14.2 14.7 %copy-start.4 = (f32[512]{0:T(512)S(1)}, f32[512]{0:T(512)}, u32[]{:S(2)}) copy-start(f32[512]{0:T(512)} %param.11) | copy-start | bytes 6148
  24.0 9.1 %collective-permute-start.4 = (f32[264,256]{1,0:T(8,128)S(1)}, f32[264,256]{1,0:T(8,128)S(1)}, u32[]{:S(2)}, u32[]{:S(2)}) collective-permute-start(f32[264,256]{1,0:T(8,128)S(1)} %get-tuple-element.44), channel_id=1, source_target_pairs={{0,24},{8,16},{16,8},{24,0},{1,25},{9,17},{17,9},{25,1},{2,26},{10... | collective-permute-start | bytes 811016 | tf_op jit(solution)/shard_map/sum_products/ppermute | solution.py:355
  26.3 21.3 %collective-permute-start.5 = (f32[264,256]{1,0:T(8,128)S(1)}, f32[264,256]{1,0:T(8,128)S(1)}, u32[]{:S(2)}, u32[]{:S(2)}) collective-permute-start(f32[264,256]{1,0:T(8,128)S(1)} %get-tuple-element.45), channel_id=1, source_target_pairs={{0,16},{8,24},{16,0},{24,8},{1,17},{9,25},{17,1},{25,9},{2,18},{10... | collective-permute-start | bytes 811016 | tf_op jit(solution)/shard_map/sum_products/ppermute | solution.py:355
  26.3 21.3 %collective-permute-start.6 = (f32[264,256]{1,0:T(8,128)S(1)}, f32[264,256]{1,0:T(8,128)S(1)}, u32[]{:S(2)}, u32[]{:S(2)}) collective-permute-start(f32[264,256]{1,0:T(8,128)S(1)} %get-tuple-element.46), channel_id=1, source_target_pairs={{0,8},{8,0},{16,24},{24,16},{1,9},{9,1},{17,25},{25,17},{2,10},{10... | collective-permute-start | bytes 811016 | tf_op jit(solution)/shard_map/sum_products/ppermute | solution.py:355
  27.6 37.0 %collective-permute-start.14 = (bf16[272,1024]{1,0:T(8,128)(2,1)S(1)}, bf16[272,1024]{1,0:T(8,128)(2,1)S(1)}, u32[]{:S(2)}, u32[]{:S(2)}) collective-permute-start(bf16[272,1024]{1,0:T(8,128)(2,1)S(1)} %get-tuple-element.56.refs_0_), channel_id=1, source_target_pairs={{0,1},{1,0},{2,3},{3,2},{4,5},{5,4},{6,7},{7,6},{8,9},{9,8},{10,11... | collective-permute-start | bytes 1671176 | tf_op jit(solution)/shard_map/share_generators/ppermute | solution.py:366
  29.0 2.9 %collective-permute-start.8 = (f32[8,512]{1,0:T(8,128)S(1)}, f32[8,512]{1,0:T(8,128)S(1)}, u32[]{:S(2)}, u32[]{:S(2)}) collective-permute-start(f32[8,512]{1,0:T(8,128)S(1)} %get-tuple-element.73), channel_id=1, source_target_pairs={{0,2},{2,0},{4,6},{6,4},{1,3},{3,1},{5,7},{7,5},{8,10},{10,8},{12,... | collective-permute-start | bytes 49160 | tf_op jit(solution)/shard_map/swap_cores/ppermute | solution.py:360
  31.9 1.3 %collective-permute-start.7 = (bf16[256,128]{1,0:T(8,128)(2,1)S(1)}, bf16[256,128]{1,0:T(8,128)(2,1)S(1)}, u32[]{:S(2)}, u32[]{:S(2)}) collective-permute-start(bf16[256,128]{1,0:T(8,128)(2,1)S(1)} %get-tuple-element.48), channel_id=1, source_target_pairs={{0,2},{2,0},{4,6},{6,4},{1,3},{3,1},{5,7},{7,5},{8,10},{10,8},{12,... | collective-permute-start | bytes 196616 | tf_op jit(solution)/shard_map/sum_products/ppermute | solution.py:360
  48.4 6.3 %collective-permute-start.10 = (bf16[336,256]{1,0:T(8,128)(2,1)S(1)}, bf16[336,256]{1,0:T(8,128)(2,1)S(1)}, u32[]{:S(2)}, u32[]{:S(2)}) collective-permute-start(bf16[336,256]{1,0:T(8,128)(2,1)S(1)} %get-tuple-element.51), channel_id=1, source_target_pairs={{0,24},{8,16},{16,8},{24,0},{1,25},{9,17},{17,9},{25,1},{2,26},{10... | collective-permute-start | bytes 516104 | tf_op jit(solution)/shard_map/exchange_back/ppermute | solution.py:355
  49.5 11.8 %collective-permute-start.11 = (bf16[336,256]{1,0:T(8,128)(2,1)S(1)}, bf16[336,256]{1,0:T(8,128)(2,1)S(1)}, u32[]{:S(2)}, u32[]{:S(2)}) collective-permute-start(bf16[336,256]{1,0:T(8,128)(2,1)S(1)} %get-tuple-element.52), channel_id=1, source_target_pairs={{0,8},{8,0},{16,24},{24,16},{1,9},{9,1},{17,25},{25,17},{2,10},{10... | collective-permute-start | bytes 516104 | tf_op jit(solution)/shard_map/exchange_back/ppermute | solution.py:355
  49.5 12.5 %collective-permute-start.9 = (bf16[336,256]{1,0:T(8,128)(2,1)S(1)}, bf16[336,256]{1,0:T(8,128)(2,1)S(1)}, u32[]{:S(2)}, u32[]{:S(2)}) collective-permute-start(bf16[336,256]{1,0:T(8,128)(2,1)S(1)} %get-tuple-element.50), channel_id=1, source_target_pairs={{0,16},{8,24},{16,0},{24,8},{1,17},{9,25},{17,1},{25,9},{2,18},{10... | collective-permute-start | bytes 516104 | tf_op jit(solution)/shard_map/exchange_back/ppermute | solution.py:355
  52.1 18.9 %collective-permute-start.13 = (bf16[272,1024]{1,0:T(8,128)(2,1)S(1)}, bf16[272,1024]{1,0:T(8,128)(2,1)S(1)}, u32[]{:S(2)}, u32[]{:S(2)}) collective-permute-start(bf16[272,1024]{1,0:T(8,128)(2,1)S(1)} %get-tuple-element.56.refs_0_), channel_id=1, source_target_pairs={{0,2},{2,0},{4,6},{6,4},{1,3},{3,1},{5,7},{7,5},{8,10},{10,8},{12,... | collective-permute-start | bytes 1671176 | tf_op jit(solution)/shard_map/share_generators/ppermute | solution.py:360
  63.4 6.7 %collective-permute-start.12 = (bf16[136,1024]{1,0:T(8,128)(2,1)S(1)}, bf16[136,1024]{1,0:T(8,128)(2,1)S(1)}, u32[]{:S(2)}, u32[]{:S(2)}) collective-permute-start(bf16[136,1024]{1,0:T(8,128)(2,1)S(1)} %get-tuple-element.54.refs_0_), channel_id=1, source_target_pairs={{0,4},{2,6},{4,0},{6,2},{1,5},{3,7},{5,1},{7,3},{8,12},{10,14},{12... | collective-permute-start | bytes 835592 | tf_op jit(solution)/shard_map/input_gradient/ppermute | solution.py:363
  64.7 13.3 %collective-permute-start.15 = (bf16[272,1024]{1,0:T(8,128)(2,1)S(1)}, bf16[272,1024]{1,0:T(8,128)(2,1)S(1)}, u32[]{:S(2)}, u32[]{:S(2)}) collective-permute-start(bf16[272,1024]{1,0:T(8,128)(2,1)S(1)} %collective-permute-done.14.refs_2_), channel_id=1, source_target_pairs={{0,2},{2,0},{4,6},{6,4},{1,3},{3,1},{5,7},{7,5},{8,10},{10,8},{12,... | collective-permute-start | bytes 1671176 | tf_op jit(solution)/shard_map/share_generators/ppermute | solution.py:360
  68.4 9.0 %collective-permute-start.18 = (bf16[272,512]{1,0:T(8,128)(2,1)S(1)}, bf16[272,512]{1,0:T(8,128)(2,1)S(1)}, u32[]{:S(2)}, u32[]{:S(2)}) collective-permute-start(bf16[272,512]{1,0:T(8,128)(2,1)S(1)} %get-tuple-element.60), channel_id=1, source_target_pairs={{0,3},{1,2},{2,1},{3,0},{4,7},{5,6},{6,5},{7,4},{8,11},{9,10},{10,... | collective-permute-start | bytes 835592 | tf_op jit(solution)/shard_map/input_gradient/ppermute | solution.py:370
  69.6 12.8 %collective-permute-start.16 = (bf16[336,512]{1,0:T(8,128)(2,1)S(1)}, bf16[336,512]{1,0:T(8,128)(2,1)S(1)}, u32[]{:S(2)}, u32[]{:S(2)}) collective-permute-start(bf16[336,512]{1,0:T(8,128)(2,1)S(1)} %get-tuple-element.59), channel_id=1, source_target_pairs={{0,2},{2,0},{4,6},{6,4},{1,3},{3,1},{5,7},{7,5},{8,10},{10,8},{12,... | collective-permute-start | bytes 1032200 | tf_op jit(solution)/shard_map/exchange_back/ppermute | solution.py:360
  70.1 12.2 %collective-permute-start.17 = (bf16[272,512]{1,0:T(8,128)(2,1)S(1)}, bf16[272,512]{1,0:T(8,128)(2,1)S(1)}, u32[]{:S(2)}, u32[]{:S(2)}) collective-permute-start(bf16[272,512]{1,0:T(8,128)(2,1)S(1)} %get-tuple-element.58.refs_0_), channel_id=1, source_target_pairs={{0,1},{1,0},{2,3},{3,2},{4,5},{5,4},{6,7},{7,6},{8,9},{9,8},{10,11... | collective-permute-start | bytes 835592 | tf_op jit(solution)/shard_map/input_gradient/ppermute | solution.py:366
  71.0 15.2 %collective-permute-start.19 = (bf16[72,1024]{1,0:T(8,128)(2,1)S(1)}, bf16[72,1024]{1,0:T(8,128)(2,1)S(1)}, u32[]{:S(2)}, u32[]{:S(2)}) collective-permute-start(bf16[72,1024]{1,0:T(8,128)(2,1)S(1)} %get-tuple-element.68), channel_id=1, source_target_pairs={{0,0},{2,16},{4,8},{6,24},{8,2},{10,18},{12,10},{14,26},{16,4},{18... | collective-permute-start | bytes 442376 | tf_op jit(solution)/shard_map/input_gradient/ppermute | solution.py:378
  77.4 10.3 %collective-permute-start.20 = (bf16[72,1024]{1,0:T(8,128)(2,1)S(1)}, bf16[72,1024]{1,0:T(8,128)(2,1)S(1)}, u32[]{:S(2)}, u32[]{:S(2)}) collective-permute-start(bf16[72,1024]{1,0:T(8,128)(2,1)S(1)} %get-tuple-element.55.refs_0_.after_ref), channel_id=1, source_target_pairs={{0,16},{2,0},{4,24},{6,8},{8,18},{10,2},{12,26},{14,10},{16,20},{1... | collective-permute-start | bytes 442376 | tf_op jit(solution)/shard_map/input_gradient/ppermute | solution.py:378

commit v7 on v6

--- a/solution.py
+++ b/solution.py
@@ -68,7 +68,7 @@
 HALVES = 1
 ORDER = (0, 3, 2, 1)
 BACK_ORDER = (0, 2, 3, 1)
-COSTS = {"fold": 1000000, "copy": 1000000000, "forward": 1000000000, "relax": 1000000000, "input_both": 300000000}
+COSTS = {"fold": 1000000, "copy": 1000000000, "forward": 1000000000, "relax": 1000000000, "input_both": 300000000, "input_final": 1000000000}
 
 
 def params():
@@ -310,14 +310,11 @@
         done_ref[...] = jnp.zeros(done_ref.shape, F32)
         tails = []
         for i, right in enumerate(rights):
-            stack[i * gens : (i + 1) * gens, :] = right[:gens, :cols]
             tail = right[gens : gens + CENTER_ROWS, :cols]
-            at = len(rights) * gens + i * CENTER_ROWS
-            stack[at : at + CENTER_ROWS, :] = tail
+            stack[i * CENTER_ROWS : (i + 1) * CENTER_ROWS, :] = tail
             tails.append(tail.astype(F32))
-        used = len(rights) * (gens + CENTER_ROWS)
-        if used < stack.shape[0]:
-            stack[used:, :] = jnp.zeros((stack.shape[0] - used, cols), BF)
+        used = len(rights) * CENTER_ROWS
+        stack[used:, :] = jnp.zeros((stack.shape[0] - used, cols), BF)
         bias_ref[...] = sum(jnp.sum(t[: 2 * boxes], 0, keepdims=True) for t in tails)
         for at, ref in ((2, center_ref), (4, offset_ref)):
             both = [
@@ -333,7 +330,11 @@
                 at = at * (HALVES * boxes) + h * boxes
                 gens_ref[pl.ds(at, boxes)] = out.reshape(boxes, per, -1)
 
-    weight_ref[...] = jnp.dot(left_ref[...], stack[...], preferred_element_type=F32)
+    total = jnp.dot(left_ref[:, len(rights) * gens :], stack[...], preferred_element_type=F32)
+    for i, right in enumerate(rights):
+        part = left_ref[:, i * gens : (i + 1) * gens]
+        total += jnp.dot(part, right[:gens, :cols], preferred_element_type=F32)
+    weight_ref[...] = total
 
 
 def square_body(size, gens, center, weight, bias, phase, gens_cot, center_cot, offset_cot):
@@ -517,7 +518,7 @@
                 + [whole(r) for r in rights + keeps],
                 out_specs=[pl.BlockSpec((depth // blocks, cols), lambda i, s: (i, 0))]
                 + [whole(o) for o in out_shape[1:]],
-                scratch_shapes=[pltpu.VMEM((left.shape[1], cols), BF)],
+                scratch_shapes=[pltpu.VMEM((128, cols), BF)],
             ),
             out_shape=out_shape,
             compiler_params=params(),

time: 89.4 us -> 89.4 us (level)
  no operation moved by 1% of the time
where the time goes in v7:
time: 89.4 us; the launch traced here: 89.1 us
  waiting for transfers between devices  40.1 us (45%)
  starting transfers between devices  30.8 us (34%)
  Pallas kernels  13.5 us (15%)
  local copies, waits for them, and re-layouts  2.36 us (3%)
  other arithmetic  1.57 us (2%)
    ppermute x9, waiting for transfers between devices, over_gen(): lax.ppermute(piece, 'gen', [(i, i ^ k) for i in range(size)])  32.8 us
    ppermute x9, starting transfers between devices, over_gen(): lax.ppermute(piece, 'gen', [(i, i ^ k) for i in range(size)])  12.3 us
    pallas_call x10, Pallas kernels, call(): pl.pallas_call(body, grid_spec=pltpu.PrefetchScalarGridSpec(num_scalar_pr...  9.81 us
    ppermute x6, starting transfers between devices, over_core(): return lax.ppermute(x, 'neur', [(i, i ^ 1) for i in range(size)])  8.8 us
    ppermute x2, starting transfers between devices, turned(): return lax.ppermute(x, ('gen', 'neur'), pairs)  5.75 us
    pallas_call x1, Pallas kernels, square_body(): pl.pallas_call(functools.partial(weight_grad_kernel, boxes), grid_spec=pl...  3.71 us
    ppermute x2, waiting for transfers between devices, over_box(): return lax.ppermute(x, 'box', [(0, 1), (1, 0)])  3.18 us
    unnamed x10, local copies, waits for them, and re-layouts  2.25 us
  transfers between devices with their start and end apart: 21, of which 10 were waited for; matrix products, arithmetic and copies ran while one was open for 2% of the time, Pallas kernels for 12%

profile of v7, /device:TPU:1, one launch (start us, length us, event | category | flops | bytes accessed | tf_op | source)
XLA Modules:
  0.0 89.1 jit_solution(2785420871873889213)
XLA Ops:
  0.8 1.3 %copy-done.1 = bf16[4,32,4096]{2,1,0:T(8,128)(2,1)S(1)} copy-done((bf16[4,32,4096]{2,1,0:T(8,128)(2,1)S(1)}, bf16[4,32,4096]{2,1,0:T(8,128)(2,1)}, u32[]{:S(2)}) %copy-start.1) | copy-done | bytes 1048600
  2.2 0.9 %copy-done.2 = bf16[4,32,512]{2,1,0:T(8,128)(2,1)S(1)} copy-done((bf16[4,32,512]{2,1,0:T(8,128)(2,1)S(1)}, bf16[4,32,512]{2,1,0:T(8,128)(2,1)}, u32[]{:S(2)}) %copy-start.2) | copy-done | bytes 131096
  3.1 1.0 %exchange_generators.1 = (bf16[80,1024]{1,0:T(8,128)(2,1)S(1)}, bf16[80,1024]{1,0:T(8,128)(2,1)S(1)}, bf16[80,1024]{1,0:T(8,128)(2,1)S(1)}, bf16[80,1024]{1,0:T(8,128)(2,1)S(1)}) custom-call(s32[4]{0:T(128)S(1)} %pad_add_fusion.s_ref, bf16[4,32,4096]{2,1,0:T(8,128)(2,1)S(1)} %copy-done.1, bf16[4,32,512]{2,1,0:T(8,128)(2,1)S(1)} %copy-done.2), custom_call_target="tpu_custom_call" | custom-call | flops 1000000 | bytes 1048576 | tf_op jit(solution)/shard_map/exchange_generators/pallas_call | solution.py:93
  4.1 4.7 %collective-permute-start = (bf16[80,1024]{1,0:T(8,128)(2,1)S(1)}, bf16[80,1024]{1,0:T(8,128)(2,1)S(1)}, u32[]{:S(2)}, u32[]{:S(2)}) collective-permute-start(bf16[80,1024]{1,0:T(8,128)(2,1)S(1)} %get-tuple-element.39), channel_id=1, source_target_pairs={{0,24},{8,16},{16,8},{24,0},{1,25},{9,17},{17,9},{25,1},{2,26},{10... | collective-permute-start | bytes 491528 | tf_op jit(solution)/shard_map/exchange_generators/ppermute | solution.py:356
  9.9 0.7 pad_maximum_fusion
  10.7 2.6 %collective-permute-done.refs_0_.refs_3_ = bf16[80,1024]{1,0:T(8,128)(2,1)S(1)} collective-permute-done((bf16[80,1024]{1,0:T(8,128)(2,1)S(1)}, bf16[80,1024]{1,0:T(8,128)(2,1)S(1)}, u32[]{:S(2)}, u32[]{:S(2)}) %collective-permute-start) | collective-permute-done | bytes 163872 | tf_op jit(solution)/shard_map/exchange_generators/ppermute | solution.py:356
  13.3 0.9 %swap_cores.1.refs_1_.refs_4_ = bf16[4,1024,256]{2,1,0:T(8,128)(2,1)S(1)} custom-call(s32[4]{0:T(128)S(1)} %pad_add_fusion.s_ref, bf16[80,1024]{1,0:T(8,128)(2,1)S(1)} %collective-permute-done.refs_0_.refs_3_, bf16[1024,512]{1,0:T(8,128)(2,1)S(1)} %copy-done, bf16[1024,512]{1,0:T(8,128)(2,1)S(1)} %collective-permute-done.1.refs_2_), custom_call_target="tpu_custom_call" | custom-call | tf_op jit(solution)/shard_map/swap_cores/pallas_call | solution.py:93
  14.2 8.5 %collective-permute-done.2.refs_4_ = bf16[80,1024]{1,0:T(8,128)(2,1)S(1)} collective-permute-done((bf16[80,1024]{1,0:T(8,128)(2,1)S(1)}, bf16[80,1024]{1,0:T(8,128)(2,1)S(1)}, u32[]{:S(2)}, u32[]{:S(2)}) %collective-permute-start.2) | collective-permute-done | bytes 163872 | tf_op jit(solution)/shard_map/exchange_generators/ppermute | solution.py:356
  22.7 1.3 %forward.1 = (bf16[272,1024]{1,0:T(8,128)(2,1)S(1)}, bf16[256,128]{1,0:T(8,128)(2,1)S(1)}, bf16[256,128]{1,0:T(8,128)(2,1)S(1)}, f32[264,256]{1,0:T(8,128)S(1)},...) custom-call(s32[4]{0:T(128)S(1)} %pad_add_fusion.s_ref, bf16[4,4096]{1,0:T(4,128)(2,1)S(1)} %copy-done.3, ...), custom_call_target="tpu_custom_call" | custom-call | flops 1000000000 | bytes 1048576 | tf_op jit(solution)/shard_map/forward/pallas_call | solution.py:93
  24.0 2.3 %collective-permute-start.4 = (f32[264,256]{1,0:T(8,128)S(1)}, f32[264,256]{1,0:T(8,128)S(1)}, u32[]{:S(2)}, u32[]{:S(2)}) collective-permute-start(f32[264,256]{1,0:T(8,128)S(1)} %get-tuple-element.44), channel_id=1, source_target_pairs={{0,24},{8,16},{16,8},{24,0},{1,25},{9,17},{17,9},{25,1},{2,26},{10... | collective-permute-start | bytes 811016 | tf_op jit(solution)/shard_map/sum_products/ppermute | solution.py:356
  26.3 1.4 %collective-permute-start.6 = (f32[264,256]{1,0:T(8,128)S(1)}, f32[264,256]{1,0:T(8,128)S(1)}, u32[]{:S(2)}, u32[]{:S(2)}) collective-permute-start(f32[264,256]{1,0:T(8,128)S(1)} %get-tuple-element.46), channel_id=1, source_target_pairs={{0,8},{8,0},{16,24},{24,16},{1,9},{9,1},{17,25},{25,17},{2,10},{10... | collective-permute-start | bytes 811016 | tf_op jit(solution)/shard_map/sum_products/ppermute | solution.py:356
  27.6 1.2 %collective-permute-start.14 = (bf16[272,1024]{1,0:T(8,128)(2,1)S(1)}, bf16[272,1024]{1,0:T(8,128)(2,1)S(1)}, u32[]{:S(2)}, u32[]{:S(2)}) collective-permute-start(bf16[272,1024]{1,0:T(8,128)(2,1)S(1)} %get-tuple-element.56.refs_0_), channel_id=1, source_target_pairs={{0,1},{1,0},{2,3},{3,2},{4,5},{5,4},{6,7},{7,6},{8,9},{9,8},{10,11... | collective-permute-start | bytes 1671176 | tf_op jit(solution)/shard_map/share_generators/ppermute | solution.py:367
  29.0 2.1 %collective-permute-start.8 = (f32[8,512]{1,0:T(8,128)S(1)}, f32[8,512]{1,0:T(8,128)S(1)}, u32[]{:S(2)}, u32[]{:S(2)}) collective-permute-start(f32[8,512]{1,0:T(8,128)S(1)} %get-tuple-element.73), channel_id=1, source_target_pairs={{0,2},{2,0},{4,6},{6,4},{1,3},{3,1},{5,7},{7,5},{8,10},{10,8},{12,... | collective-permute-start | bytes 49160 | tf_op jit(solution)/shard_map/swap_cores/ppermute | solution.py:361
  31.0 0.8 collective-permute-done.8.refs_7_
  32.2 0.9 %collective-permute-done.7.refs_5_ = bf16[256,128]{1,0:T(8,128)(2,1)S(1)} collective-permute-done((bf16[256,128]{1,0:T(8,128)(2,1)S(1)}, bf16[256,128]{1,0:T(8,128)(2,1)S(1)}, u32[]{:S(2)}, u32[]{:S(2)}) %collective-permute-start.7) | collective-permute-done | bytes 65568 | tf_op jit(solution)/shard_map/sum_products/ppermute | solution.py:361
  33.1 14.5 %collective-permute-done.5.refs_2_ = f32[264,256]{1,0:T(8,128)S(1)} collective-permute-done((f32[264,256]{1,0:T(8,128)S(1)}, f32[264,256]{1,0:T(8,128)S(1)}, u32[]{:S(2)}, u32[]{:S(2)}) %collective-permute-start.5) | collective-permute-done | bytes 270368 | tf_op jit(solution)/shard_map/sum_products/ppermute | solution.py:356
  47.6 0.8 relax.1
  48.4 1.1 %collective-permute-start.10 = (bf16[336,256]{1,0:T(8,128)(2,1)S(1)}, bf16[336,256]{1,0:T(8,128)(2,1)S(1)}, u32[]{:S(2)}, u32[]{:S(2)}) collective-permute-start(bf16[336,256]{1,0:T(8,128)(2,1)S(1)} %get-tuple-element.51), channel_id=1, source_target_pairs={{0,24},{8,16},{16,8},{24,0},{1,25},{9,17},{17,9},{25,1},{2,26},{10... | collective-permute-start | bytes 516104 | tf_op jit(solution)/shard_map/exchange_back/ppermute | solution.py:356
  49.5 2.5 %collective-permute-start.9 = (bf16[336,256]{1,0:T(8,128)(2,1)S(1)}, bf16[336,256]{1,0:T(8,128)(2,1)S(1)}, u32[]{:S(2)}, u32[]{:S(2)}) collective-permute-start(bf16[336,256]{1,0:T(8,128)(2,1)S(1)} %get-tuple-element.50), channel_id=1, source_target_pairs={{0,16},{8,24},{16,0},{24,8},{1,17},{9,25},{17,1},{25,9},{2,18},{10... | collective-permute-start | bytes 516104 | tf_op jit(solution)/shard_map/exchange_back/ppermute | solution.py:356
  52.1 2.7 %collective-permute-start.13 = (bf16[272,1024]{1,0:T(8,128)(2,1)S(1)}, bf16[272,1024]{1,0:T(8,128)(2,1)S(1)}, u32[]{:S(2)}, u32[]{:S(2)}) collective-permute-start(bf16[272,1024]{1,0:T(8,128)(2,1)S(1)} %get-tuple-element.56.refs_0_), channel_id=1, source_target_pairs={{0,2},{2,0},{4,6},{6,4},{1,3},{3,1},{5,7},{7,5},{8,10},{10,8},{12,... | collective-permute-start | bytes 1671176 | tf_op jit(solution)/shard_map/share_generators/ppermute | solution.py:361
  54.8 6.5 %collective-permute-done.11.refs_3_.refs_5_ = bf16[336,256]{1,0:T(8,128)(2,1)S(1)} collective-permute-done((bf16[336,256]{1,0:T(8,128)(2,1)S(1)}, bf16[336,256]{1,0:T(8,128)(2,1)S(1)}, u32[]{:S(2)}, u32[]{:S(2)}) %collective-permute-start.11) | collective-permute-done | bytes 172064 | tf_op jit(solution)/shard_map/exchange_back/ppermute | solution.py:356
  61.3 0.7 collective-permute-done.9.refs_1_.refs_3_
  62.0 1.4 %exchange_back.2 = (bf16[136,1024]{1,0:T(8,128)(2,1)S(1)}, f32[136,1024]{1,0:T(8,128)S(1)}) custom-call(s32[4]{0:T(128)S(1)} %pad_add_fusion.s_ref, bf16[272,256]{1,0:T(8,128)(2,1)S(1)} %get-tuple-element.49.refs_0_.refs_1_, bf16[336,256]{1,0:T(8,128)(2,1)S(1)} %collective-permute-done.9.refs_1_.refs_3_, ...), custom_call_target="tpu_custom_call" | custom-call | tf_op jit(solution)/shard_map/exchange_back/pallas_call | solution.py:93
  63.4 1.3 %collective-permute-start.12 = (bf16[136,1024]{1,0:T(8,128)(2,1)S(1)}, bf16[136,1024]{1,0:T(8,128)(2,1)S(1)}, u32[]{:S(2)}, u32[]{:S(2)}) collective-permute-start(bf16[136,1024]{1,0:T(8,128)(2,1)S(1)} %get-tuple-element.54.refs_0_), channel_id=1, source_target_pairs={{0,4},{2,6},{4,0},{6,2},{1,5},{3,7},{5,1},{7,3},{8,12},{10,14},{12... | collective-permute-start | bytes 835592 | tf_op jit(solution)/shard_map/input_gradient/ppermute | solution.py:364
  64.7 3.0 %collective-permute-start.15 = (bf16[272,1024]{1,0:T(8,128)(2,1)S(1)}, bf16[272,1024]{1,0:T(8,128)(2,1)S(1)}, u32[]{:S(2)}, u32[]{:S(2)}) collective-permute-start(bf16[272,1024]{1,0:T(8,128)(2,1)S(1)} %collective-permute-done.14.refs_2_), channel_id=1, source_target_pairs={{0,2},{2,0},{4,6},{6,4},{1,3},{3,1},{5,7},{7,5},{8,10},{10,8},{12,... | collective-permute-start | bytes 1671176 | tf_op jit(solution)/shard_map/share_generators/ppermute | solution.py:361
  68.4 1.2 %collective-permute-start.18 = (bf16[272,512]{1,0:T(8,128)(2,1)S(1)}, bf16[272,512]{1,0:T(8,128)(2,1)S(1)}, u32[]{:S(2)}, u32[]{:S(2)}) collective-permute-start(bf16[272,512]{1,0:T(8,128)(2,1)S(1)} %get-tuple-element.60), channel_id=1, source_target_pairs={{0,3},{1,2},{2,1},{3,0},{4,7},{5,6},{6,5},{7,4},{8,11},{9,10},{10,... | collective-permute-start | bytes 835592 | tf_op jit(solution)/shard_map/input_gradient/ppermute | solution.py:371
  71.0 5.8 %collective-permute-start.19 = (bf16[72,1024]{1,0:T(8,128)(2,1)S(1)}, bf16[72,1024]{1,0:T(8,128)(2,1)S(1)}, u32[]{:S(2)}, u32[]{:S(2)}) collective-permute-start(bf16[72,1024]{1,0:T(8,128)(2,1)S(1)} %get-tuple-element.68), channel_id=1, source_target_pairs={{0,0},{2,16},{4,8},{6,24},{8,2},{10,18},{12,10},{14,26},{16,4},{18... | collective-permute-start | bytes 442376 | tf_op jit(solution)/shard_map/input_gradient/ppermute | solution.py:379
  78.0 1.2 %share_generators.1.left_ref = bf16[1024,1152]{1,0:T(8,128)(2,1)S(1)} custom-call(s32[4]{0:T(128)S(1)} %pad_add_fusion.s_ref, bf16[272,1024]{1,0:T(8,128)(2,1)S(1)} %get-tuple-element.56.refs_0_, bf16[272,1024]{1,0:T(8,128)(2,1)S(1)} %collective-permute-done.13.refs_1_, bf16[272,1024]{1,0:T(8,128)(2,1)S(1)} %collective-permute-done.14.refs_2_, ...), custom_call_target="tpu_custom_call" | custom-call | tf_op jit(solution)/shard_map/share_generators/pallas_call | solution.py:93
  79.2 3.2 %collective-permute-done.17.refs_2_ = bf16[272,512]{1,0:T(8,128)(2,1)S(1)} collective-permute-done((bf16[272,512]{1,0:T(8,128)(2,1)S(1)}, bf16[272,512]{1,0:T(8,128)(2,1)S(1)}, u32[]{:S(2)}, u32[]{:S(2)}) %collective-permute-start.17) | collective-permute-done | bytes 278560 | tf_op jit(solution)/shard_map/input_gradient/ppermute | solution.py:367
  82.4 3.7 %weight_gradient.1 = (f32[1024,512]{1,0:T(8,128)}, f32[1,512]{1,0:T(1,128)}, f32[4,512]{1,0:T(4,128)}, f32[4,512]{1,0:T(4,128)}, bf16[4,32,512]{2,1,0:T(8,128)(2,1)}, /*index=5*/f32[8,128]{1,0:T(8,128)S(1)}) custom-call(s32[4]{0:T(128)S(1)} %pad_add_fusion.s_ref, bf16[72,1024]{1,0:T(8,128)(2,1)S(1)} %get-tuple-element.55.refs_0_.after_ref, ...), custom_call_target="tpu_custom_call" | custom-call | tf_op jit(solution)/shard_map/weight_gradient/pallas_call | solution.py:512
  86.1 1.6 %collective-permute-done.20.refs_2_ = bf16[72,1024]{1,0:T(8,128)(2,1)S(1)} collective-permute-done((bf16[72,1024]{1,0:T(8,128)(2,1)S(1)}, bf16[72,1024]{1,0:T(8,128)(2,1)S(1)}, u32[]{:S(2)}, u32[]{:S(2)}) %collective-permute-start.20) | collective-permute-done | bytes 147488 | tf_op jit(solution)/shard_map/input_gradient/ppermute | solution.py:379
  87.7 1.4 %input_gradient.5 = (f32[4,32,1024]{2,1,0:T(8,128)}, f32[4,1024]{1,0:T(4,128)}) custom-call(s32[4]{0:T(128)S(1)} %pad_add_fusion.s_ref, f32[8,128]{1,0:T(8,128)S(1)} %get-tuple-element.67.refs_0_, bf16[72,1024]{1,0:T(8,128)(2,1)S(1)} %collective-permute-done.19.refs_1_, bf16[72,1024]{1,0:T(8,128)(2,1)S(1)} %collective-permute-done.20.refs_2_), custom_call_target="tpu_custom_call" | custom-call | flops 1000000000 | bytes 1048576 | tf_op jit(solution)/shard_map/input_gradient/pallas_call | solution.py:93
  (39 shorter events, 5.1 us)
Async XLA Ops:
  0.6 12.7 %copy-start = (bf16[1024,512]{1,0:T(8,128)(2,1)S(1)}, bf16[1024,512]{1,0:T(8,128)(2,1)}, u32[]{:S(2)}) copy-start(bf16[1024,512]{1,0:T(8,128)(2,1)} %refs_1_.3) | copy-start | bytes 3145732
  0.6 12.7 %collective-permute-start.1 = (bf16[1024,512]{1,0:T(8,128)(2,1)}, bf16[1024,512]{1,0:T(8,128)(2,1)S(1)}, u32[]{:S(2)}, u32[]{:S(2)}) collective-permute-start(bf16[1024,512]{1,0:T(8,128)(2,1)} %refs_1_.3), channel_id=1, source_target_pairs={{0,2},{2,0},{4,6},{6,4},{1,3},{3,1},{5,7},{7,5},{8,10},{10,8},{12,... | collective-permute-start | bytes 3145736 | tf_op jit(solution)/shard_map/swap_cores/ppermute | solution.py:361
  0.8 1.3 %copy-start.1 = (bf16[4,32,4096]{2,1,0:T(8,128)(2,1)S(1)}, bf16[4,32,4096]{2,1,0:T(8,128)(2,1)}, u32[]{:S(2)}) copy-start(bf16[4,32,4096]{2,1,0:T(8,128)(2,1)} %refs_0_.2) | copy-start | bytes 3145732
  2.2 0.9 %copy-start.2 = (bf16[4,32,512]{2,1,0:T(8,128)(2,1)S(1)}, bf16[4,32,512]{2,1,0:T(8,128)(2,1)}, u32[]{:S(2)}) copy-start(bf16[4,32,512]{2,1,0:T(8,128)(2,1)} %refs_1_.2) | copy-start | bytes 393220
  4.1 9.2 %collective-permute-start = (bf16[80,1024]{1,0:T(8,128)(2,1)S(1)}, bf16[80,1024]{1,0:T(8,128)(2,1)S(1)}, u32[]{:S(2)}, u32[]{:S(2)}) collective-permute-start(bf16[80,1024]{1,0:T(8,128)(2,1)S(1)} %get-tuple-element.39), channel_id=1, source_target_pairs={{0,24},{8,16},{16,8},{24,0},{1,25},{9,17},{17,9},{25,1},{2,26},{10... | collective-permute-start | bytes 491528 | tf_op jit(solution)/shard_map/exchange_generators/ppermute | solution.py:356
  8.8 13.9 %collective-permute-start.2 = (bf16[80,1024]{1,0:T(8,128)(2,1)S(1)}, bf16[80,1024]{1,0:T(8,128)(2,1)S(1)}, u32[]{:S(2)}, u32[]{:S(2)}) collective-permute-start(bf16[80,1024]{1,0:T(8,128)(2,1)S(1)} %get-tuple-element.41), channel_id=1, source_target_pairs={{0,16},{8,24},{16,0},{24,8},{1,17},{9,25},{17,1},{25,9},{2,18},{10... | collective-permute-start | bytes 491528 | tf_op jit(solution)/shard_map/exchange_generators/ppermute | solution.py:356
  8.8 13.9 %collective-permute-start.3 = (bf16[80,1024]{1,0:T(8,128)(2,1)S(1)}, bf16[80,1024]{1,0:T(8,128)(2,1)S(1)}, u32[]{:S(2)}, u32[]{:S(2)}) collective-permute-start(bf16[80,1024]{1,0:T(8,128)(2,1)S(1)} %get-tuple-element.42), channel_id=1, source_target_pairs={{0,8},{8,0},{16,24},{24,16},{1,9},{9,1},{17,25},{25,17},{2,10},{10... | collective-permute-start | bytes 491528 | tf_op jit(solution)/shard_map/exchange_generators/ppermute | solution.py:356
  10.7 12.0 %copy-start.3 = (bf16[4,4096]{1,0:T(4,128)(2,1)S(1)}, bf16[4,4096]{1,0:T(4,128)(2,1)}, u32[]{:S(2)}) copy-start(bf16[4,4096]{1,0:T(4,128)(2,1)} %refs_0_.3) | copy-start | bytes 98308
  14.2 14.7 %copy-start.4 = (f32[512]{0:T(512)S(1)}, f32[512]{0:T(512)}, u32[]{:S(2)}) copy-start(f32[512]{0:T(512)} %param.11) | copy-start | bytes 6148
  24.0 9.1 %collective-permute-start.4 = (f32[264,256]{1,0:T(8,128)S(1)}, f32[264,256]{1,0:T(8,128)S(1)}, u32[]{:S(2)}, u32[]{:S(2)}) collective-permute-start(f32[264,256]{1,0:T(8,128)S(1)} %get-tuple-element.44), channel_id=1, source_target_pairs={{0,24},{8,16},{16,8},{24,0},{1,25},{9,17},{17,9},{25,1},{2,26},{10... | collective-permute-start | bytes 811016 | tf_op jit(solution)/shard_map/sum_products/ppermute | solution.py:356
  26.3 21.3 %collective-permute-start.5 = (f32[264,256]{1,0:T(8,128)S(1)}, f32[264,256]{1,0:T(8,128)S(1)}, u32[]{:S(2)}, u32[]{:S(2)}) collective-permute-start(f32[264,256]{1,0:T(8,128)S(1)} %get-tuple-element.45), channel_id=1, source_target_pairs={{0,16},{8,24},{16,0},{24,8},{1,17},{9,25},{17,1},{25,9},{2,18},{10... | collective-permute-start | bytes 811016 | tf_op jit(solution)/shard_map/sum_products/ppermute | solution.py:356
  26.3 21.3 %collective-permute-start.6 = (f32[264,256]{1,0:T(8,128)S(1)}, f32[264,256]{1,0:T(8,128)S(1)}, u32[]{:S(2)}, u32[]{:S(2)}) collective-permute-start(f32[264,256]{1,0:T(8,128)S(1)} %get-tuple-element.46), channel_id=1, source_target_pairs={{0,8},{8,0},{16,24},{24,16},{1,9},{9,1},{17,25},{25,17},{2,10},{10... | collective-permute-start | bytes 811016 | tf_op jit(solution)/shard_map/sum_products/ppermute | solution.py:356
  27.6 37.0 %collective-permute-start.14 = (bf16[272,1024]{1,0:T(8,128)(2,1)S(1)}, bf16[272,1024]{1,0:T(8,128)(2,1)S(1)}, u32[]{:S(2)}, u32[]{:S(2)}) collective-permute-start(bf16[272,1024]{1,0:T(8,128)(2,1)S(1)} %get-tuple-element.56.refs_0_), channel_id=1, source_target_pairs={{0,1},{1,0},{2,3},{3,2},{4,5},{5,4},{6,7},{7,6},{8,9},{9,8},{10,11... | collective-permute-start | bytes 1671176 | tf_op jit(solution)/shard_map/share_generators/ppermute | solution.py:367
  29.0 2.9 %collective-permute-start.8 = (f32[8,512]{1,0:T(8,128)S(1)}, f32[8,512]{1,0:T(8,128)S(1)}, u32[]{:S(2)}, u32[]{:S(2)}) collective-permute-start(f32[8,512]{1,0:T(8,128)S(1)} %get-tuple-element.73), channel_id=1, source_target_pairs={{0,2},{2,0},{4,6},{6,4},{1,3},{3,1},{5,7},{7,5},{8,10},{10,8},{12,... | collective-permute-start | bytes 49160 | tf_op jit(solution)/shard_map/swap_cores/ppermute | solution.py:361
  31.9 1.3 %collective-permute-start.7 = (bf16[256,128]{1,0:T(8,128)(2,1)S(1)}, bf16[256,128]{1,0:T(8,128)(2,1)S(1)}, u32[]{:S(2)}, u32[]{:S(2)}) collective-permute-start(bf16[256,128]{1,0:T(8,128)(2,1)S(1)} %get-tuple-element.48), channel_id=1, source_target_pairs={{0,2},{2,0},{4,6},{6,4},{1,3},{3,1},{5,7},{7,5},{8,10},{10,8},{12,... | collective-permute-start | bytes 196616 | tf_op jit(solution)/shard_map/sum_products/ppermute | solution.py:361
  48.4 6.3 %collective-permute-start.10 = (bf16[336,256]{1,0:T(8,128)(2,1)S(1)}, bf16[336,256]{1,0:T(8,128)(2,1)S(1)}, u32[]{:S(2)}, u32[]{:S(2)}) collective-permute-start(bf16[336,256]{1,0:T(8,128)(2,1)S(1)} %get-tuple-element.51), channel_id=1, source_target_pairs={{0,24},{8,16},{16,8},{24,0},{1,25},{9,17},{17,9},{25,1},{2,26},{10... | collective-permute-start | bytes 516104 | tf_op jit(solution)/shard_map/exchange_back/ppermute | solution.py:356
  49.5 11.8 %collective-permute-start.11 = (bf16[336,256]{1,0:T(8,128)(2,1)S(1)}, bf16[336,256]{1,0:T(8,128)(2,1)S(1)}, u32[]{:S(2)}, u32[]{:S(2)}) collective-permute-start(bf16[336,256]{1,0:T(8,128)(2,1)S(1)} %get-tuple-element.52), channel_id=1, source_target_pairs={{0,8},{8,0},{16,24},{24,16},{1,9},{9,1},{17,25},{25,17},{2,10},{10... | collective-permute-start | bytes 516104 | tf_op jit(solution)/shard_map/exchange_back/ppermute | solution.py:356
  49.5 12.5 %collective-permute-start.9 = (bf16[336,256]{1,0:T(8,128)(2,1)S(1)}, bf16[336,256]{1,0:T(8,128)(2,1)S(1)}, u32[]{:S(2)}, u32[]{:S(2)}) collective-permute-start(bf16[336,256]{1,0:T(8,128)(2,1)S(1)} %get-tuple-element.50), channel_id=1, source_target_pairs={{0,16},{8,24},{16,0},{24,8},{1,17},{9,25},{17,1},{25,9},{2,18},{10... | collective-permute-start | bytes 516104 | tf_op jit(solution)/shard_map/exchange_back/ppermute | solution.py:356
  52.1 18.9 %collective-permute-start.13 = (bf16[272,1024]{1,0:T(8,128)(2,1)S(1)}, bf16[272,1024]{1,0:T(8,128)(2,1)S(1)}, u32[]{:S(2)}, u32[]{:S(2)}) collective-permute-start(bf16[272,1024]{1,0:T(8,128)(2,1)S(1)} %get-tuple-element.56.refs_0_), channel_id=1, source_target_pairs={{0,2},{2,0},{4,6},{6,4},{1,3},{3,1},{5,7},{7,5},{8,10},{10,8},{12,... | collective-permute-start | bytes 1671176 | tf_op jit(solution)/shard_map/share_generators/ppermute | solution.py:361
  63.4 6.7 %collective-permute-start.12 = (bf16[136,1024]{1,0:T(8,128)(2,1)S(1)}, bf16[136,1024]{1,0:T(8,128)(2,1)S(1)}, u32[]{:S(2)}, u32[]{:S(2)}) collective-permute-start(bf16[136,1024]{1,0:T(8,128)(2,1)S(1)} %get-tuple-element.54.refs_0_), channel_id=1, source_target_pairs={{0,4},{2,6},{4,0},{6,2},{1,5},{3,7},{5,1},{7,3},{8,12},{10,14},{12... | collective-permute-start | bytes 835592 | tf_op jit(solution)/shard_map/input_gradient/ppermute | solution.py:364
  64.7 13.3 %collective-permute-start.15 = (bf16[272,1024]{1,0:T(8,128)(2,1)S(1)}, bf16[272,1024]{1,0:T(8,128)(2,1)S(1)}, u32[]{:S(2)}, u32[]{:S(2)}) collective-permute-start(bf16[272,1024]{1,0:T(8,128)(2,1)S(1)} %collective-permute-done.14.refs_2_), channel_id=1, source_target_pairs={{0,2},{2,0},{4,6},{6,4},{1,3},{3,1},{5,7},{7,5},{8,10},{10,8},{12,... | collective-permute-start | bytes 1671176 | tf_op jit(solution)/shard_map/share_generators/ppermute | solution.py:361
  68.4 9.0 %collective-permute-start.18 = (bf16[272,512]{1,0:T(8,128)(2,1)S(1)}, bf16[272,512]{1,0:T(8,128)(2,1)S(1)}, u32[]{:S(2)}, u32[]{:S(2)}) collective-permute-start(bf16[272,512]{1,0:T(8,128)(2,1)S(1)} %get-tuple-element.60), channel_id=1, source_target_pairs={{0,3},{1,2},{2,1},{3,0},{4,7},{5,6},{6,5},{7,4},{8,11},{9,10},{10,... | collective-permute-start | bytes 835592 | tf_op jit(solution)/shard_map/input_gradient/ppermute | solution.py:371
  69.6 12.8 %collective-permute-start.16 = (bf16[336,512]{1,0:T(8,128)(2,1)S(1)}, bf16[336,512]{1,0:T(8,128)(2,1)S(1)}, u32[]{:S(2)}, u32[]{:S(2)}) collective-permute-start(bf16[336,512]{1,0:T(8,128)(2,1)S(1)} %get-tuple-element.59), channel_id=1, source_target_pairs={{0,2},{2,0},{4,6},{6,4},{1,3},{3,1},{5,7},{7,5},{8,10},{10,8},{12,... | collective-permute-start | bytes 1032200 | tf_op jit(solution)/shard_map/exchange_back/ppermute | solution.py:361
  70.1 12.2 %collective-permute-start.17 = (bf16[272,512]{1,0:T(8,128)(2,1)S(1)}, bf16[272,512]{1,0:T(8,128)(2,1)S(1)}, u32[]{:S(2)}, u32[]{:S(2)}) collective-permute-start(bf16[272,512]{1,0:T(8,128)(2,1)S(1)} %get-tuple-element.58.refs_0_), channel_id=1, source_target_pairs={{0,1},{1,0},{2,3},{3,2},{4,5},{5,4},{6,7},{7,6},{8,9},{9,8},{10,11... | collective-permute-start | bytes 835592 | tf_op jit(solution)/shard_map/input_gradient/ppermute | solution.py:367
  71.0 15.1 %collective-permute-start.19 = (bf16[72,1024]{1,0:T(8,128)(2,1)S(1)}, bf16[72,1024]{1,0:T(8,128)(2,1)S(1)}, u32[]{:S(2)}, u32[]{:S(2)}) collective-permute-start(bf16[72,1024]{1,0:T(8,128)(2,1)S(1)} %get-tuple-element.68), channel_id=1, source_target_pairs={{0,0},{2,16},{4,8},{6,24},{8,2},{10,18},{12,10},{14,26},{16,4},{18... | collective-permute-start | bytes 442376 | tf_op jit(solution)/shard_map/input_gradient/ppermute | solution.py:379
  77.4 10.3 %collective-permute-start.20 = (bf16[72,1024]{1,0:T(8,128)(2,1)S(1)}, bf16[72,1024]{1,0:T(8,128)(2,1)S(1)}, u32[]{:S(2)}, u32[]{:S(2)}) collective-permute-start(bf16[72,1024]{1,0:T(8,128)(2,1)S(1)} %get-tuple-element.55.refs_0_.after_ref), channel_id=1, source_target_pairs={{0,16},{2,0},{4,24},{6,8},{8,18},{10,2},{12,26},{14,10},{16,20},{1... | collective-permute-start | bytes 442376 | tf_op jit(solution)/shard_map/input_gradient/ppermute | solution.py:379
